TPU v7x, 256 devices: a whole 4x4x8 slice. The times are simulated.
256 devices in a mesh: dp: 32 (over x_lo, z, core), mp: 8 (over x_hi, y).
Axes of the slice: x: 4 (x_hi: 2, x_lo: 2; x = x_hi * 2 + x_lo), y: 4, z: 8, core: 2. Of those that a mesh axis runs over, the one named last changes fastest.
Arguments:
- hidden: bfloat16 [4096, 14336], P('dp', 'mp')
- residual: bfloat16 [4096, 4096], P('mp', 'dp'), may hold values from -6 to 6
- down_weight: bfloat16 [14336, 4096], P('mp', 'dp'), may hold values from -6 to 6
- mask: int32 [14336, 4096], P('mp', 'dp'), may hold values 0 or 1
- state: float32 [14336, 4096], P('mp', 'dp'), may hold values from 0.1 to 1
Outputs:
- scores: float32 [14336, 4096], P('mp', 'dp')
- new_weight: bfloat16 [14336, 4096], P('mp', 'dp')
- new_state: float32 [14336, 4096], P('mp', 'dp')
All inputs are finite; a program needn't handle non-finite values. No bound on the sum of `mask` on one device may be relied on, other than what follows from the above.
Results may differ from a plain program's by a relative error of at most 0.0029.
Values may be sent and summed in bfloat16 or wider, within the bound.
No kernel may reach another device: no remote copies, remote signals or barrier semaphores. Data moves between devices by JAX's collectives and lax.ppermute only.
A program may use at most 128 MiB of HBM per device.

v0:
```python
import math

import jax
import jax.numpy as jnp
from jax import lax
from jax.sharding import PartitionSpec as P

FFW = 14336


score_alpha = 0.5
decay_rate = 0.9
step_rate = 0.3
tiny_eps = 1e-08


def body(hidden, residual, down_weight, mask, state):
    keep = mask == 1
    cols = down_weight.shape[1]
    gathered = lax.all_gather(hidden, "dp", axis=0, tiled=True)
    count = gathered.shape[0]
    colsq = lax.psum(jnp.sum(jnp.square(hidden.astype(jnp.float32)), axis=0), "dp")
    pruned_part = jnp.where(keep, jnp.zeros_like(down_weight), -down_weight)
    paired = jnp.concatenate([down_weight, pruned_part], axis=1)
    inv_width = 1.0 / math.sqrt(FFW)
    partial_value = jnp.dot(gathered, paired, preferred_element_type=jnp.float32) * inv_width
    summed = lax.psum_scatter(partial_value, "mp", scatter_dimension=0, tiled=True)
    block_out = (residual.astype(jnp.float32) + summed[:, :cols]).astype(jnp.bfloat16)
    gap_b = summed[:, cols:].astype(jnp.bfloat16)
    both = jnp.concatenate([block_out, gap_b], axis=1)
    targets = lax.all_gather(both, "mp", axis=0, tiled=True)
    inv_count = 1.0 / math.sqrt(count)
    grads = (
        lax.dot_general(
            gathered, targets, (((0,), (0,)), ((), ())), preferred_element_type=jnp.float32
        )
        * inv_count
    )
    grad_out = grads[:, :cols]
    grad_step = jnp.where(keep, grads[:, cols:], jnp.float32(0.0))
    rms = jnp.sqrt(colsq / count + 1e-05)
    weight_f = down_weight.astype(jnp.float32)
    scores = jnp.abs(weight_f) * (score_alpha * jnp.abs(grad_out) + rms[:, None])
    new_state = decay_rate * state + (1.0 - decay_rate) * grad_step * grad_step
    moved = weight_f - step_rate * grad_step / (jnp.sqrt(new_state) + tiny_eps)
    new_weight = jnp.where(keep, moved, jnp.float32(0.0)).astype(jnp.bfloat16)
    return (scores, new_weight, new_state)


def solution(mesh):
    return jax.shard_map(
        body,
        mesh=mesh,
        in_specs=(P("dp", "mp"), P("mp", "dp"), P("mp", "dp"), P("mp", "dp"), P("mp", "dp")),
        out_specs=(P("mp", "dp"), P("mp", "dp"), P("mp", "dp")),
        check_vma=False,
    )
```

profile of v0, /device:TPU:2, one launch (start us, length us, event | category | flops | bytes accessed | tf_op | source)
XLA Modules:
  0.0 289.6 jit_solution(13838323486547344083)
XLA Ops:
  7.2 0.0 all-gather.3.cloned.1.call-start
  7.2 0.7 all-gather.3.cloned.1.call-update
  7.9 0.0 reduce-scatter.2.cloned.1.call-start
  7.9 1.2 copy.8
  9.2 1.5 copy.10
  10.7 0.2 negate_select_fusion
  10.9 91.1 %all-gather.3.cloned.1.call-done = bf16[4096,1792]{1,0:T(8,128)(2,1)} async-done(((bf16[128,1792]{1,0:T(8,128)(2,1)}), bf16[4096,1792]{1,0:T(8,128)(2,1)}) %all-gather.3.cloned.1.call-update) | async-done | bytes 14680080 | tf_op jit(solution)/shard_map/all_gather | solution.py:20
  102.0 16.0 %fusion = f32[4096,256]{0,1:T(8,128)} fusion(bf16[4096,1792]{1,0:T(8,128)(2,1)} %all-gather.3.cloned.1.call-done, bf16[1792,128]{0,1:T(8,128)(2,1)S(1)} %get-tuple-element.8, bf16[1792,128]{0,1:T(8,128)(2,1)S(1)} %copy.8), kind=kOutput, calls=%fused_computation.1 | convolution fusion | flops 3760979968 | bytes 19791872 | tf_op jit(solution)/shard_map/dot_general | solution.py:26
  118.0 0.0 copy-start.3
  118.0 0.0 copy-start.2
  118.0 0.0 reduce-scatter.2.cloned.1.call-update
  118.0 0.0 copy-start
  118.0 0.0 all-gather.5.cloned.1.call-start
  118.1 0.8 copy-done.3
  118.9 0.1 copy.9
  119.0 88.7 %reduce-scatter.2.cloned.1.call-done = f32[512,256]{0,1:T(8,128)} async-done(((f32[4096,256]{0,1:T(8,128)}), f32[512,256]{0,1:T(8,128)}) %reduce-scatter.2.cloned.1.call-update) | async-done | bytes 524304 | tf_op jit(solution)/shard_map/reduce_scatter | solution.py:27
  207.7 1.0 slice.37
  208.7 1.0 fusion.11
  209.6 0.7 pad_maximum_fusion
  210.4 0.0 all-gather.5.cloned.1.call-update
  210.4 0.0 copy-done.2
  210.4 0.3 copy.13
  210.7 0.0 copy-done
  210.7 0.1 multiply_reduce_fusion
  210.8 57.8 %psum.7 = f32[1792]{0:T(1024)S(1)} all-reduce(f32[1792]{0:T(1024)S(1)} %multiply_reduce_fusion), channel_id=1, replica_groups=mesh['dp'=32,'mp'=8] {'dp'}, use_global_device_ids=true, to_apply=%region_2.3 | all-reduce | flops 1792 | bytes 14336 | tf_op jit(solution)/shard_map/psum | solution.py:22
  268.7 1.0 all-gather.5.cloned.1.call-done
  269.7 8.4 %fusion.1 = f32[1792,256]{0,1:T(8,128)S(1)} fusion(bf16[4096,256]{0,1:T(8,128)(2,1)} %all-gather.5.cloned.1.call-done, bf16[4096,1792]{1,0:T(8,128)(2,1)} %all-gather.3.cloned.1.call-done), kind=kOutput, calls=%fused_computation.3 | convolution fusion | flops 3758555136 | bytes 18612224 | tf_op jit(solution)/shard_map/dot_general | solution.py:34
  278.1 1.6 fusion.4
  279.7 0.0 copy-start.1
  279.7 1.2 copy.14
  280.9 0.0 copy-done.1
  280.9 1.0 copy.15
  281.9 1.2 copy.16
  (1 shorter events, 0.0 us)
Async XLA Ops:
  7.2 94.8 %all-gather.3.cloned.1.call-start = ((), (), s32[]{:S(2)}) async-start(), calls=%async_computation.1 | async-start | bytes 15138816 | tf_op jit(solution)/shard_map/all_gather | solution.py:20
  7.9 199.8 %reduce-scatter.2.cloned.1.call-start = ((), (), s32[]{:S(2)}) async-start(), calls=%async_computation.2 | async-start | bytes 4718592 | tf_op jit(solution)/shard_map/reduce_scatter | solution.py:27
  118.0 0.9 copy-start.3
  118.0 92.4 %copy-start.2 = (f32[1792,128]{1,0:T(8,128)S(1)}, f32[1792,128]{1,0:T(8,128)}, u32[]{:S(2)}) copy-start(f32[1792,128]{1,0:T(8,128)} %param.9) | copy-start | bytes 2752516
  118.0 92.7 %copy-start = (bf16[128,1792]{1,0:T(8,128)(2,1)S(1)}, bf16[128,1792]{1,0:T(8,128)(2,1)}, u32[]{:S(2)}) copy-start(bf16[128,1792]{1,0:T(8,128)(2,1)} %param.5) | copy-start | bytes 1376260
  118.0 151.7 %all-gather.5.cloned.1.call-start = ((), (), s32[]{:S(2)}) async-start(), calls=%async_computation.3 | async-start | bytes 2359296 | tf_op jit(solution)/shard_map/all_gather | solution.py:31
  279.7 1.2 copy-start.1
Sparse Core Ops, SparseCore 0:
  9.9 92.0 all-gather.2
  118.1 89.5 reduce-scatter.1
  211.0 58.5 all-gather.4
where the time goes:
time: 291 us; the launch traced here: 290 us
  waiting for transfers between devices  182 us (63%)
  blocking collectives  57.8 us (20%)
  matrix products  24.4 us (8%)
  between operations  13.8 us (5%)
  local copies, waits for them, and re-layouts  8.33 us (3%)
  other arithmetic  3.64 us (1%)
    all_gather x1, waiting for transfers between devices, body(): gathered = lax.all_gather(hidden, 'dp', axis=0, tiled=True)  91.1 us
    reduce_scatter x1, waiting for transfers between devices, body(): lax.psum_scatter(partial_value, 'mp', scatter_dimension=0, tiled=True)  88.7 us
    psum x1, blocking collectives, body(): lax.psum(jnp.sum(jnp.square(hidden.astype(jnp.float32)), axis=0), 'dp')  57.8 us
    dot_general x1, matrix products, body(): jnp.dot(gathered, paired, preferred_element_type=jnp.float32) * inv_width  16 us
    dot_general x1, matrix products, body(): lax.dot_general(gathered, targets, (((0,), (0,)), ((), ())), preferred_el...  8.4 us
    unnamed x15, local copies, waits for them, and re-layouts  7.36 us
  transfers between devices with their start and end apart: 3, of which 3 were waited for; matrix products, arithmetic and copies ran while one was open for 1% of the time, Pallas kernels for 0%

commit v1 on v0

v1 whole, which is shorter than its diff:
```python
import math

import jax
import jax.numpy as jnp
from jax import lax
from jax.sharding import PartitionSpec as P

FFW = 14336
TOKENS = 4096

score_alpha = 0.5
decay_rate = 0.9
step_rate = 0.3
tiny_eps = 1e-08

Z = 8
PAIR_CORE = [(i, i ^ 1) for i in range(32)]
PAIR_X = [(i, i ^ 16) for i in range(32)]


def ring_perm():
    out = []
    for i in range(32):
        x, z, c = i // 16, (i // 2) % Z, i % 2
        z = (z + (1 if c == 0 else -1)) % Z
        out.append((i, x * 16 + z * 2 + c))
    return out


RING = ring_perm()


def exchange(value):
    return lax.all_to_all(value, "mp", 0, 0, tiled=True)


def body(hidden, residual, down_weight, mask, state):
    f32, bf16 = jnp.float32, jnp.bfloat16
    dp = lax.axis_index("dp")
    mp = lax.axis_index("mp")
    x, z, c = dp >> 4, (dp >> 1) & 7, dp & 1
    rows, cols = hidden.shape[0], down_weight.shape[1]
    keep = mask == 1
    inv_width = 1.0 / math.sqrt(FFW)
    inv_count = 1.0 / math.sqrt(TOKENS)

    sibling = lax.ppermute(hidden, "dp", PAIR_CORE)
    first = jnp.concatenate([hidden, sibling], axis=0)
    r1 = lax.ppermute(first, "dp", RING)
    s1 = lax.ppermute(r1, "dp", PAIR_CORE)
    r2 = lax.ppermute(r1, "dp", RING)
    s2 = lax.ppermute(r2, "dp", PAIR_CORE)
    r3 = lax.ppermute(r2, "dp", RING)
    s3 = lax.ppermute(r3, "dp", PAIR_CORE)
    r4 = lax.ppermute(r3[:rows], "dp", RING)
    s4 = lax.ppermute(r4, "dp", PAIR_CORE)

    pruned_part = jnp.where(keep, jnp.zeros_like(down_weight), -down_weight)
    paired = jnp.concatenate([down_weight, pruned_part], axis=1)
    paired_x = lax.ppermute(paired, "dp", PAIR_X)
    residual_x = lax.ppermute(residual, "dp", PAIR_X)
    weights = jnp.concatenate([paired, paired_x], axis=1)
    zero = jnp.zeros((rows, cols), f32)

    def residual_rows(step, core):
        at = (z + step) & 7
        here = mp == (x << 2) + (at >> 1)
        start = ((at & 1) << 8) + (core << 7)
        own = lax.dynamic_slice(residual, (start, 0), (rows, cols)).astype(f32)
        other = lax.dynamic_slice(residual_x, (start, 0), (rows, cols)).astype(f32)
        both = jnp.concatenate([own, zero, other, zero], axis=1)
        return jnp.where(here, both, 0.0)

    back = jnp.where(c == 0, -1, 1)
    parts = [
        (first, [(0, c), (0, 1 - c)]),
        (r1, [(back, c), (back, 1 - c)]),
        (s1, [(-back, 1 - c), (-back, c)]),
        (r2, [(2 * back, c), (2 * back, 1 - c)]),
        (s2, [(-2 * back, 1 - c), (-2 * back, c)]),
        (r3, [(3 * back, c), (3 * back, 1 - c)]),
        (s3, [(-3 * back, 1 - c), (-3 * back, c)]),
        (r4, [(4, c)]),
        (s4, [(4, 1 - c)]),
    ]
    groups = [parts[:3], parts[3:5], parts[5:]]

    colsq = 0.0
    grads = 0.0
    blocks = []
    for group in groups:
        tokens = jnp.concatenate([p for p, _ in group], axis=0)
        start = jnp.concatenate(
            [residual_rows(k, q) for _, where in group for k, q in where], axis=0
        )
        value = jnp.dot(tokens, weights, preferred_element_type=f32) * inv_width + start
        sent = exchange(value.astype(bf16))
        count = tokens.shape[0] // 8
        summed = jnp.sum(sent.reshape(8, count, 4 * cols).astype(f32), axis=0)
        target = summed.astype(bf16)
        spread = jnp.broadcast_to(target[None], (8, count, 4 * cols)).reshape(8 * count, 4 * cols)
        blocks.append((tokens, exchange(spread)))
        colsq = colsq + jnp.sum(jnp.square(tokens.astype(f32)), axis=0)

    for tokens, targets in blocks:
        grads = grads + lax.dot_general(
            tokens, targets, (((0,), (0,)), ((), ())), preferred_element_type=f32
        )
    grads = grads * inv_count
    colsq = colsq + lax.ppermute(colsq, "dp", PAIR_X)
    arrived = lax.ppermute(grads[:, 2 * cols :].astype(bf16), "dp", PAIR_X)
    grads = grads[:, : 2 * cols] + arrived.astype(f32)

    grad_out = grads[:, :cols]
    grad_step = jnp.where(keep, grads[:, cols:], jnp.float32(0.0))
    rms = jnp.sqrt(colsq / TOKENS + 1e-05)
    weight_f = down_weight.astype(f32)
    scores = jnp.abs(weight_f) * (score_alpha * jnp.abs(grad_out) + rms[:, None])
    new_state = decay_rate * state + (1.0 - decay_rate) * grad_step * grad_step
    moved = weight_f - step_rate * grad_step / (jnp.sqrt(new_state) + tiny_eps)
    new_weight = jnp.where(keep, moved, jnp.float32(0.0)).astype(bf16)
    return (scores, new_weight, new_state)


def solution(mesh):
    return jax.shard_map(
        body,
        mesh=mesh,
        in_specs=(P("dp", "mp"), P("mp", "dp"), P("mp", "dp"), P("mp", "dp"), P("mp", "dp")),
        out_specs=(P("mp", "dp"), P("mp", "dp"), P("mp", "dp")),
        check_vma=False,
    )
```

time: 291 us -> 185 us (0.64)
  waiting for transfers between devices: 182 us -> 89.7 us
  blocking collectives: 57.8 us -> 0 us
  starting transfers between devices: 0.12 us -> 37 us
  between operations: 13.8 us -> 1 us
  other arithmetic: 3.64 us -> 14.8 us
  local copies, waits for them, and re-layouts: 8.33 us -> 13 us
  matrix products: 24.4 us -> 27.6 us
    all_gather x2 -> x0, waiting for transfers between devices: 92.1 us -> none  [the longest x1 91.1 us: body(): gathered = lax.all_gather(hidden, 'dp', axis=0, tiled=True)]
    reduce_scatter x1 -> x0, waiting for transfers between devices: 88.7 us -> none  [body(): lax.psum_scatter(partial_value, 'mp', scatter_dimension=0, tiled=True)]
    psum x1 -> x0, blocking collectives: 57.8 us -> none  [body(): lax.psum(jnp.sum(jnp.square(hidden.astype(jnp.float32)), axis=0), 'dp')]
    ppermute x0 -> x13, waiting for transfers between devices: none -> 47.9 us  [the longest x1 17 us: body(): colsq = colsq + lax.ppermute(colsq, 'dp', PAIR_X)]
    all_to_all x0 -> x6, waiting for transfers between devices: none -> 41.8 us  [exchange(): return lax.all_to_all(value, 'mp', 0, 0, tiled=True)]
    all_to_all x0 -> x6, starting transfers between devices: none -> 28 us  [exchange(): return lax.all_to_all(value, 'mp', 0, 0, tiled=True)]
    ppermute x0 -> x13, starting transfers between devices: none -> 8.96 us  [the longest x1 2.36 us: body(): residual_x = lax.ppermute(residual, 'dp', PAIR_X)]
    reduce_sum x1 -> x6, other arithmetic: 0.11 us -> 7.6 us  [the longest x3 5.13 us: body(): colsq = colsq + jnp.sum(jnp.square(tokens.astype(f32)), axis=0)]
  transfers between devices with their start and end apart: 3 -> 19, of which waited for: 3 -> 10; matrix products, arithmetic and copies ran while one was open for 1% -> 24% of each run, Pallas kernels for 0% -> 0%
where the time goes in v1:
time: 185 us; the launch traced here: 183 us
  waiting for transfers between devices  89.7 us (48%)
  starting transfers between devices  37 us (20%)
  matrix products  27.6 us (15%)
  other arithmetic  14.8 us (8%)
  local copies, waits for them, and re-layouts  13 us (7%)
    all_to_all x6, waiting for transfers between devices, exchange(): return lax.all_to_all(value, 'mp', 0, 0, tiled=True)  41.8 us
    all_to_all x6, starting transfers between devices, exchange(): return lax.all_to_all(value, 'mp', 0, 0, tiled=True)  28 us
    ppermute x1, waiting for transfers between devices, body(): colsq = colsq + lax.ppermute(colsq, 'dp', PAIR_X)  17 us
    dot_general x3, matrix products, body(): lax.dot_general(tokens, targets, (((0,), (0,)), ((), ())), preferred_elem...  15.2 us
    ppermute x1, waiting for transfers between devices, body(): r1 = lax.ppermute(first, 'dp', RING)  13.2 us
    ppermute x1, waiting for transfers between devices, body(): r2 = lax.ppermute(r1, 'dp', RING)  12.4 us
    dot_general x3, matrix products, body(): jnp.dot(tokens, weights, preferred_element_type=f32) * inv_width + start  12.4 us
    unnamed x31, local copies, waits for them, and re-layouts  6.98 us
  transfers between devices with their start and end apart: 19, of which 10 were waited for; matrix products, arithmetic and copies ran while one was open for 24% of the time, Pallas kernels for 0%

profile of v1, /device:TPU:2, one launch (start us, length us, event | category | flops | bytes accessed | tf_op | source)
XLA Modules:
  0.0 183.1 jit_solution(4847319340295197670)
XLA Ops:
  0.7 2.4 %collective-permute-start.4 = (bf16[512,128]{1,0:T(8,128)(2,1)}, bf16[512,128]{1,0:T(8,128)(2,1)S(1)}, u32[]{:S(2)}, u32[]{:S(2)}) collective-permute-start(bf16[512,128]{1,0:T(8,128)(2,1)} %param.6), channel_id=1, source_target_pairs={{0,128},{8,136},{16,144},{24,152},{32,160},{40,168},{48,176},{56,1... | collective-permute-start | bytes 393224 | tf_op jit(solution)/shard_map/ppermute | solution.py:61
  3.0 2.2 %negate_select_fusion = (bf16[1792,128]{1,0:T(8,128)(2,1)S(1)}, pred[1792,128]{1,0:T(8,128)(4,1)}) fusion(bf16[1792,128]{1,0:T(8,128)(2,1)} %param.7, s32[1792,128]{1,0:T(8,128)} %param.8), kind=kLoop, calls=%fused_computation.57 | loop fusion | flops 688128 | bytes 2064384 | tf_op jit(solution)/shard_map/jit(_where)/select_n | solution.py:58
  5.8 0.5 copy-done.3
  6.4 1.1 collective-permute-start.1
  7.8 0.9 fusion.36
  8.6 0.9 fusion.38
  9.6 13.2 %collective-permute-done.1 = bf16[256,1792]{1,0:T(8,128)(2,1)S(1)} collective-permute-done((bf16[256,1792]{1,0:T(8,128)(2,1)S(1)}, bf16[256,1792]{1,0:T(8,128)(2,1)S(1)}, u32[]{:S(2)}, u32[]{:S(2)}) %collective-permute-start.1) | collective-permute-done | bytes 917536 | tf_op jit(solution)/shard_map/ppermute | solution.py:49
  22.8 2.0 %collective-permute-start.2 = (bf16[256,1792]{1,0:T(8,128)(2,1)S(1)}, bf16[256,1792]{1,0:T(8,128)(2,1)S(1)}, u32[]{:S(2)}, u32[]{:S(2)}) collective-permute-start(bf16[256,1792]{1,0:T(8,128)(2,1)S(1)} %collective-permute-done.1), channel_id=1, source_target_pairs={{0,8},{8,0},{16,24},{24,16},{32,40},{40,32},{48,56},{56,48},{64,72... | collective-permute-start | bytes 2752520 | tf_op jit(solution)/shard_map/ppermute | solution.py:50
  25.1 12.4 %collective-permute-done.5 = bf16[256,1792]{1,0:T(8,128)(2,1)} collective-permute-done((bf16[256,1792]{1,0:T(8,128)(2,1)S(1)}, bf16[256,1792]{1,0:T(8,128)(2,1)}, u32[]{:S(2)}, u32[]{:S(2)}) %collective-permute-start.5) | collective-permute-done | bytes 917536 | tf_op jit(solution)/shard_map/ppermute | solution.py:51
  37.5 0.9 collective-permute-start.6
  38.5 4.4 %add_convert_fusion.1 = bf16[768,512]{1,0:T(8,128)(2,1)} fusion(f32[768,512]{1,0:T(8,128)S(1)} %get-tuple-element.46, bf16[768,1792]{1,0:T(8,128)(2,1)S(1)} %constant_dynamic-update-slice_fusion, bf16[1792,256]{1,0:T(8,128)(2,1)} %collective-permute-done.3, bf16[1792,128]{1,0:T(8,128)(2,1)S(1)} %get-tuple-element.5, bf16[1792,128]{1,0:T(8,128)(2,1)S(1)} %copy-done), kind=kOutput, calls=%fused_computation.40 | convolution fusion | flops 1415970816 | bytes 6946816 | tf_op jit(solution)/shard_map/dot_general | solution.py:96
  42.8 6.0 %all-to-all-start = ((bf16[8,96,512]{2,1,0:T(8,128)(2,1)}), bf16[8,96,512]{2,1,0:T(8,128)(2,1)S(1)}, u32[]{:S(2)}, u32[]{:S(2)}) async-start(bf16[8,96,512]{2,1,0:T(8,128)(2,1)} %bitcast), calls=%async_computation | async-start | bytes 1572864 | tf_op jit(solution)/shard_map/all_to_all | solution.py:34
  48.9 1.2 constant_dynamic-update-slice_fusion.5
  50.1 2.3 %collective-permute-done.7 = bf16[256,1792]{1,0:T(8,128)(2,1)} collective-permute-done((bf16[256,1792]{1,0:T(8,128)(2,1)}, bf16[256,1792]{1,0:T(8,128)(2,1)}, u32[]{:S(2)}, u32[]{:S(2)}) %collective-permute-start.7) | collective-permute-done | bytes 917536 | tf_op jit(solution)/shard_map/ppermute | solution.py:53
  52.4 1.0 slice.21
  53.7 2.3 %constant_dynamic-update-slice_fusion.9 = bf16[768,1792]{1,0:T(8,128)(2,1)} fusion(bf16[256,1792]{1,0:T(8,128)(2,1)} %collective-permute-done.7), kind=kLoop, calls=%fused_computation.112 | loop fusion | bytes 1835008
  56.0 1.2 constant_dynamic-update-slice_fusion.4
  57.3 3.1 %fusion.1 = bf16[512,512]{1,0:T(8,128)(2,1)} fusion(bf16[512,1792]{1,0:T(8,128)(2,1)S(1)} %constant_dynamic-update-slice_fusion.4, f32[128,512]{1,0:T(8,128)S(1)} %copy-done.10, f32[128,512]{1,0:T(8,128)S(1)} %copy-done.9, f32[128,512]{1,0:T(8,128)S(1)} %copy-done.8, f32[128,512]{1,0:T(8,128)S(1)} %copy-done.7, ...), kind=kOutput, calls=%fused_computation.44 | convolution fusion | flops 946601984 | bytes 5242880 | tf_op jit(solution)/shard_map/dot_general | solution.py:96
  60.4 2.9 %collective-permute-done.9 = bf16[128,1792]{1,0:T(8,128)(2,1)S(1)} collective-permute-done((bf16[128,1792]{1,0:T(8,128)(2,1)S(1)}, bf16[128,1792]{1,0:T(8,128)(2,1)S(1)}, u32[]{:S(2)}, u32[]{:S(2)}) %collective-permute-start.9) | collective-permute-done | bytes 458784 | tf_op jit(solution)/shard_map/ppermute | solution.py:55
  63.3 1.1 constant_dynamic-update-slice_fusion.8
  64.4 0.8 constant_dynamic-update-slice_fusion.7
  65.2 0.8 constant_dynamic-update-slice_fusion.6
  66.0 6.0 %all-to-all-start.2 = ((bf16[8,64,512]{2,1,0:T(8,128)(2,1)}), bf16[8,64,512]{2,1,0:T(8,128)(2,1)}, u32[]{:S(2)}, u32[]{:S(2)}) async-start(bf16[8,64,512]{2,1,0:T(8,128)(2,1)} %bitcast.18), calls=%async_computation.2 | async-start | bytes 1048576 | tf_op jit(solution)/shard_map/all_to_all | solution.py:34
  72.0 5.0 %add_convert_fusion = bf16[768,512]{1,0:T(8,128)(2,1)} fusion(f32[768,512]{1,0:T(8,128)} %copy-done.11, bf16[768,1792]{1,0:T(8,128)(2,1)} %constant_dynamic-update-slice_fusion.6, bf16[1792,256]{1,0:T(8,128)(2,1)} %collective-permute-done.3, bf16[1792,128]{1,0:T(8,128)(2,1)S(1)} %get-tuple-element.5, bf16[1792,128]{1,0:T(8,128)(2,1)S(1)} %copy-done), kind=kOutput, calls=%fused_computation.39 | convolution fusion | flops 1415970816 | bytes 6946816 | tf_op jit(solution)/shard_map/dot_general | solution.py:96
  77.0 6.7 %all-to-all-done.2 = bf16[8,64,512]{2,1,0:T(8,128)(2,1)} async-done(((bf16[8,64,512]{2,1,0:T(8,128)(2,1)}), bf16[8,64,512]{2,1,0:T(8,128)(2,1)}, u32[]{:S(2)}, u32[]{:S(2)}) %all-to-all-start.2) | async-done | bytes 524320 | tf_op jit(solution)/shard_map/all_to_all | solution.py:34
  83.7 4.2 %all-to-all-start.4 = ((bf16[8,96,512]{2,1,0:T(8,128)(2,1)}), bf16[8,96,512]{2,1,0:T(8,128)(2,1)}, u32[]{:S(2)}, u32[]{:S(2)}) async-start(bf16[8,96,512]{2,1,0:T(8,128)(2,1)} %bitcast.17), calls=%async_computation.4 | async-start | bytes 1572864 | tf_op jit(solution)/shard_map/all_to_all | solution.py:34
  88.1 12.9 %all-to-all-done.4 = bf16[8,96,512]{2,1,0:T(8,128)(2,1)} async-done(((bf16[8,96,512]{2,1,0:T(8,128)(2,1)}), bf16[8,96,512]{2,1,0:T(8,128)(2,1)}, u32[]{:S(2)}, u32[]{:S(2)}) %all-to-all-start.4) | async-done | bytes 786464 | tf_op jit(solution)/shard_map/all_to_all | solution.py:34
  100.9 0.9 broadcast_in_dim.52
  101.9 3.7 %all-to-all-start.1 = ((bf16[8,96,512]{2,1,0:T(8,128)(2,1)}), bf16[8,96,512]{2,1,0:T(8,128)(2,1)S(1)}, u32[]{:S(2)}, u32[]{:S(2)}) async-start(bf16[8,96,512]{2,1,0:T(8,128)(2,1)} %broadcast_in_dim.52), calls=%async_computation.1 | async-start | bytes 1572864 | tf_op jit(solution)/shard_map/all_to_all | solution.py:34
  105.6 1.2 reduce_sum.65
  106.9 12.2 %all-to-all-done.1 = bf16[8,96,512]{2,1,0:T(8,128)(2,1)S(1)} async-done(((bf16[8,96,512]{2,1,0:T(8,128)(2,1)}), bf16[8,96,512]{2,1,0:T(8,128)(2,1)S(1)}, u32[]{:S(2)}, u32[]{:S(2)}) %all-to-all-start.1) | async-done | bytes 786464 | tf_op jit(solution)/shard_map/all_to_all | solution.py:34
  119.1 1.0 broadcast_in_dim.54
  120.1 4.2 %all-to-all-start.5 = ((bf16[8,96,512]{2,1,0:T(8,128)(2,1)}), bf16[8,96,512]{2,1,0:T(8,128)(2,1)}, u32[]{:S(2)}, u32[]{:S(2)}) async-start(bf16[8,96,512]{2,1,0:T(8,128)(2,1)} %broadcast_in_dim.54), calls=%async_computation.5 | async-start | bytes 1572864 | tf_op jit(solution)/shard_map/all_to_all | solution.py:34
  124.3 2.4 %multiply_reduce_fusion.1 = f32[1792]{0:T(1024)S(1)} fusion(bf16[768,1792]{1,0:T(8,128)(2,1)} %copy-done.1), kind=kLoop, calls=%fused_computation.1 | loop fusion | flops 4126976 | bytes 2759680 | tf_op jit(solution)/shard_map/reduce_sum | solution.py:103
  126.7 1.1 reduce_sum.64
  127.8 9.7 %all-to-all-done.5 = bf16[8,96,512]{2,1,0:T(8,128)(2,1)} async-done(((bf16[8,96,512]{2,1,0:T(8,128)(2,1)}), bf16[8,96,512]{2,1,0:T(8,128)(2,1)}, u32[]{:S(2)}, u32[]{:S(2)}) %all-to-all-start.5) | async-done | bytes 786464 | tf_op jit(solution)/shard_map/all_to_all | solution.py:34
  137.5 0.8 broadcast_in_dim.53
  138.4 3.7 %all-to-all-start.3 = ((bf16[8,64,512]{2,1,0:T(8,128)(2,1)}), bf16[8,64,512]{2,1,0:T(8,128)(2,1)S(1)}, u32[]{:S(2)}, u32[]{:S(2)}) async-start(bf16[8,64,512]{2,1,0:T(8,128)(2,1)} %broadcast_in_dim.53), calls=%async_computation.3 | async-start | bytes 1048576 | tf_op jit(solution)/shard_map/all_to_all | solution.py:34
  142.1 5.4 %fusion.53 = f32[1792,512]{1,0:T(8,128)} fusion(bf16[768,1792]{1,0:T(8,128)(2,1)} %copy-done.1, bf16[768,512]{1,0:T(8,128)(2,1)} %bitcast.16), kind=kOutput, calls=%fused_computation.147 | convolution fusion | flops 1409286144 | bytes 7208960 | tf_op jit(solution)/shard_map/dot_general | solution.py:106
  147.5 5.4 %fusion.54 = f32[1792,512]{1,0:T(8,128)} fusion(bf16[768,1792]{1,0:T(8,128)(2,1)} %constant_dynamic-update-slice_fusion.6, bf16[768,512]{1,0:T(8,128)(2,1)} %bitcast.5), kind=kOutput, calls=%fused_computation.148 | convolution fusion | flops 1409286144 | bytes 7208960 | tf_op jit(solution)/shard_map/dot_general | solution.py:106
  153.2 4.4 %add_multiply_fusion = f32[1792,512]{1,0:T(8,128)S(1)} fusion(f32[1792,512]{1,0:T(8,128)} %fusion.54, f32[1792,512]{1,0:T(8,128)} %fusion.53, bf16[512,1792]{1,0:T(8,128)(2,1)S(1)} %constant_dynamic-update-slice_fusion.4, bf16[512,512]{1,0:T(8,128)(2,1)S(1)} %bitcast.15), kind=kOutput, calls=%fused_computation.3 | convolution fusion | flops 942276608 | bytes 13369344 | tf_op jit(solution)/shard_map/dot_general | solution.py:106
  157.8 1.5 collective-permute-start.11
  159.2 0.4 multiply_reduce_fusion.2
  159.6 2.4 %multiply_reduce_fusion = f32[1792]{0:T(1024)S(1)} fusion(bf16[768,1792]{1,0:T(8,128)(2,1)} %constant_dynamic-update-slice_fusion.6), kind=kLoop, calls=%fused_computation | loop fusion | flops 4126976 | bytes 2759680 | tf_op jit(solution)/shard_map/reduce_sum | solution.py:103
  162.0 0.7 collective-permute-start.12
  162.7 17.0 %collective-permute-done.12 = f32[1792]{0:T(1024)S(1)} collective-permute-done((f32[1792]{0:T(1024)S(1)}, f32[1792]{0:T(1024)S(1)}, u32[]{:S(2)}, u32[]{:S(2)}) %collective-permute-start.12) | collective-permute-done | bytes 7200 | tf_op jit(solution)/shard_map/ppermute | solution.py:110
  180.0 0.9 copy-done.4
  180.9 2.2 %fusion.4 = (bf16[1792,128]{1,0:T(8,128)(2,1)}, f32[1792,128]{1,0:T(8,128)}, f32[1792,128]{1,0:T(8,128)}) fusion(pred[1792,128]{1,0:T(8,128)(4,1)S(1)} %copy-done.5, bf16[1792,128]{1,0:T(8,128)(2,1)S(1)} %copy-done, f32[1792,256]{1,0:T(8,128)S(1)} %slice_add_fusion, f32[1792,128]{1,0:T(8,128)S(1)} %copy-done.4, f32[1792]{0:T(1024)S(1)} %add_sqrt_fusion), kind=kLoop, calls=%fused_computation.49 | loop fusion | flops 3899392 | bytes 5741568 | tf_op jit(solution)/shard_map/convert_element_type | solution.py:121
  (62 shorter events, 2.3 us)
Async XLA Ops:
  0.6 4.9 %copy-start.2 = (bf16[512,128]{1,0:T(8,128)(2,1)S(1)}, bf16[512,128]{1,0:T(8,128)(2,1)}, u32[]{:S(2)}) copy-start(bf16[512,128]{1,0:T(8,128)(2,1)} %param.6) | copy-start | bytes 393220
  0.6 4.6 %copy-start = (bf16[1792,128]{1,0:T(8,128)(2,1)S(1)}, bf16[1792,128]{1,0:T(8,128)(2,1)}, u32[]{:S(2)}) copy-start(bf16[1792,128]{1,0:T(8,128)(2,1)} %param.7) | copy-start | bytes 1376260
  0.7 6.8 %collective-permute-start.4 = (bf16[512,128]{1,0:T(8,128)(2,1)}, bf16[512,128]{1,0:T(8,128)(2,1)S(1)}, u32[]{:S(2)}, u32[]{:S(2)}) collective-permute-start(bf16[512,128]{1,0:T(8,128)(2,1)} %param.6), channel_id=1, source_target_pairs={{0,128},{8,136},{16,144},{24,152},{32,160},{40,168},{48,176},{56,1... | collective-permute-start | bytes 393224 | tf_op jit(solution)/shard_map/ppermute | solution.py:61
  3.0 3.3 %collective-permute-start = (bf16[128,1792]{1,0:T(8,128)(2,1)}, bf16[128,1792]{1,0:T(8,128)(2,1)S(1)}, u32[]{:S(2)}, u32[]{:S(2)}) collective-permute-start(bf16[128,1792]{1,0:T(8,128)(2,1)} %param.5), channel_id=1, source_target_pairs={{0,8},{8,0},{16,24},{24,16},{32,40},{40,32},{48,56},{56,48},{64,72... | collective-permute-start | bytes 1376264 | tf_op jit(solution)/shard_map/ppermute | solution.py:47
  5.2 1.0 copy-start.3
  5.3 33.1 %collective-permute-start.3 = (bf16[1792,256]{1,0:T(8,128)(2,1)S(1)}, bf16[1792,256]{1,0:T(8,128)(2,1)}, u32[]{:S(2)}, u32[]{:S(2)}) collective-permute-start(bf16[1792,256]{1,0:T(8,128)(2,1)S(1)} %pad_maximum_fusion.34), channel_id=1, source_target_pairs={{0,128},{8,136},{16,144},{24,152},{32,160},{40,168},{48,176},{56,1... | collective-permute-start | bytes 2752520 | tf_op jit(solution)/shard_map/ppermute | solution.py:60
  6.4 16.4 %collective-permute-start.1 = (bf16[256,1792]{1,0:T(8,128)(2,1)S(1)}, bf16[256,1792]{1,0:T(8,128)(2,1)S(1)}, u32[]{:S(2)}, u32[]{:S(2)}) collective-permute-start(bf16[256,1792]{1,0:T(8,128)(2,1)S(1)} %pad_maximum_fusion.33), channel_id=1, source_target_pairs={{0,16},{8,120},{16,32},{24,8},{32,48},{40,24},{48,64},{56,40},{64,... | collective-permute-start | bytes 2752520 | tf_op jit(solution)/shard_map/ppermute | solution.py:49
  22.8 14.7 %collective-permute-start.5 = (bf16[256,1792]{1,0:T(8,128)(2,1)S(1)}, bf16[256,1792]{1,0:T(8,128)(2,1)}, u32[]{:S(2)}, u32[]{:S(2)}) collective-permute-start(bf16[256,1792]{1,0:T(8,128)(2,1)S(1)} %collective-permute-done.1), channel_id=1, source_target_pairs={{0,16},{8,120},{16,32},{24,8},{32,48},{40,24},{48,64},{56,40},{64,... | collective-permute-start | bytes 2752520 | tf_op jit(solution)/shard_map/ppermute | solution.py:51
  22.8 15.6 %collective-permute-start.2 = (bf16[256,1792]{1,0:T(8,128)(2,1)S(1)}, bf16[256,1792]{1,0:T(8,128)(2,1)S(1)}, u32[]{:S(2)}, u32[]{:S(2)}) collective-permute-start(bf16[256,1792]{1,0:T(8,128)(2,1)S(1)} %collective-permute-done.1), channel_id=1, source_target_pairs={{0,8},{8,0},{16,24},{24,16},{32,40},{40,32},{48,56},{56,48},{64,72... | collective-permute-start | bytes 2752520 | tf_op jit(solution)/shard_map/ppermute | solution.py:50
  24.9 13.5 %copy-start.11 = (f32[768,512]{1,0:T(8,128)}, f32[768,512]{1,0:T(8,128)S(1)}, u32[]{:S(2)}) copy-start(f32[768,512]{1,0:T(8,128)S(1)} %fusion.51) | copy-start | bytes 4718596
  37.5 14.9 %collective-permute-start.7 = (bf16[256,1792]{1,0:T(8,128)(2,1)}, bf16[256,1792]{1,0:T(8,128)(2,1)}, u32[]{:S(2)}, u32[]{:S(2)}) collective-permute-start(bf16[256,1792]{1,0:T(8,128)(2,1)} %collective-permute-done.5), channel_id=1, source_target_pairs={{0,16},{8,120},{16,32},{24,8},{32,48},{40,24},{48,64},{56,40},{64,... | collective-permute-start | bytes 2752520 | tf_op jit(solution)/shard_map/ppermute | solution.py:53
  37.5 18.5 %collective-permute-start.6 = (bf16[256,1792]{1,0:T(8,128)(2,1)}, bf16[256,1792]{1,0:T(8,128)(2,1)}, u32[]{:S(2)}, u32[]{:S(2)}) collective-permute-start(bf16[256,1792]{1,0:T(8,128)(2,1)} %collective-permute-done.5), channel_id=1, source_target_pairs={{0,8},{8,0},{16,24},{24,16},{32,40},{40,32},{48,56},{56,48},{64,72... | collective-permute-start | bytes 2752520 | tf_op jit(solution)/shard_map/ppermute | solution.py:52
  38.5 4.4 %copy-start.1 = (bf16[768,1792]{1,0:T(8,128)(2,1)}, bf16[768,1792]{1,0:T(8,128)(2,1)S(1)}, u32[]{:S(2)}) copy-start(bf16[768,1792]{1,0:T(8,128)(2,1)S(1)} %constant_dynamic-update-slice_fusion) | copy-start | bytes 8257540
  42.8 23.1 %all-to-all-start = ((bf16[8,96,512]{2,1,0:T(8,128)(2,1)}), bf16[8,96,512]{2,1,0:T(8,128)(2,1)S(1)}, u32[]{:S(2)}, u32[]{:S(2)}) async-start(bf16[8,96,512]{2,1,0:T(8,128)(2,1)} %bitcast), calls=%async_computation | async-start | bytes 1572864 | tf_op jit(solution)/shard_map/all_to_all | solution.py:34
  53.5 3.8 %copy-start.7 = (f32[128,512]{1,0:T(8,128)S(1)}, f32[128,512]{1,0:T(8,128)}, u32[]{:S(2)}) copy-start(f32[128,512]{1,0:T(8,128)} %get-tuple-element.40) | copy-start | bytes 786436
  53.5 3.8 %copy-start.8 = (f32[128,512]{1,0:T(8,128)S(1)}, f32[128,512]{1,0:T(8,128)}, u32[]{:S(2)}) copy-start(f32[128,512]{1,0:T(8,128)} %get-tuple-element.42) | copy-start | bytes 786436
  53.5 3.8 %copy-start.9 = (f32[128,512]{1,0:T(8,128)S(1)}, f32[128,512]{1,0:T(8,128)}, u32[]{:S(2)}) copy-start(f32[128,512]{1,0:T(8,128)} %get-tuple-element.43) | copy-start | bytes 786436
  53.5 3.8 %copy-start.10 = (f32[128,512]{1,0:T(8,128)S(1)}, f32[128,512]{1,0:T(8,128)}, u32[]{:S(2)}) copy-start(f32[128,512]{1,0:T(8,128)} %get-tuple-element.45) | copy-start | bytes 786436
  53.5 9.8 %collective-permute-start.9 = (bf16[128,1792]{1,0:T(8,128)(2,1)S(1)}, bf16[128,1792]{1,0:T(8,128)(2,1)S(1)}, u32[]{:S(2)}, u32[]{:S(2)}) collective-permute-start(bf16[128,1792]{1,0:T(8,128)(2,1)S(1)} %slice.21), channel_id=1, source_target_pairs={{0,16},{8,120},{16,32},{24,8},{32,48},{40,24},{48,64},{56,40},{64,... | collective-permute-start | bytes 1376264 | tf_op jit(solution)/shard_map/ppermute | solution.py:55
  53.6 9.7 %collective-permute-start.8 = (bf16[256,1792]{1,0:T(8,128)(2,1)}, bf16[256,1792]{1,0:T(8,128)(2,1)S(1)}, u32[]{:S(2)}, u32[]{:S(2)}) collective-permute-start(bf16[256,1792]{1,0:T(8,128)(2,1)} %collective-permute-done.7), channel_id=1, source_target_pairs={{0,8},{8,0},{16,24},{24,16},{32,40},{40,32},{48,56},{56,48},{64,72... | collective-permute-start | bytes 2752520 | tf_op jit(solution)/shard_map/ppermute | solution.py:54
  63.3 1.9 %collective-permute-start.10 = (bf16[128,1792]{1,0:T(8,128)(2,1)S(1)}, bf16[128,1792]{1,0:T(8,128)(2,1)S(1)}, u32[]{:S(2)}, u32[]{:S(2)}) collective-permute-start(bf16[128,1792]{1,0:T(8,128)(2,1)S(1)} %collective-permute-done.9), channel_id=1, source_target_pairs={{0,8},{8,0},{16,24},{24,16},{32,40},{40,32},{48,56},{56,48},{64,72... | collective-permute-start | bytes 1376264 | tf_op jit(solution)/shard_map/ppermute | solution.py:56
  66.0 17.7 %all-to-all-start.2 = ((bf16[8,64,512]{2,1,0:T(8,128)(2,1)}), bf16[8,64,512]{2,1,0:T(8,128)(2,1)}, u32[]{:S(2)}, u32[]{:S(2)}) async-start(bf16[8,64,512]{2,1,0:T(8,128)(2,1)} %bitcast.18), calls=%async_computation.2 | async-start | bytes 1048576 | tf_op jit(solution)/shard_map/all_to_all | solution.py:34
  83.7 17.2 %all-to-all-start.4 = ((bf16[8,96,512]{2,1,0:T(8,128)(2,1)}), bf16[8,96,512]{2,1,0:T(8,128)(2,1)}, u32[]{:S(2)}, u32[]{:S(2)}) async-start(bf16[8,96,512]{2,1,0:T(8,128)(2,1)} %bitcast.17), calls=%async_computation.4 | async-start | bytes 1572864 | tf_op jit(solution)/shard_map/all_to_all | solution.py:34
  101.9 17.2 %all-to-all-start.1 = ((bf16[8,96,512]{2,1,0:T(8,128)(2,1)}), bf16[8,96,512]{2,1,0:T(8,128)(2,1)S(1)}, u32[]{:S(2)}, u32[]{:S(2)}) async-start(bf16[8,96,512]{2,1,0:T(8,128)(2,1)} %broadcast_in_dim.52), calls=%async_computation.1 | async-start | bytes 1572864 | tf_op jit(solution)/shard_map/all_to_all | solution.py:34
  119.1 19.3 %copy-start.6 = (bf16[8,96,512]{2,1,0:T(8,128)(2,1)}, bf16[8,96,512]{2,1,0:T(8,128)(2,1)S(1)}, u32[]{:S(2)}) copy-start(bf16[8,96,512]{2,1,0:T(8,128)(2,1)S(1)} %all-to-all-done.1) | copy-start | bytes 2359300
  120.1 17.4 %all-to-all-start.5 = ((bf16[8,96,512]{2,1,0:T(8,128)(2,1)}), bf16[8,96,512]{2,1,0:T(8,128)(2,1)}, u32[]{:S(2)}, u32[]{:S(2)}) async-start(bf16[8,96,512]{2,1,0:T(8,128)(2,1)} %broadcast_in_dim.54), calls=%async_computation.5 | async-start | bytes 1572864 | tf_op jit(solution)/shard_map/all_to_all | solution.py:34
  138.4 14.9 %all-to-all-start.3 = ((bf16[8,64,512]{2,1,0:T(8,128)(2,1)}), bf16[8,64,512]{2,1,0:T(8,128)(2,1)S(1)}, u32[]{:S(2)}, u32[]{:S(2)}) async-start(bf16[8,64,512]{2,1,0:T(8,128)(2,1)} %broadcast_in_dim.53), calls=%async_computation.3 | async-start | bytes 1048576 | tf_op jit(solution)/shard_map/all_to_all | solution.py:34
  157.8 22.0 %collective-permute-start.11 = (bf16[1792,256]{1,0:T(8,128)(2,1)S(1)}, bf16[1792,256]{1,0:T(8,128)(2,1)S(1)}, u32[]{:S(2)}, u32[]{:S(2)}) collective-permute-start(bf16[1792,256]{1,0:T(8,128)(2,1)S(1)} %slice.40), channel_id=1, source_target_pairs={{0,128},{8,136},{16,144},{24,152},{32,160},{40,168},{48,176},{56,1... | collective-permute-start | bytes 2752520 | tf_op jit(solution)/shard_map/ppermute | solution.py:111
  162.0 17.7 %collective-permute-start.12 = (f32[1792]{0:T(1024)S(1)}, f32[1792]{0:T(1024)S(1)}, u32[]{:S(2)}, u32[]{:S(2)}) collective-permute-start(f32[1792]{0:T(1024)S(1)} %add_add_fusion), channel_id=1, source_target_pairs={{0,128},{8,136},{16,144},{24,152},{32,160},{40,168},{48,176},{56,1... | collective-permute-start | bytes 21512 | tf_op jit(solution)/shard_map/ppermute | solution.py:110
  179.7 1.2 copy-start.4
  179.7 1.2 copy-start.5

commit v2 on v0

v2 whole, which is shorter than its diff:
```python
import functools
import math

import jax
import jax.numpy as jnp
from jax import lax
from jax.experimental import pallas as pl
from jax.experimental.pallas import tpu as pltpu
from jax.sharding import PartitionSpec as P

FFW = 14336
TOKENS = 4096

score_alpha = 0.5
decay_rate = 0.9
step_rate = 0.3
tiny_eps = 1e-08

Z = 8
MP = 8
PAIR_CORE = [(i, i ^ 1) for i in range(32)]
PAIR_X = [(i, i ^ 16) for i in range(32)]
VMEM_LIMIT = 16 * 1024 * 1024

f32, bf16 = jnp.float32, jnp.bfloat16


def ring_perm():
    out = []
    for i in range(32):
        x, z, c = i // 16, (i // 2) % Z, i % 2
        z = (z + (1 if c == 0 else -1)) % Z
        out.append((i, x * 16 + z * 2 + c))
    return out


RING = ring_perm()


def y_perm(dy):
    return [(j, (j // 4) * 4 + (j % 4 + dy) % 4) for j in range(MP)]


PAIR_X_HI = [(j, j ^ 4) for j in range(MP)]
AHEAD = (1, 3, 2)


def place():
    dp, mp = lax.axis_index("dp"), lax.axis_index("mp")
    return dp >> 4, (dp >> 1) & 7, dp & 1, mp >> 2, mp & 3


def rows_at(block, count):
    return pl.ds(pl.multiple_of(block * count, 32), count)


def vmem_call(kernel, out_shape, scratch, flops, n_after, name, *args):
    vmem = pl.BlockSpec(memory_space=pltpu.VMEM)
    specs = [vmem] * (len(args) - n_after)
    specs += [pl.BlockSpec(memory_space=pl.ANY)] * n_after
    moved = sum(a.size * a.dtype.itemsize for a in args)
    return pl.pallas_call(
        kernel,
        out_shape=out_shape,
        in_specs=specs,
        out_specs=jax.tree.map(lambda _: vmem, out_shape),
        scratch_shapes=scratch,
        compiler_params=pltpu.CompilerParams(vmem_limit_bytes=VMEM_LIMIT),
        cost_estimate=pl.CostEstimate(flops=0, bytes_accessed=0, transcendentals=0),
        name=name,
    )(*args)


def stack_kernel(n, *refs):
    rows = refs[0].shape[0]
    for k in range(n):
        refs[-1][k * rows : (k + 1) * rows, :] = refs[k][...]


def stack(blocks, after=()):
    rows, width = blocks[0].shape
    return vmem_call(
        functools.partial(stack_kernel, len(blocks)),
        jax.ShapeDtypeStruct((len(blocks) * rows, width), bf16),
        [],
        0,
        len(after),
        "stack",
        *blocks,
        *after,
    )


ROWS = 128


def forward_kernel(units, places, scale, more, *refs):
    blocks = refs[: sum(units)]
    packs, residuals = refs[sum(units) :][:4], refs[sum(units) + 4 :][:2]
    mine, ahead, sq_ref, wide, held = refs[-7], refs[-6:-3], refs[-3], refs[-2], refs[-1]
    x, z, c, x_hi, y = place()
    back = 2 * c - 1
    width, cols = blocks[0].shape[1], packs[0].shape[1]
    for k, ref in enumerate(packs):
        wide[:, k * cols : (k + 1) * cols] = ref[...]
    total = jnp.zeros((8, width), f32)
    first, row = 0, 0
    for unit in units:
        group = [block[...] for block in blocks[first : first + unit]]
        tokens = jnp.concatenate(group, axis=0) if unit > 1 else group[0]
        first += unit
        for side, ref in enumerate(residuals):
            left = side * 2 * cols
            weights = wide[:, left : left + 2 * cols]
            value = jnp.dot(tokens, weights, preferred_element_type=f32) * scale
            for k in range(tokens.shape[0] // ROWS):
                step, same = places[row // ROWS + k]
                at = (z + step * back) & 7
                core = c if same else 1 - c
                here = (x_hi << 2) + y == (x << 2) + (at >> 1)
                start = pl.multiple_of(((at & 1) << 8) + (core << 7), ROWS)
                extra = jnp.where(here, ref[pl.ds(start, ROWS), :].astype(f32), 0.0)
                part = value[k * ROWS : (k + 1) * ROWS]
                to = pl.ds(row + k * ROWS, ROWS)
                held[to, left : left + cols] = part[:, :cols] + extra
                held[to, left + cols : left + 2 * cols] = part[:, cols:]
        squares = jnp.square(tokens.astype(f32))
        total = total + jnp.sum(squares.reshape(-1, 8, width), axis=0)
        row += tokens.shape[0]
    total = jnp.sum(total, axis=0, keepdims=True)
    sq_ref[...] = total + refs[sum(units) + 6][...] if more else total
    quarter = held.shape[0] // 4
    mine[...] = held[rows_at(y, quarter), :]
    for out, dy in zip(ahead, AHEAD):
        out[...] = held[rows_at((y + dy) & 3, quarter), :].astype(bf16)


def forward(units, places, packs, squares=(), after=()):
    blocks = [block for unit in units for block in unit]
    rows = sum(block.shape[0] for block in blocks)
    width, cols = blocks[0].shape[1], packs[0].shape[1]
    piece = (rows // 4, 4 * cols)
    out = vmem_call(
        functools.partial(
            forward_kernel,
            [len(unit) for unit in units],
            places,
            1.0 / math.sqrt(FFW),
            len(squares),
        ),
        [jax.ShapeDtypeStruct(piece, f32)]
        + [jax.ShapeDtypeStruct(piece, bf16)] * 3
        + [jax.ShapeDtypeStruct((1, width), f32)],
        [pltpu.VMEM((width, 4 * cols), bf16), pltpu.VMEM((rows, 4 * cols), f32)],
        2 * rows * width * 4 * cols,
        len(after),
        "forward",
        *blocks,
        *packs,
        *squares,
        *after,
    )
    return out[0], out[1:4], out[4]


def merge_y_kernel(*refs):
    pieces, (keep, send) = refs[:4], refs[-2:]
    x_hi = place()[3]
    count = keep.shape[0]
    for out, half in ((send, 1 - x_hi), (keep, x_hi)):
        for r in range(0, count, 32):
            at = pl.ds(pl.multiple_of(half * count + r, 32), 32)
            total = pieces[0][at, :]
            for piece in pieces[1:]:
                total = total + piece[at, :].astype(f32)
            out[r : r + 32, :] = total.astype(out.dtype)


def merge_y(mine, got, after=()):
    rows, width = mine.shape
    return vmem_call(
        merge_y_kernel,
        [jax.ShapeDtypeStruct((rows // 2, width), t) for t in (f32, bf16)],
        [],
        4 * mine.size,
        len(after),
        "merge_y",
        mine,
        *got,
        *after,
    )


def merge_x_kernel(keep, got, *refs):
    refs[-1][...] = (keep[...] + got[...].astype(f32)).astype(bf16)


def merge_x(keep, got, after=()):
    return vmem_call(
        merge_x_kernel,
        jax.ShapeDtypeStruct(keep.shape, bf16),
        [],
        keep.size,
        len(after),
        "merge_x",
        keep,
        got,
        *after,
    )


def pair_kernel(n, mine, got, *refs):
    outs = refs[-n:]
    x_hi = place()[3]
    count, part = mine.shape[0], outs[0].shape[1]
    for piece, at in ((mine, x_hi), (got, 1 - x_hi)):
        for k, out in enumerate(outs):
            out[rows_at(at, count), :] = piece[:, k * part : (k + 1) * part]


def pair(mine, got, parts, after=()):
    count, width = mine.shape
    return vmem_call(
        functools.partial(pair_kernel, parts),
        [jax.ShapeDtypeStruct((2 * count, width // parts), bf16)] * parts,
        [],
        2 * mine.size,
        len(after),
        "pair",
        mine,
        got,
        *after,
    )


def backward_kernel(n, scale, left, *refs):
    blocks, targets, o_ref, held = refs[:n], refs[n : n + 4], refs[-2], refs[-1]
    y = place()[4]
    width, cols = blocks[0].shape[1], held.shape[1]
    for ref, dy in zip(targets, (0,) + AHEAD):
        held[rows_at((y - dy) & 3, ref.shape[0]), :] = ref[...]
    for at in range(0, width, 256):
        tokens = jnp.concatenate([block[:, at : at + 256] for block in blocks], axis=0)
        value = lax.dot_general(
            tokens, held[...], (((0,), (0,)), ((), ())), preferred_element_type=f32
        )
        value = value * scale
        if left is not None:
            value = value + refs[n + 4][at : at + 256, left : left + cols]
        o_ref[at : at + 256, :] = value.astype(o_ref.dtype)


def backward(blocks, targets, dtype, init=(), left=None):
    n, width, cols = len(blocks), blocks[0].shape[1], targets[0].shape[1]
    rows = sum(block.shape[0] for block in blocks)
    return vmem_call(
        functools.partial(backward_kernel, n, 1.0 / math.sqrt(TOKENS), left),
        jax.ShapeDtypeStruct((width, cols), dtype),
        [pltpu.VMEM((rows, cols), bf16)],
        2 * rows * width * cols,
        0,
        "backward",
        *blocks,
        *targets,
        *init,
    )


def gate_kernel(*refs):
    pass


def gate(value, *after):
    hbm = pl.BlockSpec(memory_space=pl.ANY)
    return pl.pallas_call(
        gate_kernel,
        out_shape=jax.ShapeDtypeStruct(value.shape, value.dtype),
        in_specs=[hbm] * (1 + len(after)),
        out_specs=hbm,
        input_output_aliases={0: 0},
        compiler_params=pltpu.CompilerParams(vmem_limit_bytes=1024 * 1024),
        cost_estimate=pl.CostEstimate(flops=0, bytes_accessed=0, transcendentals=0),
        name="gate",
    )(value, *after)


def body(hidden, residual, down_weight, mask, state):
    cols = down_weight.shape[1]
    keep = mask == 1

    def ring(value):
        return lax.ppermute(value, "dp", RING)

    def swap(value):
        return lax.ppermute(value, "dp", PAIR_CORE)

    def across(value):
        return lax.ppermute(value, "dp", PAIR_X)

    def around(pieces):
        return [lax.ppermute(v, "mp", y_perm(dy)) for v, dy in zip(pieces, AHEAD)]

    def over(value):
        return lax.ppermute(value, "mp", PAIR_X_HI)

    sib = swap(hidden)
    a1 = ring(hidden)
    b1 = ring(sib)
    weight_x = across(down_weight)
    pruned = jnp.where(keep, jnp.zeros_like(down_weight), -down_weight)
    pruned_x = across(pruned)
    residual_x = across(residual)
    a1 = gate(a1, pruned)
    a2 = ring(a1)
    sa1 = swap(a1)
    b2 = ring(b1)
    sb1 = swap(b1)
    a2 = gate(a2, sa1, sb1, weight_x, pruned_x)
    a3 = ring(a2)
    sa2 = swap(a2)
    b2 = gate(b2, residual_x)
    b3 = ring(b2)

    packs = (down_weight, pruned, weight_x, pruned_x, residual, residual_x)
    early = [[hidden, sib], [a1, b1], [sa1, sb1], [a2, sa2]]
    places = [(0, 1), (0, 0), (1, 1), (1, 0), (-1, 0), (-1, 1), (2, 1), (-2, 0)]
    mine0, ahead0, squares0 = forward(early, places, packs)
    got0 = around(ahead0)
    a3 = gate(a3, squares0)
    a4 = ring(a3)
    keep0, send0 = merge_y(mine0, got0)
    b3 = gate(b3, keep0)
    s4 = stack([b2, a3, b3, a4])
    t4 = swap(s4)
    sent0 = over(send0)
    late = [s4, t4]
    places = [(2, 0), (3, 1), (3, 0), (4, 1), (-2, 1), (-3, 0), (-3, 1), (4, 0)]
    mine1, ahead1, squares = forward([[s4], [t4]], places, packs, [squares0], [sent0])
    got1 = around(ahead1)
    squares_x = across(squares)

    early = [block for unit in early for block in unit]
    sum0 = merge_x(keep0, sent0)
    keep1, send1 = merge_y(mine1, got1, [sum0])
    (both0,) = pair(sum0, over(sum0), 1, [keep1])
    sum1 = merge_x(keep1, over(send1), [both0])
    init = backward(early, [both0] + around([both0] * 3), f32)
    own1, other1 = pair(sum1, over(sum1), 2, [init])
    other1 = [other1] + around([other1] * 3)
    own1 = [own1] + around([own1] * 3)
    arrived = across(backward(late, other1, bf16, [init], 2 * cols))
    grads = backward(late, own1, f32, [init], 0)
    colsq = squares + squares_x
    grads = grads + arrived.astype(f32)

    grad_out = grads[:, :cols]
    grad_step = jnp.where(keep, grads[:, cols:], jnp.float32(0.0))
    rms = jnp.sqrt(colsq.reshape(-1) / TOKENS + 1e-05)
    weight_f = down_weight.astype(f32)
    scores = jnp.abs(weight_f) * (score_alpha * jnp.abs(grad_out) + rms[:, None])
    new_state = decay_rate * state + (1.0 - decay_rate) * grad_step * grad_step
    moved = weight_f - step_rate * grad_step / (jnp.sqrt(new_state) + tiny_eps)
    new_weight = jnp.where(keep, moved, jnp.float32(0.0)).astype(bf16)
    return (scores, new_weight, new_state)


def solution(mesh):
    return jax.shard_map(
        body,
        mesh=mesh,
        in_specs=(P("dp", "mp"), P("mp", "dp"), P("mp", "dp"), P("mp", "dp"), P("mp", "dp")),
        out_specs=(P("mp", "dp"), P("mp", "dp"), P("mp", "dp")),
        check_vma=False,
    )
```

time: 291 us -> 133 us (0.46)
  waiting for transfers between devices: 182 us -> 67.4 us
  blocking collectives: 57.8 us -> 0 us
  starting transfers between devices: 0.12 us -> 47.9 us
  matrix products: 24.4 us -> 0 us
  between operations: 13.8 us -> 0.85 us
  Pallas kernels: 0 us -> 9.88 us
  local copies, waits for them, and re-layouts: 8.33 us -> 0.99 us
    all_gather x2 -> x0, waiting for transfers between devices: 92.1 us -> none  [the longest x1 91.1 us: body(): gathered = lax.all_gather(hidden, 'dp', axis=0, tiled=True)]
    reduce_scatter x1 -> x0, waiting for transfers between devices: 88.7 us -> none  [body(): lax.psum_scatter(partial_value, 'mp', scatter_dimension=0, tiled=True)]
    ppermute x0 -> x36, waiting for transfers between devices: none -> 67.4 us  [the longest x15 27.6 us: around(): return [lax.ppermute(v, 'mp', y_perm(dy)) for v, dy in zip(pieces, AHEAD)]]
    psum x1 -> x0, blocking collectives: 57.8 us -> none  [body(): lax.psum(jnp.sum(jnp.square(hidden.astype(jnp.float32)), axis=0), 'dp')]
    ppermute x0 -> x36, starting transfers between devices: none -> 47.9 us  [the longest x15 20 us: around(): return [lax.ppermute(v, 'mp', y_perm(dy)) for v, dy in zip(pieces, AHEAD)]]
    dot_general x2 -> x0, matrix products: 24.4 us -> none  [the longest x1 16 us: body(): jnp.dot(gathered, paired, preferred_element_type=jnp.float32) * inv_width]
    pallas_call x0 -> x17, Pallas kernels: none -> 9.88 us  [the longest x12 9.88 us: vmem_call(): pl.pallas_call(kernel, out_shape=out_shape, in_specs=specs, out_specs=jax...]
    unnamed x15 -> x8, local copies, waits for them, and re-layouts: 7.36 us -> 0.99 us
  transfers between devices with their start and end apart: 3 -> 36, of which waited for: 3 -> 20; matrix products, arithmetic and copies ran while one was open for 1% -> 1% of each run, Pallas kernels for 0% -> 5%
where the time goes in v2:
time: 133 us; the launch traced here: 131 us
  waiting for transfers between devices  67.4 us (51%)
  starting transfers between devices  47.9 us (36%)
  Pallas kernels  9.88 us (7%)
  other arithmetic  3.95 us (3%)
    ppermute x15, waiting for transfers between devices, around(): return [lax.ppermute(v, 'mp', y_perm(dy)) for v, dy in zip(pieces, AHEAD)]  27.6 us
    ppermute x5, waiting for transfers between devices, across(): return lax.ppermute(value, 'dp', PAIR_X)  22.7 us
    ppermute x15, starting transfers between devices, around(): return [lax.ppermute(v, 'mp', y_perm(dy)) for v, dy in zip(pieces, AHEAD)]  20 us
    pallas_call x12, Pallas kernels, vmem_call(): pl.pallas_call(kernel, out_shape=out_shape, in_specs=specs, out_specs=jax...  9.88 us
    ppermute x4, starting transfers between devices, over(): return lax.ppermute(value, 'mp', PAIR_X_HI)  8.86 us
    ppermute x7, waiting for transfers between devices, ring(): return lax.ppermute(value, 'dp', RING)  8.68 us
    ppermute x4, waiting for transfers between devices, over(): return lax.ppermute(value, 'mp', PAIR_X_HI)  8.45 us
    ppermute x5, starting transfers between devices, swap(): return lax.ppermute(value, 'dp', PAIR_CORE)  6.81 us
  transfers between devices with their start and end apart: 36, of which 20 were waited for; matrix products, arithmetic and copies ran while one was open for 1% of the time, Pallas kernels for 5%

profile of v2, /device:TPU:2, one launch (start us, length us, event | category | flops | bytes accessed | tf_op | source)
XLA Modules:
  0.0 131.1 jit_solution(8772567823152232962)
XLA Ops:
  0.7 2.0 %collective-permute-start.4 = (bf16[128,1792]{1,0:T(8,128)(2,1)}, bf16[128,1792]{1,0:T(8,128)(2,1)S(1)}, u32[]{:S(2)}, u32[]{:S(2)}) collective-permute-start(bf16[128,1792]{1,0:T(8,128)(2,1)} %refs_0_.3), channel_id=1, source_target_pairs={{0,16},{8,120},{16,32},{24,8},{32,48},{40,24},{48,64},{56,40},{64,... | collective-permute-start | bytes 1376264 | tf_op jit(solution)/shard_map/ppermute | solution.py:292
  3.3 1.9 %collective-permute-start.1 = (bf16[128,1792]{1,0:T(8,128)(2,1)S(1)}, bf16[128,1792]{1,0:T(8,128)(2,1)S(1)}, u32[]{:S(2)}, u32[]{:S(2)}) collective-permute-start(bf16[128,1792]{1,0:T(8,128)(2,1)S(1)} %collective-permute-done.refs_1_), channel_id=1, source_target_pairs={{0,16},{8,120},{16,32},{24,8},{32,48},{40,24},{48,64},{56,40},{64,... | collective-permute-start | bytes 1376264 | tf_op jit(solution)/shard_map/ppermute | solution.py:292
  5.2 1.5 %negate_select_fusion = (bf16[1792,128]{1,0:T(8,128)(2,1)S(1)}, pred[1792,128]{1,0:T(8,128)(4,1)S(1)}) fusion(bf16[1792,128]{1,0:T(8,128)(2,1)} %refs_2_.1, s32[1792,128]{1,0:T(8,128)} %param.8), kind=kLoop, calls=%fused_computation.12 | loop fusion | flops 688128 | bytes 2064384 | tf_op jit(solution)/shard_map/jit(_where)/select_n | solution.py:310
  6.7 1.6 %collective-permute-start.9 = (bf16[1792,128]{1,0:T(8,128)(2,1)S(1)}, bf16[1792,128]{1,0:T(8,128)(2,1)S(1)}, u32[]{:S(2)}, u32[]{:S(2)}) collective-permute-start(bf16[1792,128]{1,0:T(8,128)(2,1)S(1)} %get-tuple-element.37.refs_1_.refs_9_.refs_3_), channel_id=1, source_target_pairs={{0,128},{8,136},{16,144},{24,152},{32,160},{40,168},{48,176},{56,1... | collective-permute-start | bytes 1376264 | tf_op jit(solution)/shard_map/ppermute | solution.py:298
  8.3 5.0 %collective-permute-done.4.refs_0_ = bf16[128,1792]{1,0:T(8,128)(2,1)S(1)} collective-permute-done((bf16[128,1792]{1,0:T(8,128)(2,1)}, bf16[128,1792]{1,0:T(8,128)(2,1)S(1)}, u32[]{:S(2)}, u32[]{:S(2)}) %collective-permute-start.4) | collective-permute-done | bytes 458784 | tf_op jit(solution)/shard_map/ppermute | solution.py:292
  13.3 2.2 %collective-permute-start.6 = (bf16[128,1792]{1,0:T(8,128)(2,1)S(1)}, bf16[128,1792]{1,0:T(8,128)(2,1)S(1)}, u32[]{:S(2)}, u32[]{:S(2)}) collective-permute-start(bf16[128,1792]{1,0:T(8,128)(2,1)S(1)} %gate.6.refs_2_), channel_id=1, source_target_pairs={{0,8},{8,0},{16,24},{24,16},{32,40},{40,32},{48,56},{56,48},{64,72... | collective-permute-start | bytes 1376264 | tf_op jit(solution)/shard_map/ppermute | solution.py:295
  15.6 2.7 %collective-permute-done.1.refs_3_ = bf16[128,1792]{1,0:T(8,128)(2,1)S(1)} collective-permute-done((bf16[128,1792]{1,0:T(8,128)(2,1)S(1)}, bf16[128,1792]{1,0:T(8,128)(2,1)S(1)}, u32[]{:S(2)}, u32[]{:S(2)}) %collective-permute-start.1) | collective-permute-done | bytes 458784 | tf_op jit(solution)/shard_map/ppermute | solution.py:292
  18.3 4.7 %collective-permute-done.9.refs_4_.refs_11_.refs_5_ = bf16[1792,128]{1,0:T(8,128)(2,1)S(1)} collective-permute-done((bf16[1792,128]{1,0:T(8,128)(2,1)S(1)}, bf16[1792,128]{1,0:T(8,128)(2,1)S(1)}, u32[]{:S(2)}, u32[]{:S(2)}) %collective-permute-start.9) | collective-permute-done | bytes 458784 | tf_op jit(solution)/shard_map/ppermute | solution.py:298
  23.2 3.2 %collective-permute-start.11 = (bf16[128,1792]{1,0:T(8,128)(2,1)S(1)}, bf16[128,1792]{1,0:T(8,128)(2,1)S(1)}, u32[]{:S(2)}, u32[]{:S(2)}) collective-permute-start(bf16[128,1792]{1,0:T(8,128)(2,1)S(1)} %gate.7.refs_6_), channel_id=1, source_target_pairs={{0,8},{8,0},{16,24},{24,16},{32,40},{40,32},{48,56},{56,48},{64,72... | collective-permute-start | bytes 1376264 | tf_op jit(solution)/shard_map/ppermute | solution.py:295
  26.4 1.5 %collective-permute-start.3 = (bf16[512,128]{1,0:T(8,128)(2,1)S(1)}, bf16[512,128]{1,0:T(8,128)(2,1)S(1)}, u32[]{:S(2)}, u32[]{:S(2)}) collective-permute-start(bf16[512,128]{1,0:T(8,128)(2,1)S(1)} %copy-done.2), channel_id=1, source_target_pairs={{0,128},{8,136},{16,144},{24,152},{32,160},{40,168},{48,176},{56,1... | collective-permute-start | bytes 393224 | tf_op jit(solution)/shard_map/ppermute | solution.py:298
  27.9 3.4 %collective-permute-done.3.refs_1_.refs_13_.refs_7_ = bf16[512,128]{1,0:T(8,128)(2,1)S(1)} collective-permute-done((bf16[512,128]{1,0:T(8,128)(2,1)S(1)}, bf16[512,128]{1,0:T(8,128)(2,1)S(1)}, u32[]{:S(2)}, u32[]{:S(2)}) %collective-permute-start.3) | collective-permute-done | bytes 131104 | tf_op jit(solution)/shard_map/ppermute | solution.py:298
  31.4 2.3 %collective-permute-start.12 = (bf16[128,1792]{1,0:T(8,128)(2,1)S(1)}, bf16[128,1792]{1,0:T(8,128)(2,1)S(1)}, u32[]{:S(2)}, u32[]{:S(2)}) collective-permute-start(bf16[128,1792]{1,0:T(8,128)(2,1)S(1)} %gate.5.refs_0_), channel_id=1, source_target_pairs={{0,16},{8,120},{16,32},{24,8},{32,48},{40,24},{48,64},{56,40},{64,... | collective-permute-start | bytes 1376264 | tf_op jit(solution)/shard_map/ppermute | solution.py:292
  33.6 2.4 %forward.2 = (f32[256,512]{1,0:T(8,128)S(1)}, bf16[256,512]{1,0:T(8,128)(2,1)S(1)}, bf16[256,512]{1,0:T(8,128)(2,1)S(1)}, bf16[256,512]{1,0:T(8,128)(2,1)S(1)}, f32[1,1792]{1,0:T(1,128)S(1)}) custom-call(bf16[128,1792]{1,0:T(8,128)(2,1)S(1)} %copy-done.1, bf16[128,1792]{1,0:T(8,128)(2,1)S(1)} %collective-permute-done.refs_1_, ...), custom_call_target="tpu_custom_call" | custom-call | tf_op jit(solution)/shard_map/forward/pallas_call | solution.py:62
  37.1 1.6 %collective-permute-start.13 = (bf16[256,512]{1,0:T(8,128)(2,1)S(1)}, bf16[256,512]{1,0:T(8,128)(2,1)S(1)}, u32[]{:S(2)}, u32[]{:S(2)}) collective-permute-start(bf16[256,512]{1,0:T(8,128)(2,1)S(1)} %get-tuple-element.21), channel_id=1, source_target_pairs={{0,1},{1,2},{2,3},{3,0},{4,5},{5,6},{6,7},{7,4},{8,9},{9,10},{10,1... | collective-permute-start | bytes 786440 | tf_op jit(solution)/shard_map/ppermute | solution.py:301
  38.7 1.7 %collective-permute-start.14 = (bf16[256,512]{1,0:T(8,128)(2,1)S(1)}, bf16[256,512]{1,0:T(8,128)(2,1)S(1)}, u32[]{:S(2)}, u32[]{:S(2)}) collective-permute-start(bf16[256,512]{1,0:T(8,128)(2,1)S(1)} %get-tuple-element.22), channel_id=1, source_target_pairs={{0,3},{1,0},{2,1},{3,2},{4,7},{5,4},{6,5},{7,6},{8,11},{9,8},{10,9... | collective-permute-start | bytes 786440 | tf_op jit(solution)/shard_map/ppermute | solution.py:301
  40.4 2.0 %collective-permute-start.15 = (bf16[256,512]{1,0:T(8,128)(2,1)S(1)}, bf16[256,512]{1,0:T(8,128)(2,1)S(1)}, u32[]{:S(2)}, u32[]{:S(2)}) collective-permute-start(bf16[256,512]{1,0:T(8,128)(2,1)S(1)} %get-tuple-element.23), channel_id=1, source_target_pairs={{0,2},{1,3},{2,0},{3,1},{4,6},{5,7},{6,4},{7,5},{8,10},{9,11},{10,... | collective-permute-start | bytes 786440 | tf_op jit(solution)/shard_map/ppermute | solution.py:301
  42.3 3.7 %collective-permute-done.13.refs_1_ = bf16[256,512]{1,0:T(8,128)(2,1)S(1)} collective-permute-done((bf16[256,512]{1,0:T(8,128)(2,1)S(1)}, bf16[256,512]{1,0:T(8,128)(2,1)S(1)}, u32[]{:S(2)}, u32[]{:S(2)}) %collective-permute-start.13) | collective-permute-done | bytes 262176 | tf_op jit(solution)/shard_map/ppermute | solution.py:301
  46.8 6.2 %collective-permute-done.15.refs_3_ = bf16[256,512]{1,0:T(8,128)(2,1)S(1)} collective-permute-done((bf16[256,512]{1,0:T(8,128)(2,1)S(1)}, bf16[256,512]{1,0:T(8,128)(2,1)S(1)}, u32[]{:S(2)}, u32[]{:S(2)}) %collective-permute-start.15) | collective-permute-done | bytes 262176 | tf_op jit(solution)/shard_map/ppermute | solution.py:301
  53.3 1.3 collective-permute-start.17
  54.6 2.1 %collective-permute-start.18 = (bf16[128,512]{1,0:T(8,128)(2,1)S(1)}, bf16[128,512]{1,0:T(8,128)(2,1)S(1)}, u32[]{:S(2)}, u32[]{:S(2)}) collective-permute-start(bf16[128,512]{1,0:T(8,128)(2,1)S(1)} %get-tuple-element.25), channel_id=1, source_target_pairs={{0,4},{1,5},{2,6},{3,7},{4,0},{5,1},{6,2},{7,3},{8,12},{9,13},{10,... | collective-permute-start | bytes 393224 | tf_op jit(solution)/shard_map/ppermute | solution.py:304
  56.7 4.9 %collective-permute-done.18.refs_9_.got = bf16[128,512]{1,0:T(8,128)(2,1)S(1)} collective-permute-done((bf16[128,512]{1,0:T(8,128)(2,1)S(1)}, bf16[128,512]{1,0:T(8,128)(2,1)S(1)}, u32[]{:S(2)}, u32[]{:S(2)}) %collective-permute-start.18) | collective-permute-done | bytes 131104 | tf_op jit(solution)/shard_map/ppermute | solution.py:304
  61.6 2.4 %forward.3 = (f32[256,512]{1,0:T(8,128)S(1)}, bf16[256,512]{1,0:T(8,128)(2,1)S(1)}, bf16[256,512]{1,0:T(8,128)(2,1)S(1)}, bf16[256,512]{1,0:T(8,128)(2,1)S(1)}, f32[1,1792]{1,0:T(1,128)S(1)}) custom-call(bf16[512,1792]{1,0:T(8,128)(2,1)S(1)} %stack.1.refs_0_, bf16[512,1792]{1,0:T(8,128)(2,1)S(1)} %collective-permute-done.17.refs_1_, ...), custom_call_target="tpu_custom_call" | custom-call | tf_op jit(solution)/shard_map/forward/pallas_call | solution.py:62
  64.0 1.5 %collective-permute-start.19 = (bf16[256,512]{1,0:T(8,128)(2,1)S(1)}, bf16[256,512]{1,0:T(8,128)(2,1)S(1)}, u32[]{:S(2)}, u32[]{:S(2)}) collective-permute-start(bf16[256,512]{1,0:T(8,128)(2,1)S(1)} %get-tuple-element.27), channel_id=1, source_target_pairs={{0,1},{1,2},{2,3},{3,0},{4,5},{5,6},{6,7},{7,4},{8,9},{9,10},{10,1... | collective-permute-start | bytes 786440 | tf_op jit(solution)/shard_map/ppermute | solution.py:301
  65.5 1.8 %collective-permute-start.20 = (bf16[256,512]{1,0:T(8,128)(2,1)S(1)}, bf16[256,512]{1,0:T(8,128)(2,1)S(1)}, u32[]{:S(2)}, u32[]{:S(2)}) collective-permute-start(bf16[256,512]{1,0:T(8,128)(2,1)S(1)} %get-tuple-element.28), channel_id=1, source_target_pairs={{0,3},{1,0},{2,1},{3,2},{4,7},{5,4},{6,5},{7,6},{8,11},{9,8},{10,9... | collective-permute-start | bytes 786440 | tf_op jit(solution)/shard_map/ppermute | solution.py:301
  67.7 2.2 %collective-permute-start.23 = (bf16[128,512]{1,0:T(8,128)(2,1)S(1)}, bf16[128,512]{1,0:T(8,128)(2,1)S(1)}, u32[]{:S(2)}, u32[]{:S(2)}) collective-permute-start(bf16[128,512]{1,0:T(8,128)(2,1)S(1)} %merge_x.2.refs_4_.mine), channel_id=1, source_target_pairs={{0,4},{1,5},{2,6},{3,7},{4,0},{5,1},{6,2},{7,3},{8,12},{9,13},{10,... | collective-permute-start | bytes 393224 | tf_op jit(solution)/shard_map/ppermute | solution.py:304
  69.9 4.4 %collective-permute-done.19.refs_1_ = bf16[256,512]{1,0:T(8,128)(2,1)S(1)} collective-permute-done((bf16[256,512]{1,0:T(8,128)(2,1)S(1)}, bf16[256,512]{1,0:T(8,128)(2,1)S(1)}, u32[]{:S(2)}, u32[]{:S(2)}) %collective-permute-start.19) | collective-permute-done | bytes 262176 | tf_op jit(solution)/shard_map/ppermute | solution.py:301
  74.3 3.4 %collective-permute-done.20.refs_2_ = bf16[256,512]{1,0:T(8,128)(2,1)S(1)} collective-permute-done((bf16[256,512]{1,0:T(8,128)(2,1)S(1)}, bf16[256,512]{1,0:T(8,128)(2,1)S(1)}, u32[]{:S(2)}, u32[]{:S(2)}) %collective-permute-start.20) | collective-permute-done | bytes 262176 | tf_op jit(solution)/shard_map/ppermute | solution.py:301
  77.7 0.9 collective-permute-done.21.refs_3_
  78.8 1.2 collective-permute-start.25
  80.0 2.1 %collective-permute-start.26 = (bf16[256,512]{1,0:T(8,128)(2,1)S(1)}, bf16[256,512]{1,0:T(8,128)(2,1)S(1)}, u32[]{:S(2)}, u32[]{:S(2)}) collective-permute-start(bf16[256,512]{1,0:T(8,128)(2,1)S(1)} %pair.2.refs_0_.refs_8_), channel_id=1, source_target_pairs={{0,3},{1,0},{2,1},{3,2},{4,7},{5,4},{6,5},{7,6},{8,11},{9,8},{10,9... | collective-permute-start | bytes 786440 | tf_op jit(solution)/shard_map/ppermute | solution.py:301
  82.1 2.1 %collective-permute-start.22 = (bf16[128,512]{1,0:T(8,128)(2,1)S(1)}, bf16[128,512]{1,0:T(8,128)(2,1)S(1)}, u32[]{:S(2)}, u32[]{:S(2)}) collective-permute-start(bf16[128,512]{1,0:T(8,128)(2,1)S(1)} %get-tuple-element.31), channel_id=1, source_target_pairs={{0,4},{1,5},{2,6},{3,7},{4,0},{5,1},{6,2},{7,3},{8,12},{9,13},{10,... | collective-permute-start | bytes 393224 | tf_op jit(solution)/shard_map/ppermute | solution.py:304
  84.2 1.0 collective-permute-start.27
  85.2 3.4 %collective-permute-done.22.got = bf16[128,512]{1,0:T(8,128)(2,1)S(1)} collective-permute-done((bf16[128,512]{1,0:T(8,128)(2,1)S(1)}, bf16[128,512]{1,0:T(8,128)(2,1)S(1)}, u32[]{:S(2)}, u32[]{:S(2)}) %collective-permute-start.22) | collective-permute-done | bytes 131104 | tf_op jit(solution)/shard_map/ppermute | solution.py:304
  88.6 2.4 %collective-permute-start.24 = (bf16[128,512]{1,0:T(8,128)(2,1)S(1)}, bf16[128,512]{1,0:T(8,128)(2,1)S(1)}, u32[]{:S(2)}, u32[]{:S(2)}) collective-permute-start(bf16[128,512]{1,0:T(8,128)(2,1)S(1)} %merge_x.3.mine), channel_id=1, source_target_pairs={{0,4},{1,5},{2,6},{3,7},{4,0},{5,1},{6,2},{7,3},{8,12},{9,13},{10,... | collective-permute-start | bytes 393224 | tf_op jit(solution)/shard_map/ppermute | solution.py:304
  91.5 1.5 %collective-permute-done.27.refs_11_ = bf16[256,512]{1,0:T(8,128)(2,1)S(1)} collective-permute-done((bf16[256,512]{1,0:T(8,128)(2,1)S(1)}, bf16[256,512]{1,0:T(8,128)(2,1)S(1)}, u32[]{:S(2)}, u32[]{:S(2)}) %collective-permute-start.27) | collective-permute-done | bytes 262176 | tf_op jit(solution)/shard_map/ppermute | solution.py:301
  93.0 2.2 %backward.3.refs_0_.refs_6_ = f32[1792,512]{1,0:T(8,128)S(1)} custom-call(bf16[128,1792]{1,0:T(8,128)(2,1)S(1)} %copy-done.1, bf16[128,1792]{1,0:T(8,128)(2,1)S(1)} %collective-permute-done.refs_1_, bf16[128,1792]{1,0:T(8,128)(2,1)S(1)} %gate.6.refs_2_, bf16[128,1792]{1,0:T(8,128)(2,1)S(1)} %collective-permute-done.1.refs_3_, ...), custom_call_target="tpu_custom_call" | custom-call | tf_op jit(solution)/shard_map/backward/pallas_call | solution.py:62
  95.4 0.8 collective-permute-start.31
  96.2 2.5 %collective-permute-start.32 = (bf16[256,256]{1,0:T(8,128)(2,1)S(1)}, bf16[256,256]{1,0:T(8,128)(2,1)S(1)}, u32[]{:S(2)}, u32[]{:S(2)}) collective-permute-start(bf16[256,256]{1,0:T(8,128)(2,1)S(1)} %get-tuple-element.33.refs_2_), channel_id=1, source_target_pairs={{0,3},{1,0},{2,1},{3,2},{4,7},{5,4},{6,5},{7,6},{8,11},{9,8},{10,9... | collective-permute-start | bytes 393224 | tf_op jit(solution)/shard_map/ppermute | solution.py:301
  99.0 4.1 %collective-permute-done.31.refs_3_ = bf16[256,256]{1,0:T(8,128)(2,1)S(1)} collective-permute-done((bf16[256,256]{1,0:T(8,128)(2,1)S(1)}, bf16[256,256]{1,0:T(8,128)(2,1)S(1)}, u32[]{:S(2)}, u32[]{:S(2)}) %collective-permute-start.31) | collective-permute-done | bytes 131104 | tf_op jit(solution)/shard_map/ppermute | solution.py:301
  103.1 2.1 %collective-permute-done.33.refs_5_ = bf16[256,256]{1,0:T(8,128)(2,1)S(1)} collective-permute-done((bf16[256,256]{1,0:T(8,128)(2,1)S(1)}, bf16[256,256]{1,0:T(8,128)(2,1)S(1)}, u32[]{:S(2)}, u32[]{:S(2)}) %collective-permute-start.33) | collective-permute-done | bytes 131104 | tf_op jit(solution)/shard_map/ppermute | solution.py:301
  105.2 1.2 backward.5
  106.4 1.0 collective-permute-start.34
  107.4 3.2 %collective-permute-start.29 = (bf16[256,256]{1,0:T(8,128)(2,1)S(1)}, bf16[256,256]{1,0:T(8,128)(2,1)S(1)}, u32[]{:S(2)}, u32[]{:S(2)}) collective-permute-start(bf16[256,256]{1,0:T(8,128)(2,1)S(1)} %get-tuple-element.32.refs_2_), channel_id=1, source_target_pairs={{0,3},{1,0},{2,1},{3,2},{4,7},{5,4},{6,5},{7,6},{8,11},{9,8},{10,9... | collective-permute-start | bytes 393224 | tf_op jit(solution)/shard_map/ppermute | solution.py:301
  110.6 1.2 collective-permute-start.35
  111.8 14.6 %collective-permute-done.35 = f32[1,1792]{1,0:T(1,128)S(1)} collective-permute-done((f32[1,1792]{1,0:T(1,128)S(1)}, f32[1,1792]{1,0:T(1,128)S(1)}, u32[]{:S(2)}, u32[]{:S(2)}) %collective-permute-start.35) | collective-permute-done | bytes 7200 | tf_op jit(solution)/shard_map/ppermute | solution.py:298
  126.5 1.2 backward.4
  127.9 1.0 copy-done.3
  128.9 2.2 %fusion.2 = (bf16[1792,128]{1,0:T(8,128)(2,1)}, f32[1792,128]{1,0:T(8,128)}, f32[1792,128]{1,0:T(8,128)}) fusion(pred[1792,128]{1,0:T(8,128)(4,1)S(1)} %get-tuple-element.38, bf16[1792,128]{1,0:T(8,128)(2,1)S(1)} %copy-done, f32[1792,256]{1,0:T(8,128)S(1)} %convert_add_fusion, f32[1792,128]{1,0:T(8,128)S(1)} %copy-done.3, f32[1792]{0:T(1024)S(1)} %sqrt_reduce_fusion), kind=kLoop, calls=%fused_computation.6 | loop fusion | flops 3899392 | bytes 5741568 | tf_op jit(solution)/shard_map/convert_element_type | solution.py:363
  (53 shorter events, 4.8 us)
Async XLA Ops:
  0.6 2.6 %collective-permute-start = (bf16[128,1792]{1,0:T(8,128)(2,1)}, bf16[128,1792]{1,0:T(8,128)(2,1)S(1)}, u32[]{:S(2)}, u32[]{:S(2)}) collective-permute-start(bf16[128,1792]{1,0:T(8,128)(2,1)} %refs_0_.3), channel_id=1, source_target_pairs={{0,8},{8,0},{16,24},{24,16},{32,40},{40,32},{48,56},{56,48},{64,72... | collective-permute-start | bytes 1376264 | tf_op jit(solution)/shard_map/ppermute | solution.py:295
  0.7 12.6 %collective-permute-start.4 = (bf16[128,1792]{1,0:T(8,128)(2,1)}, bf16[128,1792]{1,0:T(8,128)(2,1)S(1)}, u32[]{:S(2)}, u32[]{:S(2)}) collective-permute-start(bf16[128,1792]{1,0:T(8,128)(2,1)} %refs_0_.3), channel_id=1, source_target_pairs={{0,16},{8,120},{16,32},{24,8},{32,48},{40,24},{48,64},{56,40},{64,... | collective-permute-start | bytes 1376264 | tf_op jit(solution)/shard_map/ppermute | solution.py:292
  2.7 15.5 %collective-permute-start.8 = (bf16[1792,128]{1,0:T(8,128)(2,1)}, bf16[1792,128]{1,0:T(8,128)(2,1)S(1)}, u32[]{:S(2)}, u32[]{:S(2)}) collective-permute-start(bf16[1792,128]{1,0:T(8,128)(2,1)} %refs_2_.1), channel_id=1, source_target_pairs={{0,128},{8,136},{16,144},{24,152},{32,160},{40,168},{48,176},{56,1... | collective-permute-start | bytes 1376264 | tf_op jit(solution)/shard_map/ppermute | solution.py:298
  3.3 15.0 %collective-permute-start.1 = (bf16[128,1792]{1,0:T(8,128)(2,1)S(1)}, bf16[128,1792]{1,0:T(8,128)(2,1)S(1)}, u32[]{:S(2)}, u32[]{:S(2)}) collective-permute-start(bf16[128,1792]{1,0:T(8,128)(2,1)S(1)} %collective-permute-done.refs_1_), channel_id=1, source_target_pairs={{0,16},{8,120},{16,32},{24,8},{32,48},{40,24},{48,64},{56,40},{64,... | collective-permute-start | bytes 1376264 | tf_op jit(solution)/shard_map/ppermute | solution.py:292
  6.7 19.7 %copy-start.2 = (bf16[512,128]{1,0:T(8,128)(2,1)S(1)}, bf16[512,128]{1,0:T(8,128)(2,1)}, u32[]{:S(2)}) copy-start(bf16[512,128]{1,0:T(8,128)(2,1)} %refs_6_.1) | copy-start | bytes 393220
  6.7 16.3 %collective-permute-start.9 = (bf16[1792,128]{1,0:T(8,128)(2,1)S(1)}, bf16[1792,128]{1,0:T(8,128)(2,1)S(1)}, u32[]{:S(2)}, u32[]{:S(2)}) collective-permute-start(bf16[1792,128]{1,0:T(8,128)(2,1)S(1)} %get-tuple-element.37.refs_1_.refs_9_.refs_3_), channel_id=1, source_target_pairs={{0,128},{8,136},{16,144},{24,152},{32,160},{40,168},{48,176},{56,1... | collective-permute-start | bytes 1376264 | tf_op jit(solution)/shard_map/ppermute | solution.py:298
  13.3 20.3 %copy-start = (bf16[1792,128]{1,0:T(8,128)(2,1)S(1)}, bf16[1792,128]{1,0:T(8,128)(2,1)}, u32[]{:S(2)}) copy-start(bf16[1792,128]{1,0:T(8,128)(2,1)} %refs_2_.1) | copy-start | bytes 1376260
  13.3 20.3 %copy-start.1 = (bf16[128,1792]{1,0:T(8,128)(2,1)S(1)}, bf16[128,1792]{1,0:T(8,128)(2,1)}, u32[]{:S(2)}) copy-start(bf16[128,1792]{1,0:T(8,128)(2,1)} %refs_0_.3) | copy-start | bytes 1376260
  13.3 9.8 %collective-permute-start.5 = (bf16[128,1792]{1,0:T(8,128)(2,1)S(1)}, bf16[128,1792]{1,0:T(8,128)(2,1)S(1)}, u32[]{:S(2)}, u32[]{:S(2)}) collective-permute-start(bf16[128,1792]{1,0:T(8,128)(2,1)S(1)} %gate.6.refs_2_), channel_id=1, source_target_pairs={{0,16},{8,120},{16,32},{24,8},{32,48},{40,24},{48,64},{56,40},{64,... | collective-permute-start | bytes 1376264 | tf_op jit(solution)/shard_map/ppermute | solution.py:292
  13.3 9.8 %collective-permute-start.6 = (bf16[128,1792]{1,0:T(8,128)(2,1)S(1)}, bf16[128,1792]{1,0:T(8,128)(2,1)S(1)}, u32[]{:S(2)}, u32[]{:S(2)}) collective-permute-start(bf16[128,1792]{1,0:T(8,128)(2,1)S(1)} %gate.6.refs_2_), channel_id=1, source_target_pairs={{0,8},{8,0},{16,24},{24,16},{32,40},{40,32},{48,56},{56,48},{64,72... | collective-permute-start | bytes 1376264 | tf_op jit(solution)/shard_map/ppermute | solution.py:295
  18.3 4.9 %collective-permute-start.7 = (bf16[128,1792]{1,0:T(8,128)(2,1)S(1)}, bf16[128,1792]{1,0:T(8,128)(2,1)S(1)}, u32[]{:S(2)}, u32[]{:S(2)}) collective-permute-start(bf16[128,1792]{1,0:T(8,128)(2,1)S(1)} %collective-permute-done.1.refs_3_), channel_id=1, source_target_pairs={{0,8},{8,0},{16,24},{24,16},{32,40},{40,32},{48,56},{56,48},{64,72... | collective-permute-start | bytes 1376264 | tf_op jit(solution)/shard_map/ppermute | solution.py:295
  18.3 13.1 %collective-permute-start.2 = (bf16[128,1792]{1,0:T(8,128)(2,1)S(1)}, bf16[128,1792]{1,0:T(8,128)(2,1)S(1)}, u32[]{:S(2)}, u32[]{:S(2)}) collective-permute-start(bf16[128,1792]{1,0:T(8,128)(2,1)S(1)} %collective-permute-done.1.refs_3_), channel_id=1, source_target_pairs={{0,16},{8,120},{16,32},{24,8},{32,48},{40,24},{48,64},{56,40},{64,... | collective-permute-start | bytes 1376264 | tf_op jit(solution)/shard_map/ppermute | solution.py:292
  23.2 10.5 %collective-permute-start.11 = (bf16[128,1792]{1,0:T(8,128)(2,1)S(1)}, bf16[128,1792]{1,0:T(8,128)(2,1)S(1)}, u32[]{:S(2)}, u32[]{:S(2)}) collective-permute-start(bf16[128,1792]{1,0:T(8,128)(2,1)S(1)} %gate.7.refs_6_), channel_id=1, source_target_pairs={{0,8},{8,0},{16,24},{24,16},{32,40},{40,32},{48,56},{56,48},{64,72... | collective-permute-start | bytes 1376264 | tf_op jit(solution)/shard_map/ppermute | solution.py:295
  26.4 10.4 %collective-permute-start.10 = (bf16[128,1792]{1,0:T(8,128)(2,1)S(1)}, bf16[128,1792]{1,0:T(8,128)(2,1)S(1)}, u32[]{:S(2)}, u32[]{:S(2)}) collective-permute-start(bf16[128,1792]{1,0:T(8,128)(2,1)S(1)} %gate.7.refs_6_), channel_id=1, source_target_pairs={{0,16},{8,120},{16,32},{24,8},{32,48},{40,24},{48,64},{56,40},{64,... | collective-permute-start | bytes 1376264 | tf_op jit(solution)/shard_map/ppermute | solution.py:292
  26.4 5.0 %collective-permute-start.3 = (bf16[512,128]{1,0:T(8,128)(2,1)S(1)}, bf16[512,128]{1,0:T(8,128)(2,1)S(1)}, u32[]{:S(2)}, u32[]{:S(2)}) collective-permute-start(bf16[512,128]{1,0:T(8,128)(2,1)S(1)} %copy-done.2), channel_id=1, source_target_pairs={{0,128},{8,136},{16,144},{24,152},{32,160},{40,168},{48,176},{56,1... | collective-permute-start | bytes 393224 | tf_op jit(solution)/shard_map/ppermute | solution.py:298
  31.4 21.7 %collective-permute-start.12 = (bf16[128,1792]{1,0:T(8,128)(2,1)S(1)}, bf16[128,1792]{1,0:T(8,128)(2,1)S(1)}, u32[]{:S(2)}, u32[]{:S(2)}) collective-permute-start(bf16[128,1792]{1,0:T(8,128)(2,1)S(1)} %gate.5.refs_0_), channel_id=1, source_target_pairs={{0,16},{8,120},{16,32},{24,8},{32,48},{40,24},{48,64},{56,40},{64,... | collective-permute-start | bytes 1376264 | tf_op jit(solution)/shard_map/ppermute | solution.py:292
  36.8 16.3 %collective-permute-start.16 = (bf16[128,1792]{1,0:T(8,128)(2,1)S(1)}, bf16[128,1792]{1,0:T(8,128)(2,1)S(1)}, u32[]{:S(2)}, u32[]{:S(2)}) collective-permute-start(bf16[128,1792]{1,0:T(8,128)(2,1)S(1)} %gate.8.refs_1_), channel_id=1, source_target_pairs={{0,16},{8,120},{16,32},{24,8},{32,48},{40,24},{48,64},{56,40},{64,... | collective-permute-start | bytes 1376264 | tf_op jit(solution)/shard_map/ppermute | solution.py:292
  37.1 8.9 %collective-permute-start.13 = (bf16[256,512]{1,0:T(8,128)(2,1)S(1)}, bf16[256,512]{1,0:T(8,128)(2,1)S(1)}, u32[]{:S(2)}, u32[]{:S(2)}) collective-permute-start(bf16[256,512]{1,0:T(8,128)(2,1)S(1)} %get-tuple-element.21), channel_id=1, source_target_pairs={{0,1},{1,2},{2,3},{3,0},{4,5},{5,6},{6,7},{7,4},{8,9},{9,10},{10,1... | collective-permute-start | bytes 786440 | tf_op jit(solution)/shard_map/ppermute | solution.py:301
  38.7 8.1 %collective-permute-start.14 = (bf16[256,512]{1,0:T(8,128)(2,1)S(1)}, bf16[256,512]{1,0:T(8,128)(2,1)S(1)}, u32[]{:S(2)}, u32[]{:S(2)}) collective-permute-start(bf16[256,512]{1,0:T(8,128)(2,1)S(1)} %get-tuple-element.22), channel_id=1, source_target_pairs={{0,3},{1,0},{2,1},{3,2},{4,7},{5,4},{6,5},{7,6},{8,11},{9,8},{10,9... | collective-permute-start | bytes 786440 | tf_op jit(solution)/shard_map/ppermute | solution.py:301
  40.4 12.6 %collective-permute-start.15 = (bf16[256,512]{1,0:T(8,128)(2,1)S(1)}, bf16[256,512]{1,0:T(8,128)(2,1)S(1)}, u32[]{:S(2)}, u32[]{:S(2)}) collective-permute-start(bf16[256,512]{1,0:T(8,128)(2,1)S(1)} %get-tuple-element.23), channel_id=1, source_target_pairs={{0,2},{1,3},{2,0},{3,1},{4,6},{5,7},{6,4},{7,5},{8,10},{9,11},{10,... | collective-permute-start | bytes 786440 | tf_op jit(solution)/shard_map/ppermute | solution.py:301
  53.3 8.3 %collective-permute-start.17 = (bf16[512,1792]{1,0:T(8,128)(2,1)S(1)}, bf16[512,1792]{1,0:T(8,128)(2,1)S(1)}, u32[]{:S(2)}, u32[]{:S(2)}) collective-permute-start(bf16[512,1792]{1,0:T(8,128)(2,1)S(1)} %stack.1.refs_0_), channel_id=1, source_target_pairs={{0,8},{8,0},{16,24},{24,16},{32,40},{40,32},{48,56},{56,48},{64,72... | collective-permute-start | bytes 5505032 | tf_op jit(solution)/shard_map/ppermute | solution.py:295
  54.6 7.0 %collective-permute-start.18 = (bf16[128,512]{1,0:T(8,128)(2,1)S(1)}, bf16[128,512]{1,0:T(8,128)(2,1)S(1)}, u32[]{:S(2)}, u32[]{:S(2)}) collective-permute-start(bf16[128,512]{1,0:T(8,128)(2,1)S(1)} %get-tuple-element.25), channel_id=1, source_target_pairs={{0,4},{1,5},{2,6},{3,7},{4,0},{5,1},{6,2},{7,3},{8,12},{9,13},{10,... | collective-permute-start | bytes 393224 | tf_op jit(solution)/shard_map/ppermute | solution.py:304
  64.0 10.3 %collective-permute-start.19 = (bf16[256,512]{1,0:T(8,128)(2,1)S(1)}, bf16[256,512]{1,0:T(8,128)(2,1)S(1)}, u32[]{:S(2)}, u32[]{:S(2)}) collective-permute-start(bf16[256,512]{1,0:T(8,128)(2,1)S(1)} %get-tuple-element.27), channel_id=1, source_target_pairs={{0,1},{1,2},{2,3},{3,0},{4,5},{5,6},{6,7},{7,4},{8,9},{9,10},{10,1... | collective-permute-start | bytes 786440 | tf_op jit(solution)/shard_map/ppermute | solution.py:301
  65.5 12.2 %collective-permute-start.20 = (bf16[256,512]{1,0:T(8,128)(2,1)S(1)}, bf16[256,512]{1,0:T(8,128)(2,1)S(1)}, u32[]{:S(2)}, u32[]{:S(2)}) collective-permute-start(bf16[256,512]{1,0:T(8,128)(2,1)S(1)} %get-tuple-element.28), channel_id=1, source_target_pairs={{0,3},{1,0},{2,1},{3,2},{4,7},{5,4},{6,5},{7,6},{8,11},{9,8},{10,9... | collective-permute-start | bytes 786440 | tf_op jit(solution)/shard_map/ppermute | solution.py:301
  67.3 11.3 %collective-permute-start.21 = (bf16[256,512]{1,0:T(8,128)(2,1)S(1)}, bf16[256,512]{1,0:T(8,128)(2,1)S(1)}, u32[]{:S(2)}, u32[]{:S(2)}) collective-permute-start(bf16[256,512]{1,0:T(8,128)(2,1)S(1)} %get-tuple-element.29), channel_id=1, source_target_pairs={{0,2},{1,3},{2,0},{3,1},{4,6},{5,7},{6,4},{7,5},{8,10},{9,11},{10,... | collective-permute-start | bytes 786440 | tf_op jit(solution)/shard_map/ppermute | solution.py:301
  67.7 11.0 %collective-permute-start.23 = (bf16[128,512]{1,0:T(8,128)(2,1)S(1)}, bf16[128,512]{1,0:T(8,128)(2,1)S(1)}, u32[]{:S(2)}, u32[]{:S(2)}) collective-permute-start(bf16[128,512]{1,0:T(8,128)(2,1)S(1)} %merge_x.2.refs_4_.mine), channel_id=1, source_target_pairs={{0,4},{1,5},{2,6},{3,7},{4,0},{5,1},{6,2},{7,3},{8,12},{9,13},{10,... | collective-permute-start | bytes 393224 | tf_op jit(solution)/shard_map/ppermute | solution.py:304
  78.8 12.2 %collective-permute-start.25 = (bf16[256,512]{1,0:T(8,128)(2,1)S(1)}, bf16[256,512]{1,0:T(8,128)(2,1)S(1)}, u32[]{:S(2)}, u32[]{:S(2)}) collective-permute-start(bf16[256,512]{1,0:T(8,128)(2,1)S(1)} %pair.2.refs_0_.refs_8_), channel_id=1, source_target_pairs={{0,1},{1,2},{2,3},{3,0},{4,5},{5,6},{6,7},{7,4},{8,9},{9,10},{10,1... | collective-permute-start | bytes 786440 | tf_op jit(solution)/shard_map/ppermute | solution.py:301
  80.0 11.5 %collective-permute-start.26 = (bf16[256,512]{1,0:T(8,128)(2,1)S(1)}, bf16[256,512]{1,0:T(8,128)(2,1)S(1)}, u32[]{:S(2)}, u32[]{:S(2)}) collective-permute-start(bf16[256,512]{1,0:T(8,128)(2,1)S(1)} %pair.2.refs_0_.refs_8_), channel_id=1, source_target_pairs={{0,3},{1,0},{2,1},{3,2},{4,7},{5,4},{6,5},{7,6},{8,11},{9,8},{10,9... | collective-permute-start | bytes 786440 | tf_op jit(solution)/shard_map/ppermute | solution.py:301
  82.1 6.5 %collective-permute-start.22 = (bf16[128,512]{1,0:T(8,128)(2,1)S(1)}, bf16[128,512]{1,0:T(8,128)(2,1)S(1)}, u32[]{:S(2)}, u32[]{:S(2)}) collective-permute-start(bf16[128,512]{1,0:T(8,128)(2,1)S(1)} %get-tuple-element.31), channel_id=1, source_target_pairs={{0,4},{1,5},{2,6},{3,7},{4,0},{5,1},{6,2},{7,3},{8,12},{9,13},{10,... | collective-permute-start | bytes 393224 | tf_op jit(solution)/shard_map/ppermute | solution.py:304
  84.2 8.8 %collective-permute-start.27 = (bf16[256,512]{1,0:T(8,128)(2,1)S(1)}, bf16[256,512]{1,0:T(8,128)(2,1)S(1)}, u32[]{:S(2)}, u32[]{:S(2)}) collective-permute-start(bf16[256,512]{1,0:T(8,128)(2,1)S(1)} %pair.2.refs_0_.refs_8_), channel_id=1, source_target_pairs={{0,2},{1,3},{2,0},{3,1},{4,6},{5,7},{6,4},{7,5},{8,10},{9,11},{10,... | collective-permute-start | bytes 786440 | tf_op jit(solution)/shard_map/ppermute | solution.py:301
  88.6 6.8 %collective-permute-start.24 = (bf16[128,512]{1,0:T(8,128)(2,1)S(1)}, bf16[128,512]{1,0:T(8,128)(2,1)S(1)}, u32[]{:S(2)}, u32[]{:S(2)}) collective-permute-start(bf16[128,512]{1,0:T(8,128)(2,1)S(1)} %merge_x.3.mine), channel_id=1, source_target_pairs={{0,4},{1,5},{2,6},{3,7},{4,0},{5,1},{6,2},{7,3},{8,12},{9,13},{10,... | collective-permute-start | bytes 393224 | tf_op jit(solution)/shard_map/ppermute | solution.py:304
  95.4 7.7 %collective-permute-start.31 = (bf16[256,256]{1,0:T(8,128)(2,1)S(1)}, bf16[256,256]{1,0:T(8,128)(2,1)S(1)}, u32[]{:S(2)}, u32[]{:S(2)}) collective-permute-start(bf16[256,256]{1,0:T(8,128)(2,1)S(1)} %get-tuple-element.33.refs_2_), channel_id=1, source_target_pairs={{0,1},{1,2},{2,3},{3,0},{4,5},{5,6},{6,7},{7,4},{8,9},{9,10},{10,1... | collective-permute-start | bytes 393224 | tf_op jit(solution)/shard_map/ppermute | solution.py:301
  96.2 6.9 %collective-permute-start.32 = (bf16[256,256]{1,0:T(8,128)(2,1)S(1)}, bf16[256,256]{1,0:T(8,128)(2,1)S(1)}, u32[]{:S(2)}, u32[]{:S(2)}) collective-permute-start(bf16[256,256]{1,0:T(8,128)(2,1)S(1)} %get-tuple-element.33.refs_2_), channel_id=1, source_target_pairs={{0,3},{1,0},{2,1},{3,2},{4,7},{5,4},{6,5},{7,6},{8,11},{9,8},{10,9... | collective-permute-start | bytes 393224 | tf_op jit(solution)/shard_map/ppermute | solution.py:301
  98.7 6.5 %collective-permute-start.33 = (bf16[256,256]{1,0:T(8,128)(2,1)S(1)}, bf16[256,256]{1,0:T(8,128)(2,1)S(1)}, u32[]{:S(2)}, u32[]{:S(2)}) collective-permute-start(bf16[256,256]{1,0:T(8,128)(2,1)S(1)} %get-tuple-element.33.refs_2_), channel_id=1, source_target_pairs={{0,2},{1,3},{2,0},{3,1},{4,6},{5,7},{6,4},{7,5},{8,10},{9,11},{10,... | collective-permute-start | bytes 393224 | tf_op jit(solution)/shard_map/ppermute | solution.py:301
  106.4 21.3 %collective-permute-start.34 = (bf16[1792,256]{1,0:T(8,128)(2,1)S(1)}, bf16[1792,256]{1,0:T(8,128)(2,1)S(1)}, u32[]{:S(2)}, u32[]{:S(2)}) collective-permute-start(bf16[1792,256]{1,0:T(8,128)(2,1)S(1)} %backward.5), channel_id=1, source_target_pairs={{0,128},{8,136},{16,144},{24,152},{32,160},{40,168},{48,176},{56,1... | collective-permute-start | bytes 2752520 | tf_op jit(solution)/shard_map/ppermute | solution.py:298
  107.4 19.1 %collective-permute-start.28 = (bf16[256,256]{1,0:T(8,128)(2,1)S(1)}, bf16[256,256]{1,0:T(8,128)(2,1)S(1)}, u32[]{:S(2)}, u32[]{:S(2)}) collective-permute-start(bf16[256,256]{1,0:T(8,128)(2,1)S(1)} %get-tuple-element.32.refs_2_), channel_id=1, source_target_pairs={{0,1},{1,2},{2,3},{3,0},{4,5},{5,6},{6,7},{7,4},{8,9},{9,10},{10,1... | collective-permute-start | bytes 393224 | tf_op jit(solution)/shard_map/ppermute | solution.py:301
  107.4 19.1 %collective-permute-start.29 = (bf16[256,256]{1,0:T(8,128)(2,1)S(1)}, bf16[256,256]{1,0:T(8,128)(2,1)S(1)}, u32[]{:S(2)}, u32[]{:S(2)}) collective-permute-start(bf16[256,256]{1,0:T(8,128)(2,1)S(1)} %get-tuple-element.32.refs_2_), channel_id=1, source_target_pairs={{0,3},{1,0},{2,1},{3,2},{4,7},{5,4},{6,5},{7,6},{8,11},{9,8},{10,9... | collective-permute-start | bytes 393224 | tf_op jit(solution)/shard_map/ppermute | solution.py:301
  110.6 15.8 %collective-permute-start.30 = (bf16[256,256]{1,0:T(8,128)(2,1)S(1)}, bf16[256,256]{1,0:T(8,128)(2,1)S(1)}, u32[]{:S(2)}, u32[]{:S(2)}) collective-permute-start(bf16[256,256]{1,0:T(8,128)(2,1)S(1)} %get-tuple-element.32.refs_2_), channel_id=1, source_target_pairs={{0,2},{1,3},{2,0},{3,1},{4,6},{5,7},{6,4},{7,5},{8,10},{9,11},{10,... | collective-permute-start | bytes 393224 | tf_op jit(solution)/shard_map/ppermute | solution.py:301
  110.6 15.8 %collective-permute-start.35 = (f32[1,1792]{1,0:T(1,128)S(1)}, f32[1,1792]{1,0:T(1,128)S(1)}, u32[]{:S(2)}, u32[]{:S(2)}) collective-permute-start(f32[1,1792]{1,0:T(1,128)S(1)} %get-tuple-element.34), channel_id=1, source_target_pairs={{0,128},{8,136},{16,144},{24,152},{32,160},{40,168},{48,176},{56,1... | collective-permute-start | bytes 21512 | tf_op jit(solution)/shard_map/ppermute | solution.py:298
  127.7 1.2 copy-start.3

commit v3 on v2

--- a/solution.py
+++ b/solution.py
@@ -94,10 +94,11 @@
 ROWS = 128
 
 
-def forward_kernel(units, places, scale, more, *refs):
+def forward_kernel(units, places, scale, more, sides, *refs):
     blocks = refs[: sum(units)]
     packs, residuals = refs[sum(units) :][:4], refs[sum(units) + 4 :][:2]
-    mine, ahead, sq_ref, wide, held = refs[-7], refs[-6:-3], refs[-3], refs[-2], refs[-1]
+    mine, ahead = refs[-4 - 3 * sides], refs[-3 - 3 * sides : -3]
+    sq_ref, wide, held = refs[-3:]
     x, z, c, x_hi, y = place()
     back = 2 * c - 1
     width, cols = blocks[0].shape[1], packs[0].shape[1]
@@ -131,11 +132,14 @@
     sq_ref[...] = total + refs[sum(units) + 6][...] if more else total
     quarter = held.shape[0] // 4
     mine[...] = held[rows_at(y, quarter), :]
-    for out, dy in zip(ahead, AHEAD):
-        out[...] = held[rows_at((y + dy) & 3, quarter), :].astype(bf16)
-
-
-def forward(units, places, packs, squares=(), after=()):
+    part = held.shape[1] // sides
+    for k, out in enumerate(ahead):
+        at = rows_at((y + AHEAD[k % 3]) & 3, quarter)
+        left = (k // 3) * part
+        out[...] = held[at, left : left + part].astype(bf16)
+
+
+def forward(units, places, packs, sides, squares=(), after=()):
     blocks = [block for unit in units for block in unit]
     rows = sum(block.shape[0] for block in blocks)
     width, cols = blocks[0].shape[1], packs[0].shape[1]
@@ -147,9 +151,10 @@
             places,
             1.0 / math.sqrt(FFW),
             len(squares),
+            sides,
         ),
         [jax.ShapeDtypeStruct(piece, f32)]
-        + [jax.ShapeDtypeStruct(piece, bf16)] * 3
+        + [jax.ShapeDtypeStruct((rows // 4, 4 * cols // sides), bf16)] * (3 * sides)
         + [jax.ShapeDtypeStruct((1, width), f32)],
         [pltpu.VMEM((width, 4 * cols), bf16), pltpu.VMEM((rows, 4 * cols), f32)],
         2 * rows * width * 4 * cols,
@@ -160,27 +165,24 @@
         *squares,
         *after,
     )
-    return out[0], out[1:4], out[4]
-
-
-def merge_y_kernel(*refs):
+    return out[0], out[1:-1], out[-1]
+
+
+def merge_y_kernel(left, *refs):
     pieces, (keep, send) = refs[:4], refs[-2:]
-    x_hi = place()[3]
-    count = keep.shape[0]
-    for out, half in ((send, 1 - x_hi), (keep, x_hi)):
-        for r in range(0, count, 32):
-            at = pl.ds(pl.multiple_of(half * count + r, 32), 32)
-            total = pieces[0][at, :]
-            for piece in pieces[1:]:
-                total = total + piece[at, :].astype(f32)
-            out[r : r + 32, :] = total.astype(out.dtype)
-
-
-def merge_y(mine, got, after=()):
-    rows, width = mine.shape
+    for r in range(0, keep.shape[0], 32):
+        at = pl.ds(r, 32)
+        total = pieces[0][at, left : left + keep.shape[1]]
+        for piece in pieces[1:]:
+            total = total + piece[at, :].astype(f32)
+        keep[at, :] = total
+        send[at, :] = total.astype(bf16)
+
+
+def merge_y(mine, got, left=0, after=()):
     return vmem_call(
-        merge_y_kernel,
-        [jax.ShapeDtypeStruct((rows // 2, width), t) for t in (f32, bf16)],
+        functools.partial(merge_y_kernel, left),
+        [jax.ShapeDtypeStruct(got[0].shape, t) for t in (f32, bf16)],
         [],
         4 * mine.size,
         len(after),
@@ -191,78 +193,69 @@
     )
 
 
-def merge_x_kernel(keep, got, *refs):
-    refs[-1][...] = (keep[...] + got[...].astype(f32)).astype(bf16)
-
-
-def merge_x(keep, got, after=()):
+def merge_x_kernel(parts, n_above, keep, got, *refs):
+    outs = refs[-parts:]
+    part = outs[0].shape[1]
+    start = 0
+    for above in refs[:n_above]:
+        outs[0][: above.shape[0], :] = above[...]
+        start = above.shape[0]
+    for k, out in enumerate(outs):
+        at = slice(k * part, (k + 1) * part)
+        out[start:, :] = (keep[:, at] + got[:, at].astype(f32)).astype(bf16)
+
+
+def merge_x(keep, got, parts, above=(), after=()):
+    rows, width = keep.shape
+    rows += sum(a.shape[0] for a in above)
     return vmem_call(
-        merge_x_kernel,
-        jax.ShapeDtypeStruct(keep.shape, bf16),
+        functools.partial(merge_x_kernel, parts, len(above)),
+        [jax.ShapeDtypeStruct((rows, width // parts), bf16)] * parts,
         [],
         keep.size,
         len(after),
         "merge_x",
         keep,
         got,
-        *after,
-    )
-
-
-def pair_kernel(n, mine, got, *refs):
-    outs = refs[-n:]
-    x_hi = place()[3]
-    count, part = mine.shape[0], outs[0].shape[1]
-    for piece, at in ((mine, x_hi), (got, 1 - x_hi)):
-        for k, out in enumerate(outs):
-            out[rows_at(at, count), :] = piece[:, k * part : (k + 1) * part]
-
-
-def pair(mine, got, parts, after=()):
-    count, width = mine.shape
-    return vmem_call(
-        functools.partial(pair_kernel, parts),
-        [jax.ShapeDtypeStruct((2 * count, width // parts), bf16)] * parts,
-        [],
-        2 * mine.size,
-        len(after),
-        "pair",
-        mine,
-        got,
-        *after,
-    )
-
-
-def backward_kernel(n, scale, left, *refs):
+        *above,
+        *after,
+    )
+
+
+def backward_kernel(n, scale, groups, more, *refs):
     blocks, targets, o_ref, held = refs[:n], refs[n : n + 4], refs[-2], refs[-1]
     y = place()[4]
-    width, cols = blocks[0].shape[1], held.shape[1]
+    width = blocks[0].shape[1]
     for ref, dy in zip(targets, (0,) + AHEAD):
-        held[rows_at((y - dy) & 3, ref.shape[0]), :] = ref[...]
+        count = ref.shape[0] // groups
+        for g in range(groups):
+            at = rows_at(4 * g + ((y - dy) & 3), count)
+            held[at, :] = ref[g * count : (g + 1) * count, :]
     for at in range(0, width, 256):
         tokens = jnp.concatenate([block[:, at : at + 256] for block in blocks], axis=0)
         value = lax.dot_general(
             tokens, held[...], (((0,), (0,)), ((), ())), preferred_element_type=f32
         )
         value = value * scale
-        if left is not None:
-            value = value + refs[n + 4][at : at + 256, left : left + cols]
+        if more:
+            value = value + refs[n + 4][at : at + 256, :]
         o_ref[at : at + 256, :] = value.astype(o_ref.dtype)
 
 
-def backward(blocks, targets, dtype, init=(), left=None):
+def backward(blocks, targets, dtype, groups=1, init=(), after=()):
     n, width, cols = len(blocks), blocks[0].shape[1], targets[0].shape[1]
     rows = sum(block.shape[0] for block in blocks)
     return vmem_call(
-        functools.partial(backward_kernel, n, 1.0 / math.sqrt(TOKENS), left),
+        functools.partial(backward_kernel, n, 1.0 / math.sqrt(TOKENS), groups, len(init)),
         jax.ShapeDtypeStruct((width, cols), dtype),
         [pltpu.VMEM((rows, cols), bf16)],
         2 * rows * width * cols,
-        0,
+        len(after),
         "backward",
         *blocks,
         *targets,
         *init,
+        *after,
     )
 
 
@@ -298,7 +291,8 @@
         return lax.ppermute(value, "dp", PAIR_X)
 
     def around(pieces):
-        return [lax.ppermute(v, "mp", y_perm(dy)) for v, dy in zip(pieces, AHEAD)]
+        ahead = AHEAD * (len(pieces) // 3)
+        return [lax.ppermute(v, "mp", y_perm(dy)) for v, dy in zip(pieces, ahead)]
 
     def over(value):
         return lax.ppermute(value, "mp", PAIR_X_HI)
@@ -313,18 +307,18 @@
     a1 = gate(a1, pruned)
     a2 = ring(a1)
     sa1 = swap(a1)
+    b1 = gate(b1, weight_x)
     b2 = ring(b1)
     sb1 = swap(b1)
-    a2 = gate(a2, sa1, sb1, weight_x, pruned_x)
+    a2 = gate(a2, sa1, sb1, pruned_x)
     a3 = ring(a2)
     sa2 = swap(a2)
-    b2 = gate(b2, residual_x)
     b3 = ring(b2)
 
     packs = (down_weight, pruned, weight_x, pruned_x, residual, residual_x)
     early = [[hidden, sib], [a1, b1], [sa1, sb1], [a2, sa2]]
     places = [(0, 1), (0, 0), (1, 1), (1, 0), (-1, 0), (-1, 1), (2, 1), (-2, 0)]
-    mine0, ahead0, squares0 = forward(early, places, packs)
+    mine0, ahead0, squares0 = forward(early, places, packs, 1)
     got0 = around(ahead0)
     a3 = gate(a3, squares0)
     a4 = ring(a3)
@@ -332,24 +326,25 @@
     b3 = gate(b3, keep0)
     s4 = stack([b2, a3, b3, a4])
     t4 = swap(s4)
-    sent0 = over(send0)
     late = [s4, t4]
     places = [(2, 0), (3, 1), (3, 0), (4, 1), (-2, 1), (-3, 0), (-3, 1), (4, 0)]
-    mine1, ahead1, squares = forward([[s4], [t4]], places, packs, [squares0], [sent0])
-    got1 = around(ahead1)
+    mine1, ahead1, squares = forward([[s4], [t4]], places, packs, 2, [squares0], [keep0])
     squares_x = across(squares)
 
     early = [block for unit in early for block in unit]
-    sum0 = merge_x(keep0, sent0)
-    keep1, send1 = merge_y(mine1, got1, [sum0])
-    (both0,) = pair(sum0, over(sum0), 1, [keep1])
-    sum1 = merge_x(keep1, over(send1), [both0])
-    init = backward(early, [both0] + around([both0] * 3), f32)
-    own1, other1 = pair(sum1, over(sum1), 2, [init])
-    other1 = [other1] + around([other1] * 3)
-    own1 = [own1] + around([own1] * 3)
-    arrived = across(backward(late, other1, bf16, [init], 2 * cols))
-    grads = backward(late, own1, f32, [init], 0)
+    sent0 = over(send0)
+    own0, other0 = merge_x(keep0, sent0, 2, (), [squares])
+    keep1, send1 = merge_y(mine1, around(ahead1[3:]), 2 * cols, [other0])
+    back0 = around([other0] * 3)
+    (other1,) = merge_x(keep1, over(send1), 1, (), back0[:1])
+    init = backward(early, [other0] + back0, f32)
+    back1 = around([other1] * 3)
+    got2 = around([gate(v, keep1) for v in ahead1[:3]])
+    keep2, send2 = merge_y(mine1, got2, 0, [squares_x])
+    sent2 = over(send2)
+    arrived = across(backward(late, [other1] + back1, bf16, 1, [init], [sent2]))
+    (own,) = merge_x(keep2, sent2, 1, [own0])
+    grads = backward(early + late, [own] + around([own] * 3), f32, 2)
     colsq = squares + squares_x
     grads = grads + arrived.astype(f32)
 

time: 133 us -> 117 us (0.88); the launches traced: 131 us -> 116 us
  waiting for transfers between devices: 67.4 us -> 53.6 us
    ppermute x5, waiting for transfers between devices: 22.7 us -> 9.11 us  [across(): return lax.ppermute(value, 'dp', PAIR_X)]
    ppermute x15 -> x18, starting transfers between devices: 20 us -> 26.1 us  [around(): return [lax.ppermute(v, 'mp', y_perm(dy)) for v, dy in zip(pieces, ahead)]]
    ppermute x7, waiting for transfers between devices: 8.68 us -> 14.4 us  [ring(): return lax.ppermute(value, 'dp', RING)]
    ppermute x4 -> x3, waiting for transfers between devices: 8.45 us -> 3.57 us  [over(): return lax.ppermute(value, 'mp', PAIR_X_HI)]
    ppermute x4 -> x3, starting transfers between devices: 8.86 us -> 5.82 us  [over(): return lax.ppermute(value, 'mp', PAIR_X_HI)]
    ppermute x7, starting transfers between devices: 6.55 us -> 4.01 us  [ring(): return lax.ppermute(value, 'dp', RING)]
    ppermute x15 -> x18, waiting for transfers between devices: 27.6 us -> 25.2 us  [around(): return [lax.ppermute(v, 'mp', y_perm(dy)) for v, dy in zip(pieces, ahead)]]
  transfers between devices with their start and end apart: 36 -> 38, of which waited for: 20 -> 22; matrix products, arithmetic and copies ran while one was open for 1% -> 1% of each run, Pallas kernels for 5% -> 7%
where the time goes in v3:
time: 117 us; the launch traced here: 116 us
  waiting for transfers between devices  53.6 us (46%)
  starting transfers between devices  48 us (41%)
  Pallas kernels  9.9 us (8%)
  other arithmetic  4.06 us (3%)
    ppermute x18, starting transfers between devices, around(): return [lax.ppermute(v, 'mp', y_perm(dy)) for v, dy in zip(pieces, ahead)]  26.1 us
    ppermute x18, waiting for transfers between devices, around(): return [lax.ppermute(v, 'mp', y_perm(dy)) for v, dy in zip(pieces, ahead)]  25.2 us
    ppermute x7, waiting for transfers between devices, ring(): return lax.ppermute(value, 'dp', RING)  14.4 us
    pallas_call x12, Pallas kernels, vmem_call(): pl.pallas_call(kernel, out_shape=out_shape, in_specs=specs, out_specs=jax...  9.9 us
    ppermute x5, waiting for transfers between devices, across(): return lax.ppermute(value, 'dp', PAIR_X)  9.11 us
    ppermute x5, starting transfers between devices, swap(): return lax.ppermute(value, 'dp', PAIR_CORE)  6.05 us
    ppermute x5, starting transfers between devices, across(): return lax.ppermute(value, 'dp', PAIR_X)  6.05 us
    ppermute x3, starting transfers between devices, over(): return lax.ppermute(value, 'mp', PAIR_X_HI)  5.82 us
  transfers between devices with their start and end apart: 38, of which 22 were waited for; matrix products, arithmetic and copies ran while one was open for 1% of the time, Pallas kernels for 7%

profile of v3, /device:TPU:2, one launch (start us, length us, event | category | flops | bytes accessed | tf_op | source)
XLA Modules:
  0.0 116.5 jit_solution(14745148948347810279)
XLA Ops:
  0.7 2.0 %collective-permute-start.1 = (bf16[128,1792]{1,0:T(8,128)(2,1)}, bf16[128,1792]{1,0:T(8,128)(2,1)S(1)}, u32[]{:S(2)}, u32[]{:S(2)}) collective-permute-start(bf16[128,1792]{1,0:T(8,128)(2,1)} %refs_0_.5), channel_id=1, source_target_pairs={{0,16},{8,120},{16,32},{24,8},{32,48},{40,24},{48,64},{56,40},{64,... | collective-permute-start | bytes 1376264 | tf_op jit(solution)/shard_map/ppermute | solution.py:285
  3.3 1.9 %collective-permute-start.2 = (bf16[128,1792]{1,0:T(8,128)(2,1)S(1)}, bf16[128,1792]{1,0:T(8,128)(2,1)S(1)}, u32[]{:S(2)}, u32[]{:S(2)}) collective-permute-start(bf16[128,1792]{1,0:T(8,128)(2,1)S(1)} %collective-permute-done.refs_1_), channel_id=1, source_target_pairs={{0,16},{8,120},{16,32},{24,8},{32,48},{40,24},{48,64},{56,40},{64,... | collective-permute-start | bytes 1376264 | tf_op jit(solution)/shard_map/ppermute | solution.py:285
  5.2 1.5 %negate_select_fusion = (bf16[1792,128]{1,0:T(8,128)(2,1)S(1)}, pred[1792,128]{1,0:T(8,128)(4,1)S(1)}) fusion(bf16[1792,128]{1,0:T(8,128)(2,1)} %refs_2_.1, s32[1792,128]{1,0:T(8,128)} %param.8), kind=kLoop, calls=%fused_computation.12 | loop fusion | flops 688128 | bytes 2064384 | tf_op jit(solution)/shard_map/jit(_where)/select_n | solution.py:304
  6.7 1.6 %collective-permute-start.7 = (bf16[1792,128]{1,0:T(8,128)(2,1)S(1)}, bf16[1792,128]{1,0:T(8,128)(2,1)S(1)}, u32[]{:S(2)}, u32[]{:S(2)}) collective-permute-start(bf16[1792,128]{1,0:T(8,128)(2,1)S(1)} %get-tuple-element.47.refs_1_.refs_9_.refs_3_), channel_id=1, source_target_pairs={{0,128},{8,136},{16,144},{24,152},{32,160},{40,168},{48,176},{56,1... | collective-permute-start | bytes 1376264 | tf_op jit(solution)/shard_map/ppermute | solution.py:291
  8.3 5.0 %collective-permute-done.1.refs_0_ = bf16[128,1792]{1,0:T(8,128)(2,1)S(1)} collective-permute-done((bf16[128,1792]{1,0:T(8,128)(2,1)}, bf16[128,1792]{1,0:T(8,128)(2,1)S(1)}, u32[]{:S(2)}, u32[]{:S(2)}) %collective-permute-start.1) | collective-permute-done | bytes 458784 | tf_op jit(solution)/shard_map/ppermute | solution.py:285
  13.5 4.7 %collective-permute-done.2.refs_0_ = bf16[128,1792]{1,0:T(8,128)(2,1)S(1)} collective-permute-done((bf16[128,1792]{1,0:T(8,128)(2,1)S(1)}, bf16[128,1792]{1,0:T(8,128)(2,1)S(1)}, u32[]{:S(2)}, u32[]{:S(2)}) %collective-permute-start.2) | collective-permute-done | bytes 458784 | tf_op jit(solution)/shard_map/ppermute | solution.py:285
  18.3 1.4 %collective-permute-start.5 = (bf16[128,1792]{1,0:T(8,128)(2,1)S(1)}, bf16[128,1792]{1,0:T(8,128)(2,1)S(1)}, u32[]{:S(2)}, u32[]{:S(2)}) collective-permute-start(bf16[128,1792]{1,0:T(8,128)(2,1)S(1)} %gate.9.refs_3_), channel_id=1, source_target_pairs={{0,8},{8,0},{16,24},{24,16},{32,40},{40,32},{48,56},{56,48},{64,72... | collective-permute-start | bytes 1376264 | tf_op jit(solution)/shard_map/ppermute | solution.py:288
  19.6 3.4 %collective-permute-done.7.refs_3_.refs_11_.refs_5_ = bf16[1792,128]{1,0:T(8,128)(2,1)S(1)} collective-permute-done((bf16[1792,128]{1,0:T(8,128)(2,1)S(1)}, bf16[1792,128]{1,0:T(8,128)(2,1)S(1)}, u32[]{:S(2)}, u32[]{:S(2)}) %collective-permute-start.7) | collective-permute-done | bytes 458784 | tf_op jit(solution)/shard_map/ppermute | solution.py:291
  23.2 3.2 %collective-permute-start.8 = (bf16[128,1792]{1,0:T(8,128)(2,1)S(1)}, bf16[128,1792]{1,0:T(8,128)(2,1)S(1)}, u32[]{:S(2)}, u32[]{:S(2)}) collective-permute-start(bf16[128,1792]{1,0:T(8,128)(2,1)S(1)} %gate.10.refs_6_), channel_id=1, source_target_pairs={{0,8},{8,0},{16,24},{24,16},{32,40},{40,32},{48,56},{56,48},{64,72... | collective-permute-start | bytes 1376264 | tf_op jit(solution)/shard_map/ppermute | solution.py:288
  26.4 1.5 %collective-permute-start.11 = (bf16[512,128]{1,0:T(8,128)(2,1)S(1)}, bf16[512,128]{1,0:T(8,128)(2,1)S(1)}, u32[]{:S(2)}, u32[]{:S(2)}) collective-permute-start(bf16[512,128]{1,0:T(8,128)(2,1)S(1)} %copy-done.2), channel_id=1, source_target_pairs={{0,128},{8,136},{16,144},{24,152},{32,160},{40,168},{48,176},{56,1... | collective-permute-start | bytes 393224 | tf_op jit(solution)/shard_map/ppermute | solution.py:291
  27.9 1.4 %collective-permute-done.9.refs_0_ = bf16[128,1792]{1,0:T(8,128)(2,1)S(1)} collective-permute-done((bf16[128,1792]{1,0:T(8,128)(2,1)S(1)}, bf16[128,1792]{1,0:T(8,128)(2,1)S(1)}, u32[]{:S(2)}, u32[]{:S(2)}) %collective-permute-start.9) | collective-permute-done | bytes 458784 | tf_op jit(solution)/shard_map/ppermute | solution.py:285
  29.3 2.0 %collective-permute-done.11.refs_13_.refs_7_ = bf16[512,128]{1,0:T(8,128)(2,1)S(1)} collective-permute-done((bf16[512,128]{1,0:T(8,128)(2,1)S(1)}, bf16[512,128]{1,0:T(8,128)(2,1)S(1)}, u32[]{:S(2)}, u32[]{:S(2)}) %collective-permute-start.11) | collective-permute-done | bytes 131104 | tf_op jit(solution)/shard_map/ppermute | solution.py:291
  31.4 2.4 %forward.2 = (f32[256,512]{1,0:T(8,128)S(1)}, bf16[256,512]{1,0:T(8,128)(2,1)S(1)}, bf16[256,512]{1,0:T(8,128)(2,1)S(1)}, bf16[256,512]{1,0:T(8,128)(2,1)S(1)}, f32[1,1792]{1,0:T(1,128)S(1)}) custom-call(bf16[128,1792]{1,0:T(8,128)(2,1)S(1)} %copy-done.1, bf16[128,1792]{1,0:T(8,128)(2,1)S(1)} %collective-permute-done.refs_1_, ...), custom_call_target="tpu_custom_call" | custom-call | tf_op jit(solution)/shard_map/forward/pallas_call | solution.py:62
  33.8 3.0 %collective-permute-done.10.refs_0_ = bf16[128,1792]{1,0:T(8,128)(2,1)S(1)} collective-permute-done((bf16[128,1792]{1,0:T(8,128)(2,1)S(1)}, bf16[128,1792]{1,0:T(8,128)(2,1)S(1)}, u32[]{:S(2)}, u32[]{:S(2)}) %collective-permute-start.10) | collective-permute-done | bytes 458784 | tf_op jit(solution)/shard_map/ppermute | solution.py:285
  36.8 1.6 %collective-permute-start.13 = (bf16[256,512]{1,0:T(8,128)(2,1)S(1)}, bf16[256,512]{1,0:T(8,128)(2,1)S(1)}, u32[]{:S(2)}, u32[]{:S(2)}) collective-permute-start(bf16[256,512]{1,0:T(8,128)(2,1)S(1)} %get-tuple-element.26), channel_id=1, source_target_pairs={{0,1},{1,2},{2,3},{3,0},{4,5},{5,6},{6,7},{7,4},{8,9},{9,10},{10,1... | collective-permute-start | bytes 786440 | tf_op jit(solution)/shard_map/ppermute | solution.py:295
  38.4 1.7 %collective-permute-start.14 = (bf16[256,512]{1,0:T(8,128)(2,1)S(1)}, bf16[256,512]{1,0:T(8,128)(2,1)S(1)}, u32[]{:S(2)}, u32[]{:S(2)}) collective-permute-start(bf16[256,512]{1,0:T(8,128)(2,1)S(1)} %get-tuple-element.27), channel_id=1, source_target_pairs={{0,3},{1,0},{2,1},{3,2},{4,7},{5,4},{6,5},{7,6},{8,11},{9,8},{10,9... | collective-permute-start | bytes 786440 | tf_op jit(solution)/shard_map/ppermute | solution.py:295
  40.0 2.0 %collective-permute-start.15 = (bf16[256,512]{1,0:T(8,128)(2,1)S(1)}, bf16[256,512]{1,0:T(8,128)(2,1)S(1)}, u32[]{:S(2)}, u32[]{:S(2)}) collective-permute-start(bf16[256,512]{1,0:T(8,128)(2,1)S(1)} %get-tuple-element.28), channel_id=1, source_target_pairs={{0,2},{1,3},{2,0},{3,1},{4,6},{5,7},{6,4},{7,5},{8,10},{9,11},{10,... | collective-permute-start | bytes 786440 | tf_op jit(solution)/shard_map/ppermute | solution.py:295
  42.0 3.7 %collective-permute-done.13.refs_1_ = bf16[256,512]{1,0:T(8,128)(2,1)S(1)} collective-permute-done((bf16[256,512]{1,0:T(8,128)(2,1)S(1)}, bf16[256,512]{1,0:T(8,128)(2,1)S(1)}, u32[]{:S(2)}, u32[]{:S(2)}) %collective-permute-start.13) | collective-permute-done | bytes 262176 | tf_op jit(solution)/shard_map/ppermute | solution.py:295
  46.5 6.2 %collective-permute-done.15.refs_3_ = bf16[256,512]{1,0:T(8,128)(2,1)S(1)} collective-permute-done((bf16[256,512]{1,0:T(8,128)(2,1)S(1)}, bf16[256,512]{1,0:T(8,128)(2,1)S(1)}, u32[]{:S(2)}, u32[]{:S(2)}) %collective-permute-start.15) | collective-permute-done | bytes 262176 | tf_op jit(solution)/shard_map/ppermute | solution.py:295
  52.9 1.3 %collective-permute-start.17 = (bf16[512,1792]{1,0:T(8,128)(2,1)S(1)}, bf16[512,1792]{1,0:T(8,128)(2,1)S(1)}, u32[]{:S(2)}, u32[]{:S(2)}) collective-permute-start(bf16[512,1792]{1,0:T(8,128)(2,1)S(1)} %stack.1.refs_0_.refs_8_), channel_id=1, source_target_pairs={{0,8},{8,0},{16,24},{24,16},{32,40},{40,32},{48,56},{56,48},{64,72... | collective-permute-start | bytes 5505032 | tf_op jit(solution)/shard_map/ppermute | solution.py:288
  54.2 2.1 %collective-permute-start.21 = (bf16[256,512]{1,0:T(8,128)(2,1)S(1)}, bf16[256,512]{1,0:T(8,128)(2,1)S(1)}, u32[]{:S(2)}, u32[]{:S(2)}) collective-permute-start(bf16[256,512]{1,0:T(8,128)(2,1)S(1)} %get-tuple-element.35), channel_id=1, source_target_pairs={{0,4},{1,5},{2,6},{3,7},{4,0},{5,1},{6,2},{7,3},{8,12},{9,13},{10,... | collective-permute-start | bytes 786440 | tf_op jit(solution)/shard_map/ppermute | solution.py:298
  56.4 1.3 %collective-permute-done.17.refs_1_.refs_9_ = bf16[512,1792]{1,0:T(8,128)(2,1)S(1)} collective-permute-done((bf16[512,1792]{1,0:T(8,128)(2,1)S(1)}, bf16[512,1792]{1,0:T(8,128)(2,1)S(1)}, u32[]{:S(2)}, u32[]{:S(2)}) %collective-permute-start.17) | collective-permute-done | bytes 1835040 | tf_op jit(solution)/shard_map/ppermute | solution.py:288
  57.7 2.4 %forward.3 = (f32[256,512]{1,0:T(8,128)S(1)}, bf16[256,256]{1,0:T(8,128)(2,1)S(1)}, bf16[256,256]{1,0:T(8,128)(2,1)S(1)}, bf16[256,256]{1,0:T(8,128)(2,1)S(1)}, ...) custom-call(bf16[512,1792]{1,0:T(8,128)(2,1)S(1)} %stack.1.refs_0_.r, ...), custom_call_target="tpu_custom_call" | custom-call | tf_op jit(solution)/shard_map/forward/pallas_call | solution.py:62
  60.1 1.5 %collective-permute-start.18 = (bf16[256,256]{1,0:T(8,128)(2,1)S(1)}, bf16[256,256]{1,0:T(8,128)(2,1)S(1)}, u32[]{:S(2)}, u32[]{:S(2)}) collective-permute-start(bf16[256,256]{1,0:T(8,128)(2,1)S(1)} %get-tuple-element.32), channel_id=1, source_target_pairs={{0,1},{1,2},{2,3},{3,0},{4,5},{5,6},{6,7},{7,4},{8,9},{9,10},{10,1... | collective-permute-start | bytes 393224 | tf_op jit(solution)/shard_map/ppermute | solution.py:295
  61.6 1.8 %collective-permute-start.19 = (bf16[256,256]{1,0:T(8,128)(2,1)S(1)}, bf16[256,256]{1,0:T(8,128)(2,1)S(1)}, u32[]{:S(2)}, u32[]{:S(2)}) collective-permute-start(bf16[256,256]{1,0:T(8,128)(2,1)S(1)} %get-tuple-element.33), channel_id=1, source_target_pairs={{0,3},{1,0},{2,1},{3,2},{4,7},{5,4},{6,5},{7,6},{8,11},{9,8},{10,9... | collective-permute-start | bytes 393224 | tf_op jit(solution)/shard_map/ppermute | solution.py:295
  64.1 1.5 %collective-permute-start.31 = (bf16[256,256]{1,0:T(8,128)(2,1)S(1)}, bf16[256,256]{1,0:T(8,128)(2,1)S(1)}, u32[]{:S(2)}, u32[]{:S(2)}) collective-permute-start(bf16[256,256]{1,0:T(8,128)(2,1)S(1)} %get-tuple-element.37.refs_4_.refs_8_), channel_id=1, source_target_pairs={{0,1},{1,2},{2,3},{3,0},{4,5},{5,6},{6,7},{7,4},{8,9},{9,10},{10,1... | collective-permute-start | bytes 393224 | tf_op jit(solution)/shard_map/ppermute | solution.py:295
  65.6 1.5 %collective-permute-done.18.refs_1_ = bf16[256,256]{1,0:T(8,128)(2,1)S(1)} collective-permute-done((bf16[256,256]{1,0:T(8,128)(2,1)S(1)}, bf16[256,256]{1,0:T(8,128)(2,1)S(1)}, u32[]{:S(2)}, u32[]{:S(2)}) %collective-permute-start.18) | collective-permute-done | bytes 131104 | tf_op jit(solution)/shard_map/ppermute | solution.py:295
  67.1 2.1 %collective-permute-done.19.refs_2_ = bf16[256,256]{1,0:T(8,128)(2,1)S(1)} collective-permute-done((bf16[256,256]{1,0:T(8,128)(2,1)S(1)}, bf16[256,256]{1,0:T(8,128)(2,1)S(1)}, u32[]{:S(2)}, u32[]{:S(2)}) %collective-permute-start.19) | collective-permute-done | bytes 131104 | tf_op jit(solution)/shard_map/ppermute | solution.py:295
  69.3 2.1 %collective-permute-done.20.refs_3_ = bf16[256,256]{1,0:T(8,128)(2,1)S(1)} collective-permute-done((bf16[256,256]{1,0:T(8,128)(2,1)S(1)}, bf16[256,256]{1,0:T(8,128)(2,1)S(1)}, u32[]{:S(2)}, u32[]{:S(2)}) %collective-permute-start.20) | collective-permute-done | bytes 131104 | tf_op jit(solution)/shard_map/ppermute | solution.py:295
  71.4 2.2 %collective-permute-start.30 = (bf16[256,256]{1,0:T(8,128)(2,1)S(1)}, bf16[256,256]{1,0:T(8,128)(2,1)S(1)}, u32[]{:S(2)}, u32[]{:S(2)}) collective-permute-start(bf16[256,256]{1,0:T(8,128)(2,1)S(1)} %get-tuple-element.44), channel_id=1, source_target_pairs={{0,4},{1,5},{2,6},{3,7},{4,0},{5,1},{6,2},{7,3},{8,12},{9,13},{10,... | collective-permute-start | bytes 393224 | tf_op jit(solution)/shard_map/ppermute | solution.py:298
  74.5 1.7 %collective-permute-start.23 = (bf16[256,256]{1,0:T(8,128)(2,1)S(1)}, bf16[256,256]{1,0:T(8,128)(2,1)S(1)}, u32[]{:S(2)}, u32[]{:S(2)}) collective-permute-start(bf16[256,256]{1,0:T(8,128)(2,1)S(1)} %gate.14), channel_id=1, source_target_pairs={{0,3},{1,0},{2,1},{3,2},{4,7},{5,4},{6,5},{7,6},{8,11},{9,8},{10,9... | collective-permute-start | bytes 393224 | tf_op jit(solution)/shard_map/ppermute | solution.py:295
  76.6 2.9 %collective-permute-start.35 = (bf16[256,256]{1,0:T(8,128)(2,1)S(1)}, bf16[256,256]{1,0:T(8,128)(2,1)S(1)}, u32[]{:S(2)}, u32[]{:S(2)}) collective-permute-start(bf16[256,256]{1,0:T(8,128)(2,1)S(1)} %get-tuple-element.37.refs_4_.refs_8_), channel_id=1, source_target_pairs={{0,3},{1,0},{2,1},{3,2},{4,7},{5,4},{6,5},{7,6},{8,11},{9,8},{10,9... | collective-permute-start | bytes 393224 | tf_op jit(solution)/shard_map/ppermute | solution.py:295
  79.5 1.4 %collective-permute-start.25 = (f32[1,1792]{1,0:T(1,128)S(1)}, f32[1,1792]{1,0:T(1,128)S(1)}, u32[]{:S(2)}, u32[]{:S(2)}) collective-permute-start(f32[1,1792]{1,0:T(1,128)S(1)} %get-tuple-element.36.refs_0_), channel_id=1, source_target_pairs={{0,128},{8,136},{16,144},{24,152},{32,160},{40,168},{48,176},{56,1... | collective-permute-start | bytes 21512 | tf_op jit(solution)/shard_map/ppermute | solution.py:291
  81.0 2.2 %collective-permute-done.25.refs_4_ = f32[1,1792]{1,0:T(1,128)S(1)} collective-permute-done((f32[1,1792]{1,0:T(1,128)S(1)}, f32[1,1792]{1,0:T(1,128)S(1)}, u32[]{:S(2)}, u32[]{:S(2)}) %collective-permute-start.25) | collective-permute-done | bytes 7200 | tf_op jit(solution)/shard_map/ppermute | solution.py:291
  84.2 2.8 %collective-permute-start.33 = (bf16[256,256]{1,0:T(8,128)(2,1)S(1)}, bf16[256,256]{1,0:T(8,128)(2,1)S(1)}, u32[]{:S(2)}, u32[]{:S(2)}) collective-permute-start(bf16[256,256]{1,0:T(8,128)(2,1)S(1)} %merge_x.5.refs_2_), channel_id=1, source_target_pairs={{0,3},{1,0},{2,1},{3,2},{4,7},{5,4},{6,5},{7,6},{8,11},{9,8},{10,9... | collective-permute-start | bytes 393224 | tf_op jit(solution)/shard_map/ppermute | solution.py:295
  87.0 1.7 %collective-permute-start.34 = (bf16[256,256]{1,0:T(8,128)(2,1)S(1)}, bf16[256,256]{1,0:T(8,128)(2,1)S(1)}, u32[]{:S(2)}, u32[]{:S(2)}) collective-permute-start(bf16[256,256]{1,0:T(8,128)(2,1)S(1)} %merge_x.5.refs_2_), channel_id=1, source_target_pairs={{0,2},{1,3},{2,0},{3,1},{4,6},{5,7},{6,4},{7,5},{8,10},{9,11},{10,... | collective-permute-start | bytes 393224 | tf_op jit(solution)/shard_map/ppermute | solution.py:295
  88.8 1.5 %collective-permute-start.26 = (bf16[256,256]{1,0:T(8,128)(2,1)S(1)}, bf16[256,256]{1,0:T(8,128)(2,1)S(1)}, u32[]{:S(2)}, u32[]{:S(2)}) collective-permute-start(bf16[256,256]{1,0:T(8,128)(2,1)S(1)} %get-tuple-element.42), channel_id=1, source_target_pairs={{0,4},{1,5},{2,6},{3,7},{4,0},{5,1},{6,2},{7,3},{8,12},{9,13},{10,... | collective-permute-start | bytes 393224 | tf_op jit(solution)/shard_map/ppermute | solution.py:298
  90.3 1.2 %backward.4.refs_6_ = f32[1792,256]{1,0:T(8,128)S(1)} custom-call(bf16[128,1792]{1,0:T(8,128)(2,1)S(1)} %copy-done.1, bf16[128,1792]{1,0:T(8,128)(2,1)S(1)} %collective-permute-done.refs_1_, bf16[128,1792]{1,0:T(8,128)(2,1)S(1)} %gate.8.refs_2_, bf16[128,1792]{1,0:T(8,128)(2,1)S(1)} %gate.9.refs_3_, ...), custom_call_target="tpu_custom_call" | custom-call | tf_op jit(solution)/shard_map/backward/pallas_call | solution.py:62
  91.6 2.0 %collective-permute-done.34.refs_5_ = bf16[256,256]{1,0:T(8,128)(2,1)S(1)} collective-permute-done((bf16[256,256]{1,0:T(8,128)(2,1)S(1)}, bf16[256,256]{1,0:T(8,128)(2,1)S(1)}, u32[]{:S(2)}, u32[]{:S(2)}) %collective-permute-start.34) | collective-permute-done | bytes 131104 | tf_op jit(solution)/shard_map/ppermute | solution.py:295
  93.5 3.3 %collective-permute-done.26.got.refs_7_ = bf16[256,256]{1,0:T(8,128)(2,1)S(1)} collective-permute-done((bf16[256,256]{1,0:T(8,128)(2,1)S(1)}, bf16[256,256]{1,0:T(8,128)(2,1)S(1)}, u32[]{:S(2)}, u32[]{:S(2)}) %collective-permute-start.26) | collective-permute-done | bytes 131104 | tf_op jit(solution)/shard_map/ppermute | solution.py:298
  96.8 1.2 %backward.5 = bf16[1792,256]{1,0:T(8,128)(2,1)S(1)} custom-call(bf16[512,1792]{1,0:T(8,128)(2,1)S(1)} %stack.1.refs_0_.refs_8_, bf16[512,1792]{1,0:T(8,128)(2,1)S(1)} %collective-permute-done.17.refs_1_.refs_9_, bf16[256,256]{1,0:T(8,128)(2,1)S(1)} %merge_x.5.refs_2_, bf16[256,256]{1,0:T(8,128)(2,1)S(1)} %collective-permute-done.32.refs_3_, ...), custom_call_target="tpu_custom_call" | custom-call | tf_op jit(solution)/shard_map/backward/pallas_call | solution.py:62
  99.1 3.2 %collective-permute-start.28 = (bf16[512,256]{1,0:T(8,128)(2,1)S(1)}, bf16[512,256]{1,0:T(8,128)(2,1)S(1)}, u32[]{:S(2)}, u32[]{:S(2)}) collective-permute-start(bf16[512,256]{1,0:T(8,128)(2,1)S(1)} %merge_x.4.refs_10_), channel_id=1, source_target_pairs={{0,3},{1,0},{2,1},{3,2},{4,7},{5,4},{6,5},{7,6},{8,11},{9,8},{10,9... | collective-permute-start | bytes 786440 | tf_op jit(solution)/shard_map/ppermute | solution.py:295
  103.3 3.4 %collective-permute-done.27.refs_11_ = bf16[512,256]{1,0:T(8,128)(2,1)S(1)} collective-permute-done((bf16[512,256]{1,0:T(8,128)(2,1)S(1)}, bf16[512,256]{1,0:T(8,128)(2,1)S(1)}, u32[]{:S(2)}, u32[]{:S(2)}) %collective-permute-start.27) | collective-permute-done | bytes 262176 | tf_op jit(solution)/shard_map/ppermute | solution.py:295
  106.7 2.4 %collective-permute-done.28.refs_12_ = bf16[512,256]{1,0:T(8,128)(2,1)S(1)} collective-permute-done((bf16[512,256]{1,0:T(8,128)(2,1)S(1)}, bf16[512,256]{1,0:T(8,128)(2,1)S(1)}, u32[]{:S(2)}, u32[]{:S(2)}) %collective-permute-start.28) | collective-permute-done | bytes 262176 | tf_op jit(solution)/shard_map/ppermute | solution.py:295
  109.0 1.2 %collective-permute-done.29.refs_13_ = bf16[512,256]{1,0:T(8,128)(2,1)S(1)} collective-permute-done((bf16[512,256]{1,0:T(8,128)(2,1)S(1)}, bf16[512,256]{1,0:T(8,128)(2,1)S(1)}, u32[]{:S(2)}, u32[]{:S(2)}) %collective-permute-start.29) | collective-permute-done | bytes 262176 | tf_op jit(solution)/shard_map/ppermute | solution.py:295
  110.2 2.2 %backward.3 = f32[1792,256]{1,0:T(8,128)S(1)} custom-call(bf16[128,1792]{1,0:T(8,128)(2,1)S(1)} %copy-done.1, bf16[128,1792]{1,0:T(8,128)(2,1)S(1)} %collective-permute-done.refs_1_, bf16[128,1792]{1,0:T(8,128)(2,1)S(1)} %gate.8.refs_2_, bf16[128,1792]{1,0:T(8,128)(2,1)S(1)} %gate.9.refs_3_, bf16[128,1792]{1,0:T(8,128)(2,1)S(1)} %collective-permute-done.4.refs_1_.refs_4_, ...), custom_call_target="tpu_custom_call" | custom-call | tf_op jit(solution)/shard_map/backward/pallas_call | solution.py:62
  112.4 1.5 %collective-permute-done.37 = bf16[1792,256]{1,0:T(8,128)(2,1)S(1)} collective-permute-done((bf16[1792,256]{1,0:T(8,128)(2,1)S(1)}, bf16[1792,256]{1,0:T(8,128)(2,1)S(1)}, u32[]{:S(2)}, u32[]{:S(2)}) %collective-permute-start.37) | collective-permute-done | bytes 917536 | tf_op jit(solution)/shard_map/ppermute | solution.py:291
  114.3 2.2 %fusion.2 = (bf16[1792,128]{1,0:T(8,128)(2,1)}, f32[1792,128]{1,0:T(8,128)}, f32[1792,128]{1,0:T(8,128)}) fusion(pred[1792,128]{1,0:T(8,128)(4,1)S(1)} %get-tuple-element.48, bf16[1792,128]{1,0:T(8,128)(2,1)S(1)} %copy-done, f32[1792,256]{1,0:T(8,128)S(1)} %convert_add_fusion, f32[1792,128]{1,0:T(8,128)S(1)} %copy-done.3, f32[1792]{0:T(1024)S(1)} %sqrt_reduce_fusion), kind=kLoop, calls=%fused_computation.6 | loop fusion | flops 3899392 | bytes 5741568 | tf_op jit(solution)/shard_map/convert_element_type | solution.py:358
  (60 shorter events, 7.6 us)
Async XLA Ops:
  0.6 2.6 %collective-permute-start = (bf16[128,1792]{1,0:T(8,128)(2,1)}, bf16[128,1792]{1,0:T(8,128)(2,1)S(1)}, u32[]{:S(2)}, u32[]{:S(2)}) collective-permute-start(bf16[128,1792]{1,0:T(8,128)(2,1)} %refs_0_.5), channel_id=1, source_target_pairs={{0,8},{8,0},{16,24},{24,16},{32,40},{40,32},{48,56},{56,48},{64,72... | collective-permute-start | bytes 1376264 | tf_op jit(solution)/shard_map/ppermute | solution.py:288
  0.7 12.6 %collective-permute-start.1 = (bf16[128,1792]{1,0:T(8,128)(2,1)}, bf16[128,1792]{1,0:T(8,128)(2,1)S(1)}, u32[]{:S(2)}, u32[]{:S(2)}) collective-permute-start(bf16[128,1792]{1,0:T(8,128)(2,1)} %refs_0_.5), channel_id=1, source_target_pairs={{0,16},{8,120},{16,32},{24,8},{32,48},{40,24},{48,64},{56,40},{64,... | collective-permute-start | bytes 1376264 | tf_op jit(solution)/shard_map/ppermute | solution.py:285
  2.7 10.8 %collective-permute-start.3 = (bf16[1792,128]{1,0:T(8,128)(2,1)}, bf16[1792,128]{1,0:T(8,128)(2,1)S(1)}, u32[]{:S(2)}, u32[]{:S(2)}) collective-permute-start(bf16[1792,128]{1,0:T(8,128)(2,1)} %refs_2_.1), channel_id=1, source_target_pairs={{0,128},{8,136},{16,144},{24,152},{32,160},{40,168},{48,176},{56,1... | collective-permute-start | bytes 1376264 | tf_op jit(solution)/shard_map/ppermute | solution.py:291
  3.3 15.0 %collective-permute-start.2 = (bf16[128,1792]{1,0:T(8,128)(2,1)S(1)}, bf16[128,1792]{1,0:T(8,128)(2,1)S(1)}, u32[]{:S(2)}, u32[]{:S(2)}) collective-permute-start(bf16[128,1792]{1,0:T(8,128)(2,1)S(1)} %collective-permute-done.refs_1_), channel_id=1, source_target_pairs={{0,16},{8,120},{16,32},{24,8},{32,48},{40,24},{48,64},{56,40},{64,... | collective-permute-start | bytes 1376264 | tf_op jit(solution)/shard_map/ppermute | solution.py:285
  6.7 16.3 %collective-permute-start.7 = (bf16[1792,128]{1,0:T(8,128)(2,1)S(1)}, bf16[1792,128]{1,0:T(8,128)(2,1)S(1)}, u32[]{:S(2)}, u32[]{:S(2)}) collective-permute-start(bf16[1792,128]{1,0:T(8,128)(2,1)S(1)} %get-tuple-element.47.refs_1_.refs_9_.refs_3_), channel_id=1, source_target_pairs={{0,128},{8,136},{16,144},{24,152},{32,160},{40,168},{48,176},{56,1... | collective-permute-start | bytes 1376264 | tf_op jit(solution)/shard_map/ppermute | solution.py:291
  13.3 13.1 %copy-start.2 = (bf16[512,128]{1,0:T(8,128)(2,1)S(1)}, bf16[512,128]{1,0:T(8,128)(2,1)}, u32[]{:S(2)}) copy-start(bf16[512,128]{1,0:T(8,128)(2,1)} %refs_6_.1) | copy-start | bytes 393220
  13.3 18.0 %copy-start = (bf16[1792,128]{1,0:T(8,128)(2,1)S(1)}, bf16[1792,128]{1,0:T(8,128)(2,1)}, u32[]{:S(2)}) copy-start(bf16[1792,128]{1,0:T(8,128)(2,1)} %refs_2_.1) | copy-start | bytes 1376260
  13.3 18.0 %copy-start.1 = (bf16[128,1792]{1,0:T(8,128)(2,1)S(1)}, bf16[128,1792]{1,0:T(8,128)(2,1)}, u32[]{:S(2)}) copy-start(bf16[128,1792]{1,0:T(8,128)(2,1)} %refs_0_.5) | copy-start | bytes 1376260
  13.3 9.6 %collective-permute-start.4 = (bf16[128,1792]{1,0:T(8,128)(2,1)S(1)}, bf16[128,1792]{1,0:T(8,128)(2,1)S(1)}, u32[]{:S(2)}, u32[]{:S(2)}) collective-permute-start(bf16[128,1792]{1,0:T(8,128)(2,1)S(1)} %gate.8.refs_2_), channel_id=1, source_target_pairs={{0,8},{8,0},{16,24},{24,16},{32,40},{40,32},{48,56},{56,48},{64,72... | collective-permute-start | bytes 1376264 | tf_op jit(solution)/shard_map/ppermute | solution.py:288
  13.4 9.8 %collective-permute-start.6 = (bf16[128,1792]{1,0:T(8,128)(2,1)S(1)}, bf16[128,1792]{1,0:T(8,128)(2,1)S(1)}, u32[]{:S(2)}, u32[]{:S(2)}) collective-permute-start(bf16[128,1792]{1,0:T(8,128)(2,1)S(1)} %gate.8.refs_2_), channel_id=1, source_target_pairs={{0,16},{8,120},{16,32},{24,8},{32,48},{40,24},{48,64},{56,40},{64,... | collective-permute-start | bytes 1376264 | tf_op jit(solution)/shard_map/ppermute | solution.py:285
  18.3 5.0 %collective-permute-start.5 = (bf16[128,1792]{1,0:T(8,128)(2,1)S(1)}, bf16[128,1792]{1,0:T(8,128)(2,1)S(1)}, u32[]{:S(2)}, u32[]{:S(2)}) collective-permute-start(bf16[128,1792]{1,0:T(8,128)(2,1)S(1)} %gate.9.refs_3_), channel_id=1, source_target_pairs={{0,8},{8,0},{16,24},{24,16},{32,40},{40,32},{48,56},{56,48},{64,72... | collective-permute-start | bytes 1376264 | tf_op jit(solution)/shard_map/ppermute | solution.py:288
  19.6 9.7 %collective-permute-start.9 = (bf16[128,1792]{1,0:T(8,128)(2,1)S(1)}, bf16[128,1792]{1,0:T(8,128)(2,1)S(1)}, u32[]{:S(2)}, u32[]{:S(2)}) collective-permute-start(bf16[128,1792]{1,0:T(8,128)(2,1)S(1)} %gate.9.refs_3_), channel_id=1, source_target_pairs={{0,16},{8,120},{16,32},{24,8},{32,48},{40,24},{48,64},{56,40},{64,... | collective-permute-start | bytes 1376264 | tf_op jit(solution)/shard_map/ppermute | solution.py:285
  23.2 8.2 %collective-permute-start.8 = (bf16[128,1792]{1,0:T(8,128)(2,1)S(1)}, bf16[128,1792]{1,0:T(8,128)(2,1)S(1)}, u32[]{:S(2)}, u32[]{:S(2)}) collective-permute-start(bf16[128,1792]{1,0:T(8,128)(2,1)S(1)} %gate.10.refs_6_), channel_id=1, source_target_pairs={{0,8},{8,0},{16,24},{24,16},{32,40},{40,32},{48,56},{56,48},{64,72... | collective-permute-start | bytes 1376264 | tf_op jit(solution)/shard_map/ppermute | solution.py:288
  26.4 10.4 %collective-permute-start.10 = (bf16[128,1792]{1,0:T(8,128)(2,1)S(1)}, bf16[128,1792]{1,0:T(8,128)(2,1)S(1)}, u32[]{:S(2)}, u32[]{:S(2)}) collective-permute-start(bf16[128,1792]{1,0:T(8,128)(2,1)S(1)} %gate.10.refs_6_), channel_id=1, source_target_pairs={{0,16},{8,120},{16,32},{24,8},{32,48},{40,24},{48,64},{56,40},{64,... | collective-permute-start | bytes 1376264 | tf_op jit(solution)/shard_map/ppermute | solution.py:285
  26.4 5.0 %collective-permute-start.11 = (bf16[512,128]{1,0:T(8,128)(2,1)S(1)}, bf16[512,128]{1,0:T(8,128)(2,1)S(1)}, u32[]{:S(2)}, u32[]{:S(2)}) collective-permute-start(bf16[512,128]{1,0:T(8,128)(2,1)S(1)} %copy-done.2), channel_id=1, source_target_pairs={{0,128},{8,136},{16,144},{24,152},{32,160},{40,168},{48,176},{56,1... | collective-permute-start | bytes 393224 | tf_op jit(solution)/shard_map/ppermute | solution.py:291
  29.3 23.5 %collective-permute-start.12 = (bf16[128,1792]{1,0:T(8,128)(2,1)S(1)}, bf16[128,1792]{1,0:T(8,128)(2,1)S(1)}, u32[]{:S(2)}, u32[]{:S(2)}) collective-permute-start(bf16[128,1792]{1,0:T(8,128)(2,1)S(1)} %collective-permute-done.9.refs_0_), channel_id=1, source_target_pairs={{0,16},{8,120},{16,32},{24,8},{32,48},{40,24},{48,64},{56,40},{64,... | collective-permute-start | bytes 1376264 | tf_op jit(solution)/shard_map/ppermute | solution.py:285
  36.8 16.0 %collective-permute-start.16 = (bf16[128,1792]{1,0:T(8,128)(2,1)S(1)}, bf16[128,1792]{1,0:T(8,128)(2,1)S(1)}, u32[]{:S(2)}, u32[]{:S(2)}) collective-permute-start(bf16[128,1792]{1,0:T(8,128)(2,1)S(1)} %gate.11.refs_1_), channel_id=1, source_target_pairs={{0,16},{8,120},{16,32},{24,8},{32,48},{40,24},{48,64},{56,40},{64,... | collective-permute-start | bytes 1376264 | tf_op jit(solution)/shard_map/ppermute | solution.py:285
  36.8 8.9 %collective-permute-start.13 = (bf16[256,512]{1,0:T(8,128)(2,1)S(1)}, bf16[256,512]{1,0:T(8,128)(2,1)S(1)}, u32[]{:S(2)}, u32[]{:S(2)}) collective-permute-start(bf16[256,512]{1,0:T(8,128)(2,1)S(1)} %get-tuple-element.26), channel_id=1, source_target_pairs={{0,1},{1,2},{2,3},{3,0},{4,5},{5,6},{6,7},{7,4},{8,9},{9,10},{10,1... | collective-permute-start | bytes 786440 | tf_op jit(solution)/shard_map/ppermute | solution.py:295
  38.4 8.1 %collective-permute-start.14 = (bf16[256,512]{1,0:T(8,128)(2,1)S(1)}, bf16[256,512]{1,0:T(8,128)(2,1)S(1)}, u32[]{:S(2)}, u32[]{:S(2)}) collective-permute-start(bf16[256,512]{1,0:T(8,128)(2,1)S(1)} %get-tuple-element.27), channel_id=1, source_target_pairs={{0,3},{1,0},{2,1},{3,2},{4,7},{5,4},{6,5},{7,6},{8,11},{9,8},{10,9... | collective-permute-start | bytes 786440 | tf_op jit(solution)/shard_map/ppermute | solution.py:295
  40.0 12.6 %collective-permute-start.15 = (bf16[256,512]{1,0:T(8,128)(2,1)S(1)}, bf16[256,512]{1,0:T(8,128)(2,1)S(1)}, u32[]{:S(2)}, u32[]{:S(2)}) collective-permute-start(bf16[256,512]{1,0:T(8,128)(2,1)S(1)} %get-tuple-element.28), channel_id=1, source_target_pairs={{0,2},{1,3},{2,0},{3,1},{4,6},{5,7},{6,4},{7,5},{8,10},{9,11},{10,... | collective-permute-start | bytes 786440 | tf_op jit(solution)/shard_map/ppermute | solution.py:295
  52.9 4.7 %collective-permute-start.17 = (bf16[512,1792]{1,0:T(8,128)(2,1)S(1)}, bf16[512,1792]{1,0:T(8,128)(2,1)S(1)}, u32[]{:S(2)}, u32[]{:S(2)}) collective-permute-start(bf16[512,1792]{1,0:T(8,128)(2,1)S(1)} %stack.1.refs_0_.refs_8_), channel_id=1, source_target_pairs={{0,8},{8,0},{16,24},{24,16},{32,40},{40,32},{48,56},{56,48},{64,72... | collective-permute-start | bytes 5505032 | tf_op jit(solution)/shard_map/ppermute | solution.py:288
  54.2 9.8 %collective-permute-start.21 = (bf16[256,512]{1,0:T(8,128)(2,1)S(1)}, bf16[256,512]{1,0:T(8,128)(2,1)S(1)}, u32[]{:S(2)}, u32[]{:S(2)}) collective-permute-start(bf16[256,512]{1,0:T(8,128)(2,1)S(1)} %get-tuple-element.35), channel_id=1, source_target_pairs={{0,4},{1,5},{2,6},{3,7},{4,0},{5,1},{6,2},{7,3},{8,12},{9,13},{10,... | collective-permute-start | bytes 786440 | tf_op jit(solution)/shard_map/ppermute | solution.py:298
  60.1 7.1 %collective-permute-start.18 = (bf16[256,256]{1,0:T(8,128)(2,1)S(1)}, bf16[256,256]{1,0:T(8,128)(2,1)S(1)}, u32[]{:S(2)}, u32[]{:S(2)}) collective-permute-start(bf16[256,256]{1,0:T(8,128)(2,1)S(1)} %get-tuple-element.32), channel_id=1, source_target_pairs={{0,1},{1,2},{2,3},{3,0},{4,5},{5,6},{6,7},{7,4},{8,9},{9,10},{10,1... | collective-permute-start | bytes 393224 | tf_op jit(solution)/shard_map/ppermute | solution.py:295
  61.6 7.7 %collective-permute-start.19 = (bf16[256,256]{1,0:T(8,128)(2,1)S(1)}, bf16[256,256]{1,0:T(8,128)(2,1)S(1)}, u32[]{:S(2)}, u32[]{:S(2)}) collective-permute-start(bf16[256,256]{1,0:T(8,128)(2,1)S(1)} %get-tuple-element.33), channel_id=1, source_target_pairs={{0,3},{1,0},{2,1},{3,2},{4,7},{5,4},{6,5},{7,6},{8,11},{9,8},{10,9... | collective-permute-start | bytes 393224 | tf_op jit(solution)/shard_map/ppermute | solution.py:295
  63.4 7.9 %collective-permute-start.20 = (bf16[256,256]{1,0:T(8,128)(2,1)S(1)}, bf16[256,256]{1,0:T(8,128)(2,1)S(1)}, u32[]{:S(2)}, u32[]{:S(2)}) collective-permute-start(bf16[256,256]{1,0:T(8,128)(2,1)S(1)} %get-tuple-element.34), channel_id=1, source_target_pairs={{0,2},{1,3},{2,0},{3,1},{4,6},{5,7},{6,4},{7,5},{8,10},{9,11},{10,... | collective-permute-start | bytes 393224 | tf_op jit(solution)/shard_map/ppermute | solution.py:295
  64.1 12.5 %collective-permute-start.31 = (bf16[256,256]{1,0:T(8,128)(2,1)S(1)}, bf16[256,256]{1,0:T(8,128)(2,1)S(1)}, u32[]{:S(2)}, u32[]{:S(2)}) collective-permute-start(bf16[256,256]{1,0:T(8,128)(2,1)S(1)} %get-tuple-element.37.refs_4_.refs_8_), channel_id=1, source_target_pairs={{0,1},{1,2},{2,3},{3,0},{4,5},{5,6},{6,7},{7,4},{8,9},{9,10},{10,1... | collective-permute-start | bytes 393224 | tf_op jit(solution)/shard_map/ppermute | solution.py:295
  71.4 8.1 %collective-permute-start.30 = (bf16[256,256]{1,0:T(8,128)(2,1)S(1)}, bf16[256,256]{1,0:T(8,128)(2,1)S(1)}, u32[]{:S(2)}, u32[]{:S(2)}) collective-permute-start(bf16[256,256]{1,0:T(8,128)(2,1)S(1)} %get-tuple-element.44), channel_id=1, source_target_pairs={{0,4},{1,5},{2,6},{3,7},{4,0},{5,1},{6,2},{7,3},{8,12},{9,13},{10,... | collective-permute-start | bytes 393224 | tf_op jit(solution)/shard_map/ppermute | solution.py:298
  73.6 10.2 %collective-permute-start.24 = (bf16[256,256]{1,0:T(8,128)(2,1)S(1)}, bf16[256,256]{1,0:T(8,128)(2,1)S(1)}, u32[]{:S(2)}, u32[]{:S(2)}) collective-permute-start(bf16[256,256]{1,0:T(8,128)(2,1)S(1)} %gate.15), channel_id=1, source_target_pairs={{0,2},{1,3},{2,0},{3,1},{4,6},{5,7},{6,4},{7,5},{8,10},{9,11},{10,... | collective-permute-start | bytes 393224 | tf_op jit(solution)/shard_map/ppermute | solution.py:295
  74.5 9.7 %collective-permute-start.23 = (bf16[256,256]{1,0:T(8,128)(2,1)S(1)}, bf16[256,256]{1,0:T(8,128)(2,1)S(1)}, u32[]{:S(2)}, u32[]{:S(2)}) collective-permute-start(bf16[256,256]{1,0:T(8,128)(2,1)S(1)} %gate.14), channel_id=1, source_target_pairs={{0,3},{1,0},{2,1},{3,2},{4,7},{5,4},{6,5},{7,6},{8,11},{9,8},{10,9... | collective-permute-start | bytes 393224 | tf_op jit(solution)/shard_map/ppermute | solution.py:295
  76.3 10.8 %collective-permute-start.22 = (bf16[256,256]{1,0:T(8,128)(2,1)S(1)}, bf16[256,256]{1,0:T(8,128)(2,1)S(1)}, u32[]{:S(2)}, u32[]{:S(2)}) collective-permute-start(bf16[256,256]{1,0:T(8,128)(2,1)S(1)} %gate.13), channel_id=1, source_target_pairs={{0,1},{1,2},{2,3},{3,0},{4,5},{5,6},{6,7},{7,4},{8,9},{9,10},{10,1... | collective-permute-start | bytes 393224 | tf_op jit(solution)/shard_map/ppermute | solution.py:295
  76.6 12.2 %collective-permute-start.35 = (bf16[256,256]{1,0:T(8,128)(2,1)S(1)}, bf16[256,256]{1,0:T(8,128)(2,1)S(1)}, u32[]{:S(2)}, u32[]{:S(2)}) collective-permute-start(bf16[256,256]{1,0:T(8,128)(2,1)S(1)} %get-tuple-element.37.refs_4_.refs_8_), channel_id=1, source_target_pairs={{0,3},{1,0},{2,1},{3,2},{4,7},{5,4},{6,5},{7,6},{8,11},{9,8},{10,9... | collective-permute-start | bytes 393224 | tf_op jit(solution)/shard_map/ppermute | solution.py:295
  79.5 3.6 %collective-permute-start.25 = (f32[1,1792]{1,0:T(1,128)S(1)}, f32[1,1792]{1,0:T(1,128)S(1)}, u32[]{:S(2)}, u32[]{:S(2)}) collective-permute-start(f32[1,1792]{1,0:T(1,128)S(1)} %get-tuple-element.36.refs_0_), channel_id=1, source_target_pairs={{0,128},{8,136},{16,144},{24,152},{32,160},{40,168},{48,176},{56,1... | collective-permute-start | bytes 21512 | tf_op jit(solution)/shard_map/ppermute | solution.py:291
  83.2 7.1 %collective-permute-start.36 = (bf16[256,256]{1,0:T(8,128)(2,1)S(1)}, bf16[256,256]{1,0:T(8,128)(2,1)S(1)}, u32[]{:S(2)}, u32[]{:S(2)}) collective-permute-start(bf16[256,256]{1,0:T(8,128)(2,1)S(1)} %get-tuple-element.37.refs_4_.refs_8_), channel_id=1, source_target_pairs={{0,2},{1,3},{2,0},{3,1},{4,6},{5,7},{6,4},{7,5},{8,10},{9,11},{10,... | collective-permute-start | bytes 393224 | tf_op jit(solution)/shard_map/ppermute | solution.py:295
  83.8 7.7 %collective-permute-start.32 = (bf16[256,256]{1,0:T(8,128)(2,1)S(1)}, bf16[256,256]{1,0:T(8,128)(2,1)S(1)}, u32[]{:S(2)}, u32[]{:S(2)}) collective-permute-start(bf16[256,256]{1,0:T(8,128)(2,1)S(1)} %merge_x.5.refs_2_), channel_id=1, source_target_pairs={{0,1},{1,2},{2,3},{3,0},{4,5},{5,6},{6,7},{7,4},{8,9},{9,10},{10,1... | collective-permute-start | bytes 393224 | tf_op jit(solution)/shard_map/ppermute | solution.py:295
  84.2 7.3 %collective-permute-start.33 = (bf16[256,256]{1,0:T(8,128)(2,1)S(1)}, bf16[256,256]{1,0:T(8,128)(2,1)S(1)}, u32[]{:S(2)}, u32[]{:S(2)}) collective-permute-start(bf16[256,256]{1,0:T(8,128)(2,1)S(1)} %merge_x.5.refs_2_), channel_id=1, source_target_pairs={{0,3},{1,0},{2,1},{3,2},{4,7},{5,4},{6,5},{7,6},{8,11},{9,8},{10,9... | collective-permute-start | bytes 393224 | tf_op jit(solution)/shard_map/ppermute | solution.py:295
  87.0 6.5 %collective-permute-start.34 = (bf16[256,256]{1,0:T(8,128)(2,1)S(1)}, bf16[256,256]{1,0:T(8,128)(2,1)S(1)}, u32[]{:S(2)}, u32[]{:S(2)}) collective-permute-start(bf16[256,256]{1,0:T(8,128)(2,1)S(1)} %merge_x.5.refs_2_), channel_id=1, source_target_pairs={{0,2},{1,3},{2,0},{3,1},{4,6},{5,7},{6,4},{7,5},{8,10},{9,11},{10,... | collective-permute-start | bytes 393224 | tf_op jit(solution)/shard_map/ppermute | solution.py:295
  88.8 8.0 %collective-permute-start.26 = (bf16[256,256]{1,0:T(8,128)(2,1)S(1)}, bf16[256,256]{1,0:T(8,128)(2,1)S(1)}, u32[]{:S(2)}, u32[]{:S(2)}) collective-permute-start(bf16[256,256]{1,0:T(8,128)(2,1)S(1)} %get-tuple-element.42), channel_id=1, source_target_pairs={{0,4},{1,5},{2,6},{3,7},{4,0},{5,1},{6,2},{7,3},{8,12},{9,13},{10,... | collective-permute-start | bytes 393224 | tf_op jit(solution)/shard_map/ppermute | solution.py:298
  98.0 16.0 %collective-permute-start.37 = (bf16[1792,256]{1,0:T(8,128)(2,1)S(1)}, bf16[1792,256]{1,0:T(8,128)(2,1)S(1)}, u32[]{:S(2)}, u32[]{:S(2)}) collective-permute-start(bf16[1792,256]{1,0:T(8,128)(2,1)S(1)} %backward.5), channel_id=1, source_target_pairs={{0,128},{8,136},{16,144},{24,152},{32,160},{40,168},{48,176},{56,1... | collective-permute-start | bytes 2752520 | tf_op jit(solution)/shard_map/ppermute | solution.py:291
  99.0 7.7 %collective-permute-start.27 = (bf16[512,256]{1,0:T(8,128)(2,1)S(1)}, bf16[512,256]{1,0:T(8,128)(2,1)S(1)}, u32[]{:S(2)}, u32[]{:S(2)}) collective-permute-start(bf16[512,256]{1,0:T(8,128)(2,1)S(1)} %merge_x.4.refs_10_), channel_id=1, source_target_pairs={{0,1},{1,2},{2,3},{3,0},{4,5},{5,6},{6,7},{7,4},{8,9},{9,10},{10,1... | collective-permute-start | bytes 786440 | tf_op jit(solution)/shard_map/ppermute | solution.py:295
  99.1 9.9 %collective-permute-start.28 = (bf16[512,256]{1,0:T(8,128)(2,1)S(1)}, bf16[512,256]{1,0:T(8,128)(2,1)S(1)}, u32[]{:S(2)}, u32[]{:S(2)}) collective-permute-start(bf16[512,256]{1,0:T(8,128)(2,1)S(1)} %merge_x.4.refs_10_), channel_id=1, source_target_pairs={{0,3},{1,0},{2,1},{3,2},{4,7},{5,4},{6,5},{7,6},{8,11},{9,8},{10,9... | collective-permute-start | bytes 786440 | tf_op jit(solution)/shard_map/ppermute | solution.py:295
  102.3 7.9 %collective-permute-start.29 = (bf16[512,256]{1,0:T(8,128)(2,1)S(1)}, bf16[512,256]{1,0:T(8,128)(2,1)S(1)}, u32[]{:S(2)}, u32[]{:S(2)}) collective-permute-start(bf16[512,256]{1,0:T(8,128)(2,1)S(1)} %merge_x.4.refs_10_), channel_id=1, source_target_pairs={{0,2},{1,3},{2,0},{3,1},{4,6},{5,7},{6,4},{7,5},{8,10},{9,11},{10,... | collective-permute-start | bytes 786440 | tf_op jit(solution)/shard_map/ppermute | solution.py:295
  112.4 1.8 %copy-start.3 = (f32[1792,128]{1,0:T(8,128)S(1)}, f32[1792,128]{1,0:T(8,128)}, u32[]{:S(2)}) copy-start(f32[1792,128]{1,0:T(8,128)} %param.9) | copy-start | bytes 2752516

commit v4 on v3

--- a/solution.py
+++ b/solution.py
@@ -336,7 +336,7 @@
     own0, other0 = merge_x(keep0, sent0, 2, (), [squares])
     keep1, send1 = merge_y(mine1, around(ahead1[3:]), 2 * cols, [other0])
     back0 = around([other0] * 3)
-    (other1,) = merge_x(keep1, over(send1), 1, (), back0[:1])
+    (other1,) = merge_x(keep1, over(send1), 1, (), back0)
     init = backward(early, [other0] + back0, f32)
     back1 = around([other1] * 3)
     got2 = around([gate(v, keep1) for v in ahead1[:3]])

time: 117 us -> 115 us (0.983)
  waiting for transfers between devices: 53.6 us -> 48.1 us
  starting transfers between devices: 48 us -> 51.6 us
    ppermute x18, waiting for transfers between devices: 25.2 us -> 20.9 us  [around(): return [lax.ppermute(v, 'mp', y_perm(dy)) for v, dy in zip(pieces, ahead)]]
    ppermute x18, starting transfers between devices: 26.1 us -> 28 us  [around(): return [lax.ppermute(v, 'mp', y_perm(dy)) for v, dy in zip(pieces, ahead)]]
    ppermute x3, waiting for transfers between devices: 3.57 us -> 1.84 us  [over(): return lax.ppermute(value, 'mp', PAIR_X_HI)]
  transfers between devices with their start and end apart: 38 -> 38, of which waited for: 22 -> 20; matrix products, arithmetic and copies ran while one was open for 1% -> 1% of each run, Pallas kernels for 7% -> 7%
where the time goes in v4:
time: 115 us; the launch traced here: 114 us
  starting transfers between devices  51.6 us (45%)
  waiting for transfers between devices  48.1 us (42%)
  Pallas kernels  9.89 us (9%)
  other arithmetic  4.06 us (4%)
    ppermute x18, starting transfers between devices, around(): return [lax.ppermute(v, 'mp', y_perm(dy)) for v, dy in zip(pieces, ahead)]  28 us
    ppermute x18, waiting for transfers between devices, around(): return [lax.ppermute(v, 'mp', y_perm(dy)) for v, dy in zip(pieces, ahead)]  20.9 us
    ppermute x7, waiting for transfers between devices, ring(): return lax.ppermute(value, 'dp', RING)  14.4 us
    pallas_call x12, Pallas kernels, vmem_call(): pl.pallas_call(kernel, out_shape=out_shape, in_specs=specs, out_specs=jax...  9.88 us
    ppermute x5, waiting for transfers between devices, across(): return lax.ppermute(value, 'dp', PAIR_X)  9.62 us
    ppermute x3, starting transfers between devices, over(): return lax.ppermute(value, 'mp', PAIR_X_HI)  6.88 us
    ppermute x5, starting transfers between devices, across(): return lax.ppermute(value, 'dp', PAIR_X)  6.68 us
    ppermute x5, starting transfers between devices, swap(): return lax.ppermute(value, 'dp', PAIR_CORE)  6.05 us
  transfers between devices with their start and end apart: 38, of which 20 were waited for; matrix products, arithmetic and copies ran while one was open for 1% of the time, Pallas kernels for 7%

profile of v4, /device:TPU:2, one launch (start us, length us, event | category | flops | bytes accessed | tf_op | source)
XLA Modules:
  0.0 114.5 jit_solution(8722341412407560972)
XLA Ops:
  0.7 2.0 %collective-permute-start.1 = (bf16[128,1792]{1,0:T(8,128)(2,1)}, bf16[128,1792]{1,0:T(8,128)(2,1)S(1)}, u32[]{:S(2)}, u32[]{:S(2)}) collective-permute-start(bf16[128,1792]{1,0:T(8,128)(2,1)} %refs_0_.5), channel_id=1, source_target_pairs={{0,16},{8,120},{16,32},{24,8},{32,48},{40,24},{48,64},{56,40},{64,... | collective-permute-start | bytes 1376264 | tf_op jit(solution)/shard_map/ppermute | solution.py:285
  3.3 1.9 %collective-permute-start.2 = (bf16[128,1792]{1,0:T(8,128)(2,1)S(1)}, bf16[128,1792]{1,0:T(8,128)(2,1)S(1)}, u32[]{:S(2)}, u32[]{:S(2)}) collective-permute-start(bf16[128,1792]{1,0:T(8,128)(2,1)S(1)} %collective-permute-done.refs_1_), channel_id=1, source_target_pairs={{0,16},{8,120},{16,32},{24,8},{32,48},{40,24},{48,64},{56,40},{64,... | collective-permute-start | bytes 1376264 | tf_op jit(solution)/shard_map/ppermute | solution.py:285
  5.2 1.5 %negate_select_fusion = (bf16[1792,128]{1,0:T(8,128)(2,1)S(1)}, pred[1792,128]{1,0:T(8,128)(4,1)S(1)}) fusion(bf16[1792,128]{1,0:T(8,128)(2,1)} %refs_2_.1, s32[1792,128]{1,0:T(8,128)} %param.8), kind=kLoop, calls=%fused_computation.12 | loop fusion | flops 688128 | bytes 2064384 | tf_op jit(solution)/shard_map/jit(_where)/select_n | solution.py:304
  6.7 1.6 %collective-permute-start.7 = (bf16[1792,128]{1,0:T(8,128)(2,1)S(1)}, bf16[1792,128]{1,0:T(8,128)(2,1)S(1)}, u32[]{:S(2)}, u32[]{:S(2)}) collective-permute-start(bf16[1792,128]{1,0:T(8,128)(2,1)S(1)} %get-tuple-element.47.refs_1_.refs_9_.refs_3_), channel_id=1, source_target_pairs={{0,128},{8,136},{16,144},{24,152},{32,160},{40,168},{48,176},{56,1... | collective-permute-start | bytes 1376264 | tf_op jit(solution)/shard_map/ppermute | solution.py:291
  8.3 5.0 %collective-permute-done.1.refs_0_ = bf16[128,1792]{1,0:T(8,128)(2,1)S(1)} collective-permute-done((bf16[128,1792]{1,0:T(8,128)(2,1)}, bf16[128,1792]{1,0:T(8,128)(2,1)S(1)}, u32[]{:S(2)}, u32[]{:S(2)}) %collective-permute-start.1) | collective-permute-done | bytes 458784 | tf_op jit(solution)/shard_map/ppermute | solution.py:285
  13.5 4.7 %collective-permute-done.2.refs_0_ = bf16[128,1792]{1,0:T(8,128)(2,1)S(1)} collective-permute-done((bf16[128,1792]{1,0:T(8,128)(2,1)S(1)}, bf16[128,1792]{1,0:T(8,128)(2,1)S(1)}, u32[]{:S(2)}, u32[]{:S(2)}) %collective-permute-start.2) | collective-permute-done | bytes 458784 | tf_op jit(solution)/shard_map/ppermute | solution.py:285
  18.3 1.4 %collective-permute-start.5 = (bf16[128,1792]{1,0:T(8,128)(2,1)S(1)}, bf16[128,1792]{1,0:T(8,128)(2,1)S(1)}, u32[]{:S(2)}, u32[]{:S(2)}) collective-permute-start(bf16[128,1792]{1,0:T(8,128)(2,1)S(1)} %gate.9.refs_3_), channel_id=1, source_target_pairs={{0,8},{8,0},{16,24},{24,16},{32,40},{40,32},{48,56},{56,48},{64,72... | collective-permute-start | bytes 1376264 | tf_op jit(solution)/shard_map/ppermute | solution.py:288
  19.6 3.4 %collective-permute-done.7.refs_3_.refs_11_.refs_5_ = bf16[1792,128]{1,0:T(8,128)(2,1)S(1)} collective-permute-done((bf16[1792,128]{1,0:T(8,128)(2,1)S(1)}, bf16[1792,128]{1,0:T(8,128)(2,1)S(1)}, u32[]{:S(2)}, u32[]{:S(2)}) %collective-permute-start.7) | collective-permute-done | bytes 458784 | tf_op jit(solution)/shard_map/ppermute | solution.py:291
  23.2 3.2 %collective-permute-start.8 = (bf16[128,1792]{1,0:T(8,128)(2,1)S(1)}, bf16[128,1792]{1,0:T(8,128)(2,1)S(1)}, u32[]{:S(2)}, u32[]{:S(2)}) collective-permute-start(bf16[128,1792]{1,0:T(8,128)(2,1)S(1)} %gate.10.refs_6_), channel_id=1, source_target_pairs={{0,8},{8,0},{16,24},{24,16},{32,40},{40,32},{48,56},{56,48},{64,72... | collective-permute-start | bytes 1376264 | tf_op jit(solution)/shard_map/ppermute | solution.py:288
  26.4 1.5 %collective-permute-start.11 = (bf16[512,128]{1,0:T(8,128)(2,1)S(1)}, bf16[512,128]{1,0:T(8,128)(2,1)S(1)}, u32[]{:S(2)}, u32[]{:S(2)}) collective-permute-start(bf16[512,128]{1,0:T(8,128)(2,1)S(1)} %copy-done.2), channel_id=1, source_target_pairs={{0,128},{8,136},{16,144},{24,152},{32,160},{40,168},{48,176},{56,1... | collective-permute-start | bytes 393224 | tf_op jit(solution)/shard_map/ppermute | solution.py:291
  27.9 1.4 %collective-permute-done.9.refs_0_ = bf16[128,1792]{1,0:T(8,128)(2,1)S(1)} collective-permute-done((bf16[128,1792]{1,0:T(8,128)(2,1)S(1)}, bf16[128,1792]{1,0:T(8,128)(2,1)S(1)}, u32[]{:S(2)}, u32[]{:S(2)}) %collective-permute-start.9) | collective-permute-done | bytes 458784 | tf_op jit(solution)/shard_map/ppermute | solution.py:285
  29.3 2.0 %collective-permute-done.11.refs_13_.refs_7_ = bf16[512,128]{1,0:T(8,128)(2,1)S(1)} collective-permute-done((bf16[512,128]{1,0:T(8,128)(2,1)S(1)}, bf16[512,128]{1,0:T(8,128)(2,1)S(1)}, u32[]{:S(2)}, u32[]{:S(2)}) %collective-permute-start.11) | collective-permute-done | bytes 131104 | tf_op jit(solution)/shard_map/ppermute | solution.py:291
  31.4 2.4 %forward.2 = (f32[256,512]{1,0:T(8,128)S(1)}, bf16[256,512]{1,0:T(8,128)(2,1)S(1)}, bf16[256,512]{1,0:T(8,128)(2,1)S(1)}, bf16[256,512]{1,0:T(8,128)(2,1)S(1)}, f32[1,1792]{1,0:T(1,128)S(1)}) custom-call(bf16[128,1792]{1,0:T(8,128)(2,1)S(1)} %copy-done.1, bf16[128,1792]{1,0:T(8,128)(2,1)S(1)} %collective-permute-done.refs_1_, ...), custom_call_target="tpu_custom_call" | custom-call | tf_op jit(solution)/shard_map/forward/pallas_call | solution.py:62
  33.8 3.0 %collective-permute-done.10.refs_0_ = bf16[128,1792]{1,0:T(8,128)(2,1)S(1)} collective-permute-done((bf16[128,1792]{1,0:T(8,128)(2,1)S(1)}, bf16[128,1792]{1,0:T(8,128)(2,1)S(1)}, u32[]{:S(2)}, u32[]{:S(2)}) %collective-permute-start.10) | collective-permute-done | bytes 458784 | tf_op jit(solution)/shard_map/ppermute | solution.py:285
  36.8 1.6 %collective-permute-start.13 = (bf16[256,512]{1,0:T(8,128)(2,1)S(1)}, bf16[256,512]{1,0:T(8,128)(2,1)S(1)}, u32[]{:S(2)}, u32[]{:S(2)}) collective-permute-start(bf16[256,512]{1,0:T(8,128)(2,1)S(1)} %get-tuple-element.26), channel_id=1, source_target_pairs={{0,1},{1,2},{2,3},{3,0},{4,5},{5,6},{6,7},{7,4},{8,9},{9,10},{10,1... | collective-permute-start | bytes 786440 | tf_op jit(solution)/shard_map/ppermute | solution.py:295
  38.4 1.7 %collective-permute-start.14 = (bf16[256,512]{1,0:T(8,128)(2,1)S(1)}, bf16[256,512]{1,0:T(8,128)(2,1)S(1)}, u32[]{:S(2)}, u32[]{:S(2)}) collective-permute-start(bf16[256,512]{1,0:T(8,128)(2,1)S(1)} %get-tuple-element.27), channel_id=1, source_target_pairs={{0,3},{1,0},{2,1},{3,2},{4,7},{5,4},{6,5},{7,6},{8,11},{9,8},{10,9... | collective-permute-start | bytes 786440 | tf_op jit(solution)/shard_map/ppermute | solution.py:295
  40.0 2.0 %collective-permute-start.15 = (bf16[256,512]{1,0:T(8,128)(2,1)S(1)}, bf16[256,512]{1,0:T(8,128)(2,1)S(1)}, u32[]{:S(2)}, u32[]{:S(2)}) collective-permute-start(bf16[256,512]{1,0:T(8,128)(2,1)S(1)} %get-tuple-element.28), channel_id=1, source_target_pairs={{0,2},{1,3},{2,0},{3,1},{4,6},{5,7},{6,4},{7,5},{8,10},{9,11},{10,... | collective-permute-start | bytes 786440 | tf_op jit(solution)/shard_map/ppermute | solution.py:295
  42.0 3.7 %collective-permute-done.13.refs_1_ = bf16[256,512]{1,0:T(8,128)(2,1)S(1)} collective-permute-done((bf16[256,512]{1,0:T(8,128)(2,1)S(1)}, bf16[256,512]{1,0:T(8,128)(2,1)S(1)}, u32[]{:S(2)}, u32[]{:S(2)}) %collective-permute-start.13) | collective-permute-done | bytes 262176 | tf_op jit(solution)/shard_map/ppermute | solution.py:295
  46.5 6.2 %collective-permute-done.15.refs_3_ = bf16[256,512]{1,0:T(8,128)(2,1)S(1)} collective-permute-done((bf16[256,512]{1,0:T(8,128)(2,1)S(1)}, bf16[256,512]{1,0:T(8,128)(2,1)S(1)}, u32[]{:S(2)}, u32[]{:S(2)}) %collective-permute-start.15) | collective-permute-done | bytes 262176 | tf_op jit(solution)/shard_map/ppermute | solution.py:295
  52.9 1.3 %collective-permute-start.17 = (bf16[512,1792]{1,0:T(8,128)(2,1)S(1)}, bf16[512,1792]{1,0:T(8,128)(2,1)S(1)}, u32[]{:S(2)}, u32[]{:S(2)}) collective-permute-start(bf16[512,1792]{1,0:T(8,128)(2,1)S(1)} %stack.1.refs_0_.refs_8_), channel_id=1, source_target_pairs={{0,8},{8,0},{16,24},{24,16},{32,40},{40,32},{48,56},{56,48},{64,72... | collective-permute-start | bytes 5505032 | tf_op jit(solution)/shard_map/ppermute | solution.py:288
  54.2 2.1 %collective-permute-start.21 = (bf16[256,512]{1,0:T(8,128)(2,1)S(1)}, bf16[256,512]{1,0:T(8,128)(2,1)S(1)}, u32[]{:S(2)}, u32[]{:S(2)}) collective-permute-start(bf16[256,512]{1,0:T(8,128)(2,1)S(1)} %get-tuple-element.35), channel_id=1, source_target_pairs={{0,4},{1,5},{2,6},{3,7},{4,0},{5,1},{6,2},{7,3},{8,12},{9,13},{10,... | collective-permute-start | bytes 786440 | tf_op jit(solution)/shard_map/ppermute | solution.py:298
  56.4 1.3 %collective-permute-done.17.refs_1_.refs_9_ = bf16[512,1792]{1,0:T(8,128)(2,1)S(1)} collective-permute-done((bf16[512,1792]{1,0:T(8,128)(2,1)S(1)}, bf16[512,1792]{1,0:T(8,128)(2,1)S(1)}, u32[]{:S(2)}, u32[]{:S(2)}) %collective-permute-start.17) | collective-permute-done | bytes 1835040 | tf_op jit(solution)/shard_map/ppermute | solution.py:288
  57.7 2.4 %forward.3 = (f32[256,512]{1,0:T(8,128)S(1)}, bf16[256,256]{1,0:T(8,128)(2,1)S(1)}, bf16[256,256]{1,0:T(8,128)(2,1)S(1)}, bf16[256,256]{1,0:T(8,128)(2,1)S(1)}, ...) custom-call(bf16[512,1792]{1,0:T(8,128)(2,1)S(1)} %stack.1.refs_0_.r, ...), custom_call_target="tpu_custom_call" | custom-call | tf_op jit(solution)/shard_map/forward/pallas_call | solution.py:62
  60.1 1.5 %collective-permute-start.18 = (bf16[256,256]{1,0:T(8,128)(2,1)S(1)}, bf16[256,256]{1,0:T(8,128)(2,1)S(1)}, u32[]{:S(2)}, u32[]{:S(2)}) collective-permute-start(bf16[256,256]{1,0:T(8,128)(2,1)S(1)} %get-tuple-element.32), channel_id=1, source_target_pairs={{0,1},{1,2},{2,3},{3,0},{4,5},{5,6},{6,7},{7,4},{8,9},{9,10},{10,1... | collective-permute-start | bytes 393224 | tf_op jit(solution)/shard_map/ppermute | solution.py:295
  61.6 1.8 %collective-permute-start.19 = (bf16[256,256]{1,0:T(8,128)(2,1)S(1)}, bf16[256,256]{1,0:T(8,128)(2,1)S(1)}, u32[]{:S(2)}, u32[]{:S(2)}) collective-permute-start(bf16[256,256]{1,0:T(8,128)(2,1)S(1)} %get-tuple-element.33), channel_id=1, source_target_pairs={{0,3},{1,0},{2,1},{3,2},{4,7},{5,4},{6,5},{7,6},{8,11},{9,8},{10,9... | collective-permute-start | bytes 393224 | tf_op jit(solution)/shard_map/ppermute | solution.py:295
  64.1 1.5 %collective-permute-start.31 = (bf16[256,256]{1,0:T(8,128)(2,1)S(1)}, bf16[256,256]{1,0:T(8,128)(2,1)S(1)}, u32[]{:S(2)}, u32[]{:S(2)}) collective-permute-start(bf16[256,256]{1,0:T(8,128)(2,1)S(1)} %get-tuple-element.37.refs_4_.refs_8_), channel_id=1, source_target_pairs={{0,1},{1,2},{2,3},{3,0},{4,5},{5,6},{6,7},{7,4},{8,9},{9,10},{10,1... | collective-permute-start | bytes 393224 | tf_op jit(solution)/shard_map/ppermute | solution.py:295
  65.6 1.8 %collective-permute-start.32 = (bf16[256,256]{1,0:T(8,128)(2,1)S(1)}, bf16[256,256]{1,0:T(8,128)(2,1)S(1)}, u32[]{:S(2)}, u32[]{:S(2)}) collective-permute-start(bf16[256,256]{1,0:T(8,128)(2,1)S(1)} %get-tuple-element.37.refs_4_.refs_8_), channel_id=1, source_target_pairs={{0,3},{1,0},{2,1},{3,2},{4,7},{5,4},{6,5},{7,6},{8,11},{9,8},{10,9... | collective-permute-start | bytes 393224 | tf_op jit(solution)/shard_map/ppermute | solution.py:295
  67.4 1.7 %collective-permute-start.33 = (bf16[256,256]{1,0:T(8,128)(2,1)S(1)}, bf16[256,256]{1,0:T(8,128)(2,1)S(1)}, u32[]{:S(2)}, u32[]{:S(2)}) collective-permute-start(bf16[256,256]{1,0:T(8,128)(2,1)S(1)} %get-tuple-element.37.refs_4_.refs_8_), channel_id=1, source_target_pairs={{0,2},{1,3},{2,0},{3,1},{4,6},{5,7},{6,4},{7,5},{8,10},{9,11},{10,... | collective-permute-start | bytes 393224 | tf_op jit(solution)/shard_map/ppermute | solution.py:295
  69.1 2.2 %collective-permute-done.20.refs_3_ = bf16[256,256]{1,0:T(8,128)(2,1)S(1)} collective-permute-done((bf16[256,256]{1,0:T(8,128)(2,1)S(1)}, bf16[256,256]{1,0:T(8,128)(2,1)S(1)}, u32[]{:S(2)}, u32[]{:S(2)}) %collective-permute-start.20) | collective-permute-done | bytes 131104 | tf_op jit(solution)/shard_map/ppermute | solution.py:295
  71.4 2.2 %collective-permute-start.30 = (bf16[256,256]{1,0:T(8,128)(2,1)S(1)}, bf16[256,256]{1,0:T(8,128)(2,1)S(1)}, u32[]{:S(2)}, u32[]{:S(2)}) collective-permute-start(bf16[256,256]{1,0:T(8,128)(2,1)S(1)} %get-tuple-element.44), channel_id=1, source_target_pairs={{0,4},{1,5},{2,6},{3,7},{4,0},{5,1},{6,2},{7,3},{8,12},{9,13},{10,... | collective-permute-start | bytes 393224 | tf_op jit(solution)/shard_map/ppermute | solution.py:298
  74.5 2.6 %collective-permute-start.23 = (bf16[256,256]{1,0:T(8,128)(2,1)S(1)}, bf16[256,256]{1,0:T(8,128)(2,1)S(1)}, u32[]{:S(2)}, u32[]{:S(2)}) collective-permute-start(bf16[256,256]{1,0:T(8,128)(2,1)S(1)} %gate.14), channel_id=1, source_target_pairs={{0,3},{1,0},{2,1},{3,2},{4,7},{5,4},{6,5},{7,6},{8,11},{9,8},{10,9... | collective-permute-start | bytes 393224 | tf_op jit(solution)/shard_map/ppermute | solution.py:295
  77.2 1.5 %collective-permute-start.25 = (f32[1,1792]{1,0:T(1,128)S(1)}, f32[1,1792]{1,0:T(1,128)S(1)}, u32[]{:S(2)}, u32[]{:S(2)}) collective-permute-start(f32[1,1792]{1,0:T(1,128)S(1)} %get-tuple-element.36.refs_0_), channel_id=1, source_target_pairs={{0,128},{8,136},{16,144},{24,152},{32,160},{40,168},{48,176},{56,1... | collective-permute-start | bytes 21512 | tf_op jit(solution)/shard_map/ppermute | solution.py:291
  78.8 1.6 %collective-permute-start.34 = (bf16[256,256]{1,0:T(8,128)(2,1)S(1)}, bf16[256,256]{1,0:T(8,128)(2,1)S(1)}, u32[]{:S(2)}, u32[]{:S(2)}) collective-permute-start(bf16[256,256]{1,0:T(8,128)(2,1)S(1)} %merge_x.5.refs_2_), channel_id=1, source_target_pairs={{0,1},{1,2},{2,3},{3,0},{4,5},{5,6},{6,7},{7,4},{8,9},{9,10},{10,1... | collective-permute-start | bytes 393224 | tf_op jit(solution)/shard_map/ppermute | solution.py:295
  80.9 3.1 %collective-permute-start.35 = (bf16[256,256]{1,0:T(8,128)(2,1)S(1)}, bf16[256,256]{1,0:T(8,128)(2,1)S(1)}, u32[]{:S(2)}, u32[]{:S(2)}) collective-permute-start(bf16[256,256]{1,0:T(8,128)(2,1)S(1)} %merge_x.5.refs_2_), channel_id=1, source_target_pairs={{0,3},{1,0},{2,1},{3,2},{4,7},{5,4},{6,5},{7,6},{8,11},{9,8},{10,9... | collective-permute-start | bytes 393224 | tf_op jit(solution)/shard_map/ppermute | solution.py:295
  85.3 2.5 %collective-permute-start.26 = (bf16[256,256]{1,0:T(8,128)(2,1)S(1)}, bf16[256,256]{1,0:T(8,128)(2,1)S(1)}, u32[]{:S(2)}, u32[]{:S(2)}) collective-permute-start(bf16[256,256]{1,0:T(8,128)(2,1)S(1)} %get-tuple-element.42), channel_id=1, source_target_pairs={{0,4},{1,5},{2,6},{3,7},{4,0},{5,1},{6,2},{7,3},{8,12},{9,13},{10,... | collective-permute-start | bytes 393224 | tf_op jit(solution)/shard_map/ppermute | solution.py:298
  87.8 1.2 %backward.4.refs_6_ = f32[1792,256]{1,0:T(8,128)S(1)} custom-call(bf16[128,1792]{1,0:T(8,128)(2,1)S(1)} %copy-done.1, bf16[128,1792]{1,0:T(8,128)(2,1)S(1)} %collective-permute-done.refs_1_, bf16[128,1792]{1,0:T(8,128)(2,1)S(1)} %gate.8.refs_2_, bf16[128,1792]{1,0:T(8,128)(2,1)S(1)} %gate.9.refs_3_, ...), custom_call_target="tpu_custom_call" | custom-call | tf_op jit(solution)/shard_map/backward/pallas_call | solution.py:62
  89.1 1.5 %collective-permute-done.36.refs_5_ = bf16[256,256]{1,0:T(8,128)(2,1)S(1)} collective-permute-done((bf16[256,256]{1,0:T(8,128)(2,1)S(1)}, bf16[256,256]{1,0:T(8,128)(2,1)S(1)}, u32[]{:S(2)}, u32[]{:S(2)}) %collective-permute-start.36) | collective-permute-done | bytes 131104 | tf_op jit(solution)/shard_map/ppermute | solution.py:295
  90.6 1.5 %collective-permute-done.26.got.refs_7_ = bf16[256,256]{1,0:T(8,128)(2,1)S(1)} collective-permute-done((bf16[256,256]{1,0:T(8,128)(2,1)S(1)}, bf16[256,256]{1,0:T(8,128)(2,1)S(1)}, u32[]{:S(2)}, u32[]{:S(2)}) %collective-permute-start.26) | collective-permute-done | bytes 131104 | tf_op jit(solution)/shard_map/ppermute | solution.py:298
  92.1 1.2 %backward.5 = bf16[1792,256]{1,0:T(8,128)(2,1)S(1)} custom-call(bf16[512,1792]{1,0:T(8,128)(2,1)S(1)} %stack.1.refs_0_.refs_8_, bf16[512,1792]{1,0:T(8,128)(2,1)S(1)} %collective-permute-done.17.refs_1_.refs_9_, bf16[256,256]{1,0:T(8,128)(2,1)S(1)} %merge_x.5.refs_2_, bf16[256,256]{1,0:T(8,128)(2,1)S(1)} %collective-permute-done.34.refs_3_, ...), custom_call_target="tpu_custom_call" | custom-call | tf_op jit(solution)/shard_map/backward/pallas_call | solution.py:62
  93.3 1.5 %collective-permute-start.37 = (bf16[1792,256]{1,0:T(8,128)(2,1)S(1)}, bf16[1792,256]{1,0:T(8,128)(2,1)S(1)}, u32[]{:S(2)}, u32[]{:S(2)}) collective-permute-start(bf16[1792,256]{1,0:T(8,128)(2,1)S(1)} %backward.5), channel_id=1, source_target_pairs={{0,128},{8,136},{16,144},{24,152},{32,160},{40,168},{48,176},{56,1... | collective-permute-start | bytes 2752520 | tf_op jit(solution)/shard_map/ppermute | solution.py:291
  94.9 1.6 %collective-permute-start.27 = (bf16[512,256]{1,0:T(8,128)(2,1)S(1)}, bf16[512,256]{1,0:T(8,128)(2,1)S(1)}, u32[]{:S(2)}, u32[]{:S(2)}) collective-permute-start(bf16[512,256]{1,0:T(8,128)(2,1)S(1)} %merge_x.4.refs_10_), channel_id=1, source_target_pairs={{0,1},{1,2},{2,3},{3,0},{4,5},{5,6},{6,7},{7,4},{8,9},{9,10},{10,1... | collective-permute-start | bytes 786440 | tf_op jit(solution)/shard_map/ppermute | solution.py:295
  96.5 1.7 %collective-permute-start.28 = (bf16[512,256]{1,0:T(8,128)(2,1)S(1)}, bf16[512,256]{1,0:T(8,128)(2,1)S(1)}, u32[]{:S(2)}, u32[]{:S(2)}) collective-permute-start(bf16[512,256]{1,0:T(8,128)(2,1)S(1)} %merge_x.4.refs_10_), channel_id=1, source_target_pairs={{0,3},{1,0},{2,1},{3,2},{4,7},{5,4},{6,5},{7,6},{8,11},{9,8},{10,9... | collective-permute-start | bytes 786440 | tf_op jit(solution)/shard_map/ppermute | solution.py:295
  98.2 1.3 %collective-permute-start.29 = (bf16[512,256]{1,0:T(8,128)(2,1)S(1)}, bf16[512,256]{1,0:T(8,128)(2,1)S(1)}, u32[]{:S(2)}, u32[]{:S(2)}) collective-permute-start(bf16[512,256]{1,0:T(8,128)(2,1)S(1)} %merge_x.4.refs_10_), channel_id=1, source_target_pairs={{0,2},{1,3},{2,0},{3,1},{4,6},{5,7},{6,4},{7,5},{8,10},{9,11},{10,... | collective-permute-start | bytes 786440 | tf_op jit(solution)/shard_map/ppermute | solution.py:295
  99.5 3.0 %collective-permute-done.27.refs_11_ = bf16[512,256]{1,0:T(8,128)(2,1)S(1)} collective-permute-done((bf16[512,256]{1,0:T(8,128)(2,1)S(1)}, bf16[512,256]{1,0:T(8,128)(2,1)S(1)}, u32[]{:S(2)}, u32[]{:S(2)}) %collective-permute-start.27) | collective-permute-done | bytes 262176 | tf_op jit(solution)/shard_map/ppermute | solution.py:295
  102.9 3.2 %collective-permute-done.29.refs_13_ = bf16[512,256]{1,0:T(8,128)(2,1)S(1)} collective-permute-done((bf16[512,256]{1,0:T(8,128)(2,1)S(1)}, bf16[512,256]{1,0:T(8,128)(2,1)S(1)}, u32[]{:S(2)}, u32[]{:S(2)}) %collective-permute-start.29) | collective-permute-done | bytes 262176 | tf_op jit(solution)/shard_map/ppermute | solution.py:295
  106.1 2.2 %backward.3 = f32[1792,256]{1,0:T(8,128)S(1)} custom-call(bf16[128,1792]{1,0:T(8,128)(2,1)S(1)} %copy-done.1, bf16[128,1792]{1,0:T(8,128)(2,1)S(1)} %collective-permute-done.refs_1_, bf16[128,1792]{1,0:T(8,128)(2,1)S(1)} %gate.8.refs_2_, bf16[128,1792]{1,0:T(8,128)(2,1)S(1)} %gate.9.refs_3_, bf16[128,1792]{1,0:T(8,128)(2,1)S(1)} %collective-permute-done.4.refs_1_.refs_4_, ...), custom_call_target="tpu_custom_call" | custom-call | tf_op jit(solution)/shard_map/backward/pallas_call | solution.py:62
  108.3 3.7 %collective-permute-done.37 = bf16[1792,256]{1,0:T(8,128)(2,1)S(1)} collective-permute-done((bf16[1792,256]{1,0:T(8,128)(2,1)S(1)}, bf16[1792,256]{1,0:T(8,128)(2,1)S(1)}, u32[]{:S(2)}, u32[]{:S(2)}) %collective-permute-start.37) | collective-permute-done | bytes 917536 | tf_op jit(solution)/shard_map/ppermute | solution.py:291
  112.3 2.2 %fusion.2 = (bf16[1792,128]{1,0:T(8,128)(2,1)}, f32[1792,128]{1,0:T(8,128)}, f32[1792,128]{1,0:T(8,128)}) fusion(pred[1792,128]{1,0:T(8,128)(4,1)S(1)} %get-tuple-element.48, bf16[1792,128]{1,0:T(8,128)(2,1)S(1)} %copy-done, f32[1792,256]{1,0:T(8,128)S(1)} %convert_add_fusion, f32[1792,128]{1,0:T(8,128)S(1)} %copy-done.3, f32[1792]{0:T(1024)S(1)} %sqrt_reduce_fusion), kind=kLoop, calls=%fused_computation.6 | loop fusion | flops 3899392 | bytes 5741568 | tf_op jit(solution)/shard_map/convert_element_type | solution.py:358
  (60 shorter events, 6.3 us)
Async XLA Ops:
  0.6 2.6 %collective-permute-start = (bf16[128,1792]{1,0:T(8,128)(2,1)}, bf16[128,1792]{1,0:T(8,128)(2,1)S(1)}, u32[]{:S(2)}, u32[]{:S(2)}) collective-permute-start(bf16[128,1792]{1,0:T(8,128)(2,1)} %refs_0_.5), channel_id=1, source_target_pairs={{0,8},{8,0},{16,24},{24,16},{32,40},{40,32},{48,56},{56,48},{64,72... | collective-permute-start | bytes 1376264 | tf_op jit(solution)/shard_map/ppermute | solution.py:288
  0.7 12.6 %collective-permute-start.1 = (bf16[128,1792]{1,0:T(8,128)(2,1)}, bf16[128,1792]{1,0:T(8,128)(2,1)S(1)}, u32[]{:S(2)}, u32[]{:S(2)}) collective-permute-start(bf16[128,1792]{1,0:T(8,128)(2,1)} %refs_0_.5), channel_id=1, source_target_pairs={{0,16},{8,120},{16,32},{24,8},{32,48},{40,24},{48,64},{56,40},{64,... | collective-permute-start | bytes 1376264 | tf_op jit(solution)/shard_map/ppermute | solution.py:285
  2.7 10.8 %collective-permute-start.3 = (bf16[1792,128]{1,0:T(8,128)(2,1)}, bf16[1792,128]{1,0:T(8,128)(2,1)S(1)}, u32[]{:S(2)}, u32[]{:S(2)}) collective-permute-start(bf16[1792,128]{1,0:T(8,128)(2,1)} %refs_2_.1), channel_id=1, source_target_pairs={{0,128},{8,136},{16,144},{24,152},{32,160},{40,168},{48,176},{56,1... | collective-permute-start | bytes 1376264 | tf_op jit(solution)/shard_map/ppermute | solution.py:291
  3.3 15.0 %collective-permute-start.2 = (bf16[128,1792]{1,0:T(8,128)(2,1)S(1)}, bf16[128,1792]{1,0:T(8,128)(2,1)S(1)}, u32[]{:S(2)}, u32[]{:S(2)}) collective-permute-start(bf16[128,1792]{1,0:T(8,128)(2,1)S(1)} %collective-permute-done.refs_1_), channel_id=1, source_target_pairs={{0,16},{8,120},{16,32},{24,8},{32,48},{40,24},{48,64},{56,40},{64,... | collective-permute-start | bytes 1376264 | tf_op jit(solution)/shard_map/ppermute | solution.py:285
  6.7 16.3 %collective-permute-start.7 = (bf16[1792,128]{1,0:T(8,128)(2,1)S(1)}, bf16[1792,128]{1,0:T(8,128)(2,1)S(1)}, u32[]{:S(2)}, u32[]{:S(2)}) collective-permute-start(bf16[1792,128]{1,0:T(8,128)(2,1)S(1)} %get-tuple-element.47.refs_1_.refs_9_.refs_3_), channel_id=1, source_target_pairs={{0,128},{8,136},{16,144},{24,152},{32,160},{40,168},{48,176},{56,1... | collective-permute-start | bytes 1376264 | tf_op jit(solution)/shard_map/ppermute | solution.py:291
  13.3 13.1 %copy-start.2 = (bf16[512,128]{1,0:T(8,128)(2,1)S(1)}, bf16[512,128]{1,0:T(8,128)(2,1)}, u32[]{:S(2)}) copy-start(bf16[512,128]{1,0:T(8,128)(2,1)} %refs_6_.1) | copy-start | bytes 393220
  13.3 18.0 %copy-start = (bf16[1792,128]{1,0:T(8,128)(2,1)S(1)}, bf16[1792,128]{1,0:T(8,128)(2,1)}, u32[]{:S(2)}) copy-start(bf16[1792,128]{1,0:T(8,128)(2,1)} %refs_2_.1) | copy-start | bytes 1376260
  13.3 18.0 %copy-start.1 = (bf16[128,1792]{1,0:T(8,128)(2,1)S(1)}, bf16[128,1792]{1,0:T(8,128)(2,1)}, u32[]{:S(2)}) copy-start(bf16[128,1792]{1,0:T(8,128)(2,1)} %refs_0_.5) | copy-start | bytes 1376260
  13.3 9.6 %collective-permute-start.4 = (bf16[128,1792]{1,0:T(8,128)(2,1)S(1)}, bf16[128,1792]{1,0:T(8,128)(2,1)S(1)}, u32[]{:S(2)}, u32[]{:S(2)}) collective-permute-start(bf16[128,1792]{1,0:T(8,128)(2,1)S(1)} %gate.8.refs_2_), channel_id=1, source_target_pairs={{0,8},{8,0},{16,24},{24,16},{32,40},{40,32},{48,56},{56,48},{64,72... | collective-permute-start | bytes 1376264 | tf_op jit(solution)/shard_map/ppermute | solution.py:288
  13.4 9.8 %collective-permute-start.6 = (bf16[128,1792]{1,0:T(8,128)(2,1)S(1)}, bf16[128,1792]{1,0:T(8,128)(2,1)S(1)}, u32[]{:S(2)}, u32[]{:S(2)}) collective-permute-start(bf16[128,1792]{1,0:T(8,128)(2,1)S(1)} %gate.8.refs_2_), channel_id=1, source_target_pairs={{0,16},{8,120},{16,32},{24,8},{32,48},{40,24},{48,64},{56,40},{64,... | collective-permute-start | bytes 1376264 | tf_op jit(solution)/shard_map/ppermute | solution.py:285
  18.3 5.0 %collective-permute-start.5 = (bf16[128,1792]{1,0:T(8,128)(2,1)S(1)}, bf16[128,1792]{1,0:T(8,128)(2,1)S(1)}, u32[]{:S(2)}, u32[]{:S(2)}) collective-permute-start(bf16[128,1792]{1,0:T(8,128)(2,1)S(1)} %gate.9.refs_3_), channel_id=1, source_target_pairs={{0,8},{8,0},{16,24},{24,16},{32,40},{40,32},{48,56},{56,48},{64,72... | collective-permute-start | bytes 1376264 | tf_op jit(solution)/shard_map/ppermute | solution.py:288
  19.6 9.7 %collective-permute-start.9 = (bf16[128,1792]{1,0:T(8,128)(2,1)S(1)}, bf16[128,1792]{1,0:T(8,128)(2,1)S(1)}, u32[]{:S(2)}, u32[]{:S(2)}) collective-permute-start(bf16[128,1792]{1,0:T(8,128)(2,1)S(1)} %gate.9.refs_3_), channel_id=1, source_target_pairs={{0,16},{8,120},{16,32},{24,8},{32,48},{40,24},{48,64},{56,40},{64,... | collective-permute-start | bytes 1376264 | tf_op jit(solution)/shard_map/ppermute | solution.py:285
  23.2 8.2 %collective-permute-start.8 = (bf16[128,1792]{1,0:T(8,128)(2,1)S(1)}, bf16[128,1792]{1,0:T(8,128)(2,1)S(1)}, u32[]{:S(2)}, u32[]{:S(2)}) collective-permute-start(bf16[128,1792]{1,0:T(8,128)(2,1)S(1)} %gate.10.refs_6_), channel_id=1, source_target_pairs={{0,8},{8,0},{16,24},{24,16},{32,40},{40,32},{48,56},{56,48},{64,72... | collective-permute-start | bytes 1376264 | tf_op jit(solution)/shard_map/ppermute | solution.py:288
  26.4 10.4 %collective-permute-start.10 = (bf16[128,1792]{1,0:T(8,128)(2,1)S(1)}, bf16[128,1792]{1,0:T(8,128)(2,1)S(1)}, u32[]{:S(2)}, u32[]{:S(2)}) collective-permute-start(bf16[128,1792]{1,0:T(8,128)(2,1)S(1)} %gate.10.refs_6_), channel_id=1, source_target_pairs={{0,16},{8,120},{16,32},{24,8},{32,48},{40,24},{48,64},{56,40},{64,... | collective-permute-start | bytes 1376264 | tf_op jit(solution)/shard_map/ppermute | solution.py:285
  26.4 5.0 %collective-permute-start.11 = (bf16[512,128]{1,0:T(8,128)(2,1)S(1)}, bf16[512,128]{1,0:T(8,128)(2,1)S(1)}, u32[]{:S(2)}, u32[]{:S(2)}) collective-permute-start(bf16[512,128]{1,0:T(8,128)(2,1)S(1)} %copy-done.2), channel_id=1, source_target_pairs={{0,128},{8,136},{16,144},{24,152},{32,160},{40,168},{48,176},{56,1... | collective-permute-start | bytes 393224 | tf_op jit(solution)/shard_map/ppermute | solution.py:291
  29.3 23.5 %collective-permute-start.12 = (bf16[128,1792]{1,0:T(8,128)(2,1)S(1)}, bf16[128,1792]{1,0:T(8,128)(2,1)S(1)}, u32[]{:S(2)}, u32[]{:S(2)}) collective-permute-start(bf16[128,1792]{1,0:T(8,128)(2,1)S(1)} %collective-permute-done.9.refs_0_), channel_id=1, source_target_pairs={{0,16},{8,120},{16,32},{24,8},{32,48},{40,24},{48,64},{56,40},{64,... | collective-permute-start | bytes 1376264 | tf_op jit(solution)/shard_map/ppermute | solution.py:285
  36.8 16.0 %collective-permute-start.16 = (bf16[128,1792]{1,0:T(8,128)(2,1)S(1)}, bf16[128,1792]{1,0:T(8,128)(2,1)S(1)}, u32[]{:S(2)}, u32[]{:S(2)}) collective-permute-start(bf16[128,1792]{1,0:T(8,128)(2,1)S(1)} %gate.11.refs_1_), channel_id=1, source_target_pairs={{0,16},{8,120},{16,32},{24,8},{32,48},{40,24},{48,64},{56,40},{64,... | collective-permute-start | bytes 1376264 | tf_op jit(solution)/shard_map/ppermute | solution.py:285
  36.8 8.9 %collective-permute-start.13 = (bf16[256,512]{1,0:T(8,128)(2,1)S(1)}, bf16[256,512]{1,0:T(8,128)(2,1)S(1)}, u32[]{:S(2)}, u32[]{:S(2)}) collective-permute-start(bf16[256,512]{1,0:T(8,128)(2,1)S(1)} %get-tuple-element.26), channel_id=1, source_target_pairs={{0,1},{1,2},{2,3},{3,0},{4,5},{5,6},{6,7},{7,4},{8,9},{9,10},{10,1... | collective-permute-start | bytes 786440 | tf_op jit(solution)/shard_map/ppermute | solution.py:295
  38.4 8.1 %collective-permute-start.14 = (bf16[256,512]{1,0:T(8,128)(2,1)S(1)}, bf16[256,512]{1,0:T(8,128)(2,1)S(1)}, u32[]{:S(2)}, u32[]{:S(2)}) collective-permute-start(bf16[256,512]{1,0:T(8,128)(2,1)S(1)} %get-tuple-element.27), channel_id=1, source_target_pairs={{0,3},{1,0},{2,1},{3,2},{4,7},{5,4},{6,5},{7,6},{8,11},{9,8},{10,9... | collective-permute-start | bytes 786440 | tf_op jit(solution)/shard_map/ppermute | solution.py:295
  40.0 12.6 %collective-permute-start.15 = (bf16[256,512]{1,0:T(8,128)(2,1)S(1)}, bf16[256,512]{1,0:T(8,128)(2,1)S(1)}, u32[]{:S(2)}, u32[]{:S(2)}) collective-permute-start(bf16[256,512]{1,0:T(8,128)(2,1)S(1)} %get-tuple-element.28), channel_id=1, source_target_pairs={{0,2},{1,3},{2,0},{3,1},{4,6},{5,7},{6,4},{7,5},{8,10},{9,11},{10,... | collective-permute-start | bytes 786440 | tf_op jit(solution)/shard_map/ppermute | solution.py:295
  52.9 4.7 %collective-permute-start.17 = (bf16[512,1792]{1,0:T(8,128)(2,1)S(1)}, bf16[512,1792]{1,0:T(8,128)(2,1)S(1)}, u32[]{:S(2)}, u32[]{:S(2)}) collective-permute-start(bf16[512,1792]{1,0:T(8,128)(2,1)S(1)} %stack.1.refs_0_.refs_8_), channel_id=1, source_target_pairs={{0,8},{8,0},{16,24},{24,16},{32,40},{40,32},{48,56},{56,48},{64,72... | collective-permute-start | bytes 5505032 | tf_op jit(solution)/shard_map/ppermute | solution.py:288
  54.2 9.8 %collective-permute-start.21 = (bf16[256,512]{1,0:T(8,128)(2,1)S(1)}, bf16[256,512]{1,0:T(8,128)(2,1)S(1)}, u32[]{:S(2)}, u32[]{:S(2)}) collective-permute-start(bf16[256,512]{1,0:T(8,128)(2,1)S(1)} %get-tuple-element.35), channel_id=1, source_target_pairs={{0,4},{1,5},{2,6},{3,7},{4,0},{5,1},{6,2},{7,3},{8,12},{9,13},{10,... | collective-permute-start | bytes 786440 | tf_op jit(solution)/shard_map/ppermute | solution.py:298
  60.1 7.4 %collective-permute-start.18 = (bf16[256,256]{1,0:T(8,128)(2,1)S(1)}, bf16[256,256]{1,0:T(8,128)(2,1)S(1)}, u32[]{:S(2)}, u32[]{:S(2)}) collective-permute-start(bf16[256,256]{1,0:T(8,128)(2,1)S(1)} %get-tuple-element.32), channel_id=1, source_target_pairs={{0,1},{1,2},{2,3},{3,0},{4,5},{5,6},{6,7},{7,4},{8,9},{9,10},{10,1... | collective-permute-start | bytes 393224 | tf_op jit(solution)/shard_map/ppermute | solution.py:295
  61.6 7.5 %collective-permute-start.19 = (bf16[256,256]{1,0:T(8,128)(2,1)S(1)}, bf16[256,256]{1,0:T(8,128)(2,1)S(1)}, u32[]{:S(2)}, u32[]{:S(2)}) collective-permute-start(bf16[256,256]{1,0:T(8,128)(2,1)S(1)} %get-tuple-element.33), channel_id=1, source_target_pairs={{0,3},{1,0},{2,1},{3,2},{4,7},{5,4},{6,5},{7,6},{8,11},{9,8},{10,9... | collective-permute-start | bytes 393224 | tf_op jit(solution)/shard_map/ppermute | solution.py:295
  63.4 7.9 %collective-permute-start.20 = (bf16[256,256]{1,0:T(8,128)(2,1)S(1)}, bf16[256,256]{1,0:T(8,128)(2,1)S(1)}, u32[]{:S(2)}, u32[]{:S(2)}) collective-permute-start(bf16[256,256]{1,0:T(8,128)(2,1)S(1)} %get-tuple-element.34), channel_id=1, source_target_pairs={{0,2},{1,3},{2,0},{3,1},{4,6},{5,7},{6,4},{7,5},{8,10},{9,11},{10,... | collective-permute-start | bytes 393224 | tf_op jit(solution)/shard_map/ppermute | solution.py:295
  64.1 10.4 %collective-permute-start.31 = (bf16[256,256]{1,0:T(8,128)(2,1)S(1)}, bf16[256,256]{1,0:T(8,128)(2,1)S(1)}, u32[]{:S(2)}, u32[]{:S(2)}) collective-permute-start(bf16[256,256]{1,0:T(8,128)(2,1)S(1)} %get-tuple-element.37.refs_4_.refs_8_), channel_id=1, source_target_pairs={{0,1},{1,2},{2,3},{3,0},{4,5},{5,6},{6,7},{7,4},{8,9},{9,10},{10,1... | collective-permute-start | bytes 393224 | tf_op jit(solution)/shard_map/ppermute | solution.py:295
  65.6 11.6 %collective-permute-start.32 = (bf16[256,256]{1,0:T(8,128)(2,1)S(1)}, bf16[256,256]{1,0:T(8,128)(2,1)S(1)}, u32[]{:S(2)}, u32[]{:S(2)}) collective-permute-start(bf16[256,256]{1,0:T(8,128)(2,1)S(1)} %get-tuple-element.37.refs_4_.refs_8_), channel_id=1, source_target_pairs={{0,3},{1,0},{2,1},{3,2},{4,7},{5,4},{6,5},{7,6},{8,11},{9,8},{10,9... | collective-permute-start | bytes 393224 | tf_op jit(solution)/shard_map/ppermute | solution.py:295
  67.4 9.8 %collective-permute-start.33 = (bf16[256,256]{1,0:T(8,128)(2,1)S(1)}, bf16[256,256]{1,0:T(8,128)(2,1)S(1)}, u32[]{:S(2)}, u32[]{:S(2)}) collective-permute-start(bf16[256,256]{1,0:T(8,128)(2,1)S(1)} %get-tuple-element.37.refs_4_.refs_8_), channel_id=1, source_target_pairs={{0,2},{1,3},{2,0},{3,1},{4,6},{5,7},{6,4},{7,5},{8,10},{9,11},{10,... | collective-permute-start | bytes 393224 | tf_op jit(solution)/shard_map/ppermute | solution.py:295
  71.4 7.4 %collective-permute-start.30 = (bf16[256,256]{1,0:T(8,128)(2,1)S(1)}, bf16[256,256]{1,0:T(8,128)(2,1)S(1)}, u32[]{:S(2)}, u32[]{:S(2)}) collective-permute-start(bf16[256,256]{1,0:T(8,128)(2,1)S(1)} %get-tuple-element.44), channel_id=1, source_target_pairs={{0,4},{1,5},{2,6},{3,7},{4,0},{5,1},{6,2},{7,3},{8,12},{9,13},{10,... | collective-permute-start | bytes 393224 | tf_op jit(solution)/shard_map/ppermute | solution.py:298
  73.6 10.5 %collective-permute-start.24 = (bf16[256,256]{1,0:T(8,128)(2,1)S(1)}, bf16[256,256]{1,0:T(8,128)(2,1)S(1)}, u32[]{:S(2)}, u32[]{:S(2)}) collective-permute-start(bf16[256,256]{1,0:T(8,128)(2,1)S(1)} %gate.15), channel_id=1, source_target_pairs={{0,2},{1,3},{2,0},{3,1},{4,6},{5,7},{6,4},{7,5},{8,10},{9,11},{10,... | collective-permute-start | bytes 393224 | tf_op jit(solution)/shard_map/ppermute | solution.py:295
  74.5 10.7 %collective-permute-start.23 = (bf16[256,256]{1,0:T(8,128)(2,1)S(1)}, bf16[256,256]{1,0:T(8,128)(2,1)S(1)}, u32[]{:S(2)}, u32[]{:S(2)}) collective-permute-start(bf16[256,256]{1,0:T(8,128)(2,1)S(1)} %gate.14), channel_id=1, source_target_pairs={{0,3},{1,0},{2,1},{3,2},{4,7},{5,4},{6,5},{7,6},{8,11},{9,8},{10,9... | collective-permute-start | bytes 393224 | tf_op jit(solution)/shard_map/ppermute | solution.py:295
  77.2 8.0 %collective-permute-start.22 = (bf16[256,256]{1,0:T(8,128)(2,1)S(1)}, bf16[256,256]{1,0:T(8,128)(2,1)S(1)}, u32[]{:S(2)}, u32[]{:S(2)}) collective-permute-start(bf16[256,256]{1,0:T(8,128)(2,1)S(1)} %gate.13), channel_id=1, source_target_pairs={{0,1},{1,2},{2,3},{3,0},{4,5},{5,6},{6,7},{7,4},{8,9},{9,10},{10,1... | collective-permute-start | bytes 393224 | tf_op jit(solution)/shard_map/ppermute | solution.py:295
  77.2 3.7 %collective-permute-start.25 = (f32[1,1792]{1,0:T(1,128)S(1)}, f32[1,1792]{1,0:T(1,128)S(1)}, u32[]{:S(2)}, u32[]{:S(2)}) collective-permute-start(f32[1,1792]{1,0:T(1,128)S(1)} %get-tuple-element.36.refs_0_), channel_id=1, source_target_pairs={{0,128},{8,136},{16,144},{24,152},{32,160},{40,168},{48,176},{56,1... | collective-permute-start | bytes 21512 | tf_op jit(solution)/shard_map/ppermute | solution.py:291
  78.8 10.3 %collective-permute-start.34 = (bf16[256,256]{1,0:T(8,128)(2,1)S(1)}, bf16[256,256]{1,0:T(8,128)(2,1)S(1)}, u32[]{:S(2)}, u32[]{:S(2)}) collective-permute-start(bf16[256,256]{1,0:T(8,128)(2,1)S(1)} %merge_x.5.refs_2_), channel_id=1, source_target_pairs={{0,1},{1,2},{2,3},{3,0},{4,5},{5,6},{6,7},{7,4},{8,9},{9,10},{10,1... | collective-permute-start | bytes 393224 | tf_op jit(solution)/shard_map/ppermute | solution.py:295
  80.9 8.1 %collective-permute-start.35 = (bf16[256,256]{1,0:T(8,128)(2,1)S(1)}, bf16[256,256]{1,0:T(8,128)(2,1)S(1)}, u32[]{:S(2)}, u32[]{:S(2)}) collective-permute-start(bf16[256,256]{1,0:T(8,128)(2,1)S(1)} %merge_x.5.refs_2_), channel_id=1, source_target_pairs={{0,3},{1,0},{2,1},{3,2},{4,7},{5,4},{6,5},{7,6},{8,11},{9,8},{10,9... | collective-permute-start | bytes 393224 | tf_op jit(solution)/shard_map/ppermute | solution.py:295
  84.1 6.5 %collective-permute-start.36 = (bf16[256,256]{1,0:T(8,128)(2,1)S(1)}, bf16[256,256]{1,0:T(8,128)(2,1)S(1)}, u32[]{:S(2)}, u32[]{:S(2)}) collective-permute-start(bf16[256,256]{1,0:T(8,128)(2,1)S(1)} %merge_x.5.refs_2_), channel_id=1, source_target_pairs={{0,2},{1,3},{2,0},{3,1},{4,6},{5,7},{6,4},{7,5},{8,10},{9,11},{10,... | collective-permute-start | bytes 393224 | tf_op jit(solution)/shard_map/ppermute | solution.py:295
  85.3 6.8 %collective-permute-start.26 = (bf16[256,256]{1,0:T(8,128)(2,1)S(1)}, bf16[256,256]{1,0:T(8,128)(2,1)S(1)}, u32[]{:S(2)}, u32[]{:S(2)}) collective-permute-start(bf16[256,256]{1,0:T(8,128)(2,1)S(1)} %get-tuple-element.42), channel_id=1, source_target_pairs={{0,4},{1,5},{2,6},{3,7},{4,0},{5,1},{6,2},{7,3},{8,12},{9,13},{10,... | collective-permute-start | bytes 393224 | tf_op jit(solution)/shard_map/ppermute | solution.py:298
  93.3 18.6 %collective-permute-start.37 = (bf16[1792,256]{1,0:T(8,128)(2,1)S(1)}, bf16[1792,256]{1,0:T(8,128)(2,1)S(1)}, u32[]{:S(2)}, u32[]{:S(2)}) collective-permute-start(bf16[1792,256]{1,0:T(8,128)(2,1)S(1)} %backward.5), channel_id=1, source_target_pairs={{0,128},{8,136},{16,144},{24,152},{32,160},{40,168},{48,176},{56,1... | collective-permute-start | bytes 2752520 | tf_op jit(solution)/shard_map/ppermute | solution.py:291
  94.9 7.7 %collective-permute-start.27 = (bf16[512,256]{1,0:T(8,128)(2,1)S(1)}, bf16[512,256]{1,0:T(8,128)(2,1)S(1)}, u32[]{:S(2)}, u32[]{:S(2)}) collective-permute-start(bf16[512,256]{1,0:T(8,128)(2,1)S(1)} %merge_x.4.refs_10_), channel_id=1, source_target_pairs={{0,1},{1,2},{2,3},{3,0},{4,5},{5,6},{6,7},{7,4},{8,9},{9,10},{10,1... | collective-permute-start | bytes 786440 | tf_op jit(solution)/shard_map/ppermute | solution.py:295
  96.5 6.4 %collective-permute-start.28 = (bf16[512,256]{1,0:T(8,128)(2,1)S(1)}, bf16[512,256]{1,0:T(8,128)(2,1)S(1)}, u32[]{:S(2)}, u32[]{:S(2)}) collective-permute-start(bf16[512,256]{1,0:T(8,128)(2,1)S(1)} %merge_x.4.refs_10_), channel_id=1, source_target_pairs={{0,3},{1,0},{2,1},{3,2},{4,7},{5,4},{6,5},{7,6},{8,11},{9,8},{10,9... | collective-permute-start | bytes 786440 | tf_op jit(solution)/shard_map/ppermute | solution.py:295
  98.2 7.9 %collective-permute-start.29 = (bf16[512,256]{1,0:T(8,128)(2,1)S(1)}, bf16[512,256]{1,0:T(8,128)(2,1)S(1)}, u32[]{:S(2)}, u32[]{:S(2)}) collective-permute-start(bf16[512,256]{1,0:T(8,128)(2,1)S(1)} %merge_x.4.refs_10_), channel_id=1, source_target_pairs={{0,2},{1,3},{2,0},{3,1},{4,6},{5,7},{6,4},{7,5},{8,10},{9,11},{10,... | collective-permute-start | bytes 786440 | tf_op jit(solution)/shard_map/ppermute | solution.py:295
  108.3 4.0 %copy-start.3 = (f32[1792,128]{1,0:T(8,128)S(1)}, f32[1792,128]{1,0:T(8,128)}, u32[]{:S(2)}) copy-start(f32[1792,128]{1,0:T(8,128)} %param.9) | copy-start | bytes 2752516

commit v5 on v4

--- a/solution.py
+++ b/solution.py
@@ -340,9 +340,9 @@
     init = backward(early, [other0] + back0, f32)
     back1 = around([other1] * 3)
     got2 = around([gate(v, keep1) for v in ahead1[:3]])
-    keep2, send2 = merge_y(mine1, got2, 0, [squares_x])
+    keep2, send2 = merge_y(mine1, got2)
     sent2 = over(send2)
-    arrived = across(backward(late, [other1] + back1, bf16, 1, [init], [sent2]))
+    arrived = across(backward(late, [other1] + back1, bf16, 1, [init], [sent2, squares_x]))
     (own,) = merge_x(keep2, sent2, 1, [own0])
     grads = backward(early + late, [own] + around([own] * 3), f32, 2)
     colsq = squares + squares_x

time: 115 us -> 114 us (level)
  starting transfers between devices: 51.6 us -> 49.2 us
  waiting for transfers between devices: 48.1 us -> 50 us
    ppermute x18, waiting for transfers between devices: 20.9 us -> 22.6 us  [around(): return [lax.ppermute(v, 'mp', y_perm(dy)) for v, dy in zip(pieces, ahead)]]
    ppermute x18, starting transfers between devices: 28 us -> 26.4 us  [around(): return [lax.ppermute(v, 'mp', y_perm(dy)) for v, dy in zip(pieces, ahead)]]
  transfers between devices with their start and end apart: 38 -> 38, of which waited for: 20 -> 22; matrix products, arithmetic and copies ran while one was open for 1% -> 1% of each run, Pallas kernels for 7% -> 8%
where the time goes in v5:
time: 114 us
  waiting for transfers between devices  50 us (44%)
  starting transfers between devices  49.2 us (43%)
  Pallas kernels  9.92 us (9%)
  other arithmetic  4.06 us (4%)
    ppermute x18, starting transfers between devices, around(): return [lax.ppermute(v, 'mp', y_perm(dy)) for v, dy in zip(pieces, ahead)]  26.4 us
    ppermute x18, waiting for transfers between devices, around(): return [lax.ppermute(v, 'mp', y_perm(dy)) for v, dy in zip(pieces, ahead)]  22.6 us
    ppermute x7, waiting for transfers between devices, ring(): return lax.ppermute(value, 'dp', RING)  14.4 us
    ppermute x5, waiting for transfers between devices, across(): return lax.ppermute(value, 'dp', PAIR_X)  10.2 us
    pallas_call x12, Pallas kernels, vmem_call(): pl.pallas_call(kernel, out_shape=out_shape, in_specs=specs, out_specs=jax...  9.91 us
    ppermute x5, starting transfers between devices, across(): return lax.ppermute(value, 'dp', PAIR_X)  6.91 us
    ppermute x5, starting transfers between devices, swap(): return lax.ppermute(value, 'dp', PAIR_CORE)  6.05 us
    ppermute x3, starting transfers between devices, over(): return lax.ppermute(value, 'mp', PAIR_X_HI)  5.84 us
  transfers between devices with their start and end apart: 38, of which 22 were waited for; matrix products, arithmetic and copies ran while one was open for 1% of the time, Pallas kernels for 8%

profile of v5, /device:TPU:2, one launch (start us, length us, event | category | flops | bytes accessed | tf_op | source)
XLA Modules:
  0.0 114.1 jit_solution(7426093191988368229)
XLA Ops:
  0.7 2.0 %collective-permute-start.1 = (bf16[128,1792]{1,0:T(8,128)(2,1)}, bf16[128,1792]{1,0:T(8,128)(2,1)S(1)}, u32[]{:S(2)}, u32[]{:S(2)}) collective-permute-start(bf16[128,1792]{1,0:T(8,128)(2,1)} %refs_0_.5), channel_id=1, source_target_pairs={{0,16},{8,120},{16,32},{24,8},{32,48},{40,24},{48,64},{56,40},{64,... | collective-permute-start | bytes 1376264 | tf_op jit(solution)/shard_map/ppermute | solution.py:285
  3.3 1.9 %collective-permute-start.2 = (bf16[128,1792]{1,0:T(8,128)(2,1)S(1)}, bf16[128,1792]{1,0:T(8,128)(2,1)S(1)}, u32[]{:S(2)}, u32[]{:S(2)}) collective-permute-start(bf16[128,1792]{1,0:T(8,128)(2,1)S(1)} %collective-permute-done.refs_1_), channel_id=1, source_target_pairs={{0,16},{8,120},{16,32},{24,8},{32,48},{40,24},{48,64},{56,40},{64,... | collective-permute-start | bytes 1376264 | tf_op jit(solution)/shard_map/ppermute | solution.py:285
  5.2 1.5 %negate_select_fusion = (bf16[1792,128]{1,0:T(8,128)(2,1)S(1)}, pred[1792,128]{1,0:T(8,128)(4,1)S(1)}) fusion(bf16[1792,128]{1,0:T(8,128)(2,1)} %refs_2_.1, s32[1792,128]{1,0:T(8,128)} %param.8), kind=kLoop, calls=%fused_computation.12 | loop fusion | flops 688128 | bytes 2064384 | tf_op jit(solution)/shard_map/jit(_where)/select_n | solution.py:304
  6.7 1.6 %collective-permute-start.7 = (bf16[1792,128]{1,0:T(8,128)(2,1)S(1)}, bf16[1792,128]{1,0:T(8,128)(2,1)S(1)}, u32[]{:S(2)}, u32[]{:S(2)}) collective-permute-start(bf16[1792,128]{1,0:T(8,128)(2,1)S(1)} %get-tuple-element.47.refs_1_.refs_9_.refs_3_), channel_id=1, source_target_pairs={{0,128},{8,136},{16,144},{24,152},{32,160},{40,168},{48,176},{56,1... | collective-permute-start | bytes 1376264 | tf_op jit(solution)/shard_map/ppermute | solution.py:291
  8.3 5.0 %collective-permute-done.1.refs_0_ = bf16[128,1792]{1,0:T(8,128)(2,1)S(1)} collective-permute-done((bf16[128,1792]{1,0:T(8,128)(2,1)}, bf16[128,1792]{1,0:T(8,128)(2,1)S(1)}, u32[]{:S(2)}, u32[]{:S(2)}) %collective-permute-start.1) | collective-permute-done | bytes 458784 | tf_op jit(solution)/shard_map/ppermute | solution.py:285
  13.5 4.7 %collective-permute-done.2.refs_0_ = bf16[128,1792]{1,0:T(8,128)(2,1)S(1)} collective-permute-done((bf16[128,1792]{1,0:T(8,128)(2,1)S(1)}, bf16[128,1792]{1,0:T(8,128)(2,1)S(1)}, u32[]{:S(2)}, u32[]{:S(2)}) %collective-permute-start.2) | collective-permute-done | bytes 458784 | tf_op jit(solution)/shard_map/ppermute | solution.py:285
  18.3 1.4 %collective-permute-start.5 = (bf16[128,1792]{1,0:T(8,128)(2,1)S(1)}, bf16[128,1792]{1,0:T(8,128)(2,1)S(1)}, u32[]{:S(2)}, u32[]{:S(2)}) collective-permute-start(bf16[128,1792]{1,0:T(8,128)(2,1)S(1)} %gate.9.refs_3_), channel_id=1, source_target_pairs={{0,8},{8,0},{16,24},{24,16},{32,40},{40,32},{48,56},{56,48},{64,72... | collective-permute-start | bytes 1376264 | tf_op jit(solution)/shard_map/ppermute | solution.py:288
  19.6 3.4 %collective-permute-done.7.refs_3_.refs_11_.refs_5_ = bf16[1792,128]{1,0:T(8,128)(2,1)S(1)} collective-permute-done((bf16[1792,128]{1,0:T(8,128)(2,1)S(1)}, bf16[1792,128]{1,0:T(8,128)(2,1)S(1)}, u32[]{:S(2)}, u32[]{:S(2)}) %collective-permute-start.7) | collective-permute-done | bytes 458784 | tf_op jit(solution)/shard_map/ppermute | solution.py:291
  23.2 3.2 %collective-permute-start.8 = (bf16[128,1792]{1,0:T(8,128)(2,1)S(1)}, bf16[128,1792]{1,0:T(8,128)(2,1)S(1)}, u32[]{:S(2)}, u32[]{:S(2)}) collective-permute-start(bf16[128,1792]{1,0:T(8,128)(2,1)S(1)} %gate.10.refs_6_), channel_id=1, source_target_pairs={{0,8},{8,0},{16,24},{24,16},{32,40},{40,32},{48,56},{56,48},{64,72... | collective-permute-start | bytes 1376264 | tf_op jit(solution)/shard_map/ppermute | solution.py:288
  26.4 1.5 %collective-permute-start.11 = (bf16[512,128]{1,0:T(8,128)(2,1)S(1)}, bf16[512,128]{1,0:T(8,128)(2,1)S(1)}, u32[]{:S(2)}, u32[]{:S(2)}) collective-permute-start(bf16[512,128]{1,0:T(8,128)(2,1)S(1)} %copy-done.2), channel_id=1, source_target_pairs={{0,128},{8,136},{16,144},{24,152},{32,160},{40,168},{48,176},{56,1... | collective-permute-start | bytes 393224 | tf_op jit(solution)/shard_map/ppermute | solution.py:291
  27.9 1.4 %collective-permute-done.9.refs_0_ = bf16[128,1792]{1,0:T(8,128)(2,1)S(1)} collective-permute-done((bf16[128,1792]{1,0:T(8,128)(2,1)S(1)}, bf16[128,1792]{1,0:T(8,128)(2,1)S(1)}, u32[]{:S(2)}, u32[]{:S(2)}) %collective-permute-start.9) | collective-permute-done | bytes 458784 | tf_op jit(solution)/shard_map/ppermute | solution.py:285
  29.3 2.0 %collective-permute-done.11.refs_13_.refs_7_ = bf16[512,128]{1,0:T(8,128)(2,1)S(1)} collective-permute-done((bf16[512,128]{1,0:T(8,128)(2,1)S(1)}, bf16[512,128]{1,0:T(8,128)(2,1)S(1)}, u32[]{:S(2)}, u32[]{:S(2)}) %collective-permute-start.11) | collective-permute-done | bytes 131104 | tf_op jit(solution)/shard_map/ppermute | solution.py:291
  31.4 2.4 %forward.2 = (f32[256,512]{1,0:T(8,128)S(1)}, bf16[256,512]{1,0:T(8,128)(2,1)S(1)}, bf16[256,512]{1,0:T(8,128)(2,1)S(1)}, bf16[256,512]{1,0:T(8,128)(2,1)S(1)}, f32[1,1792]{1,0:T(1,128)S(1)}) custom-call(bf16[128,1792]{1,0:T(8,128)(2,1)S(1)} %copy-done.1, bf16[128,1792]{1,0:T(8,128)(2,1)S(1)} %collective-permute-done.refs_1_, ...), custom_call_target="tpu_custom_call" | custom-call | tf_op jit(solution)/shard_map/forward/pallas_call | solution.py:62
  33.8 3.0 %collective-permute-done.10.refs_0_ = bf16[128,1792]{1,0:T(8,128)(2,1)S(1)} collective-permute-done((bf16[128,1792]{1,0:T(8,128)(2,1)S(1)}, bf16[128,1792]{1,0:T(8,128)(2,1)S(1)}, u32[]{:S(2)}, u32[]{:S(2)}) %collective-permute-start.10) | collective-permute-done | bytes 458784 | tf_op jit(solution)/shard_map/ppermute | solution.py:285
  36.8 1.6 %collective-permute-start.13 = (bf16[256,512]{1,0:T(8,128)(2,1)S(1)}, bf16[256,512]{1,0:T(8,128)(2,1)S(1)}, u32[]{:S(2)}, u32[]{:S(2)}) collective-permute-start(bf16[256,512]{1,0:T(8,128)(2,1)S(1)} %get-tuple-element.26), channel_id=1, source_target_pairs={{0,1},{1,2},{2,3},{3,0},{4,5},{5,6},{6,7},{7,4},{8,9},{9,10},{10,1... | collective-permute-start | bytes 786440 | tf_op jit(solution)/shard_map/ppermute | solution.py:295
  38.4 1.7 %collective-permute-start.14 = (bf16[256,512]{1,0:T(8,128)(2,1)S(1)}, bf16[256,512]{1,0:T(8,128)(2,1)S(1)}, u32[]{:S(2)}, u32[]{:S(2)}) collective-permute-start(bf16[256,512]{1,0:T(8,128)(2,1)S(1)} %get-tuple-element.27), channel_id=1, source_target_pairs={{0,3},{1,0},{2,1},{3,2},{4,7},{5,4},{6,5},{7,6},{8,11},{9,8},{10,9... | collective-permute-start | bytes 786440 | tf_op jit(solution)/shard_map/ppermute | solution.py:295
  40.0 2.0 %collective-permute-start.15 = (bf16[256,512]{1,0:T(8,128)(2,1)S(1)}, bf16[256,512]{1,0:T(8,128)(2,1)S(1)}, u32[]{:S(2)}, u32[]{:S(2)}) collective-permute-start(bf16[256,512]{1,0:T(8,128)(2,1)S(1)} %get-tuple-element.28), channel_id=1, source_target_pairs={{0,2},{1,3},{2,0},{3,1},{4,6},{5,7},{6,4},{7,5},{8,10},{9,11},{10,... | collective-permute-start | bytes 786440 | tf_op jit(solution)/shard_map/ppermute | solution.py:295
  42.0 3.7 %collective-permute-done.13.refs_1_ = bf16[256,512]{1,0:T(8,128)(2,1)S(1)} collective-permute-done((bf16[256,512]{1,0:T(8,128)(2,1)S(1)}, bf16[256,512]{1,0:T(8,128)(2,1)S(1)}, u32[]{:S(2)}, u32[]{:S(2)}) %collective-permute-start.13) | collective-permute-done | bytes 262176 | tf_op jit(solution)/shard_map/ppermute | solution.py:295
  46.5 6.2 %collective-permute-done.15.refs_3_ = bf16[256,512]{1,0:T(8,128)(2,1)S(1)} collective-permute-done((bf16[256,512]{1,0:T(8,128)(2,1)S(1)}, bf16[256,512]{1,0:T(8,128)(2,1)S(1)}, u32[]{:S(2)}, u32[]{:S(2)}) %collective-permute-start.15) | collective-permute-done | bytes 262176 | tf_op jit(solution)/shard_map/ppermute | solution.py:295
  52.9 1.3 %collective-permute-start.17 = (bf16[512,1792]{1,0:T(8,128)(2,1)S(1)}, bf16[512,1792]{1,0:T(8,128)(2,1)S(1)}, u32[]{:S(2)}, u32[]{:S(2)}) collective-permute-start(bf16[512,1792]{1,0:T(8,128)(2,1)S(1)} %stack.1.refs_0_.refs_8_), channel_id=1, source_target_pairs={{0,8},{8,0},{16,24},{24,16},{32,40},{40,32},{48,56},{56,48},{64,72... | collective-permute-start | bytes 5505032 | tf_op jit(solution)/shard_map/ppermute | solution.py:288
  54.2 2.1 %collective-permute-start.21 = (bf16[256,512]{1,0:T(8,128)(2,1)S(1)}, bf16[256,512]{1,0:T(8,128)(2,1)S(1)}, u32[]{:S(2)}, u32[]{:S(2)}) collective-permute-start(bf16[256,512]{1,0:T(8,128)(2,1)S(1)} %get-tuple-element.35), channel_id=1, source_target_pairs={{0,4},{1,5},{2,6},{3,7},{4,0},{5,1},{6,2},{7,3},{8,12},{9,13},{10,... | collective-permute-start | bytes 786440 | tf_op jit(solution)/shard_map/ppermute | solution.py:298
  56.4 1.3 %collective-permute-done.17.refs_1_.refs_9_ = bf16[512,1792]{1,0:T(8,128)(2,1)S(1)} collective-permute-done((bf16[512,1792]{1,0:T(8,128)(2,1)S(1)}, bf16[512,1792]{1,0:T(8,128)(2,1)S(1)}, u32[]{:S(2)}, u32[]{:S(2)}) %collective-permute-start.17) | collective-permute-done | bytes 1835040 | tf_op jit(solution)/shard_map/ppermute | solution.py:288
  57.7 2.4 %forward.3 = (f32[256,512]{1,0:T(8,128)S(1)}, bf16[256,256]{1,0:T(8,128)(2,1)S(1)}, bf16[256,256]{1,0:T(8,128)(2,1)S(1)}, bf16[256,256]{1,0:T(8,128)(2,1)S(1)}, ...) custom-call(bf16[512,1792]{1,0:T(8,128)(2,1)S(1)} %stack.1.refs_0_.r, ...), custom_call_target="tpu_custom_call" | custom-call | tf_op jit(solution)/shard_map/forward/pallas_call | solution.py:62
  60.1 1.5 %collective-permute-start.18 = (bf16[256,256]{1,0:T(8,128)(2,1)S(1)}, bf16[256,256]{1,0:T(8,128)(2,1)S(1)}, u32[]{:S(2)}, u32[]{:S(2)}) collective-permute-start(bf16[256,256]{1,0:T(8,128)(2,1)S(1)} %get-tuple-element.32), channel_id=1, source_target_pairs={{0,1},{1,2},{2,3},{3,0},{4,5},{5,6},{6,7},{7,4},{8,9},{9,10},{10,1... | collective-permute-start | bytes 393224 | tf_op jit(solution)/shard_map/ppermute | solution.py:295
  61.6 1.8 %collective-permute-start.19 = (bf16[256,256]{1,0:T(8,128)(2,1)S(1)}, bf16[256,256]{1,0:T(8,128)(2,1)S(1)}, u32[]{:S(2)}, u32[]{:S(2)}) collective-permute-start(bf16[256,256]{1,0:T(8,128)(2,1)S(1)} %get-tuple-element.33), channel_id=1, source_target_pairs={{0,3},{1,0},{2,1},{3,2},{4,7},{5,4},{6,5},{7,6},{8,11},{9,8},{10,9... | collective-permute-start | bytes 393224 | tf_op jit(solution)/shard_map/ppermute | solution.py:295
  64.1 1.5 %collective-permute-start.30 = (bf16[256,256]{1,0:T(8,128)(2,1)S(1)}, bf16[256,256]{1,0:T(8,128)(2,1)S(1)}, u32[]{:S(2)}, u32[]{:S(2)}) collective-permute-start(bf16[256,256]{1,0:T(8,128)(2,1)S(1)} %get-tuple-element.37.refs_4_.refs_8_), channel_id=1, source_target_pairs={{0,1},{1,2},{2,3},{3,0},{4,5},{5,6},{6,7},{7,4},{8,9},{9,10},{10,1... | collective-permute-start | bytes 393224 | tf_op jit(solution)/shard_map/ppermute | solution.py:295
  65.6 1.8 %collective-permute-start.31 = (bf16[256,256]{1,0:T(8,128)(2,1)S(1)}, bf16[256,256]{1,0:T(8,128)(2,1)S(1)}, u32[]{:S(2)}, u32[]{:S(2)}) collective-permute-start(bf16[256,256]{1,0:T(8,128)(2,1)S(1)} %get-tuple-element.37.refs_4_.refs_8_), channel_id=1, source_target_pairs={{0,3},{1,0},{2,1},{3,2},{4,7},{5,4},{6,5},{7,6},{8,11},{9,8},{10,9... | collective-permute-start | bytes 393224 | tf_op jit(solution)/shard_map/ppermute | solution.py:295
  67.4 1.7 %collective-permute-start.32 = (bf16[256,256]{1,0:T(8,128)(2,1)S(1)}, bf16[256,256]{1,0:T(8,128)(2,1)S(1)}, u32[]{:S(2)}, u32[]{:S(2)}) collective-permute-start(bf16[256,256]{1,0:T(8,128)(2,1)S(1)} %get-tuple-element.37.refs_4_.refs_8_), channel_id=1, source_target_pairs={{0,2},{1,3},{2,0},{3,1},{4,6},{5,7},{6,4},{7,5},{8,10},{9,11},{10,... | collective-permute-start | bytes 393224 | tf_op jit(solution)/shard_map/ppermute | solution.py:295
  69.1 2.2 %collective-permute-done.20.refs_3_ = bf16[256,256]{1,0:T(8,128)(2,1)S(1)} collective-permute-done((bf16[256,256]{1,0:T(8,128)(2,1)S(1)}, bf16[256,256]{1,0:T(8,128)(2,1)S(1)}, u32[]{:S(2)}, u32[]{:S(2)}) %collective-permute-start.20) | collective-permute-done | bytes 131104 | tf_op jit(solution)/shard_map/ppermute | solution.py:295
  71.4 2.2 %collective-permute-start.29 = (bf16[256,256]{1,0:T(8,128)(2,1)S(1)}, bf16[256,256]{1,0:T(8,128)(2,1)S(1)}, u32[]{:S(2)}, u32[]{:S(2)}) collective-permute-start(bf16[256,256]{1,0:T(8,128)(2,1)S(1)} %get-tuple-element.44), channel_id=1, source_target_pairs={{0,4},{1,5},{2,6},{3,7},{4,0},{5,1},{6,2},{7,3},{8,12},{9,13},{10,... | collective-permute-start | bytes 393224 | tf_op jit(solution)/shard_map/ppermute | solution.py:298
  74.5 2.6 %collective-permute-start.23 = (bf16[256,256]{1,0:T(8,128)(2,1)S(1)}, bf16[256,256]{1,0:T(8,128)(2,1)S(1)}, u32[]{:S(2)}, u32[]{:S(2)}) collective-permute-start(bf16[256,256]{1,0:T(8,128)(2,1)S(1)} %gate.14), channel_id=1, source_target_pairs={{0,3},{1,0},{2,1},{3,2},{4,7},{5,4},{6,5},{7,6},{8,11},{9,8},{10,9... | collective-permute-start | bytes 393224 | tf_op jit(solution)/shard_map/ppermute | solution.py:295
  78.0 1.0 collective-permute-start.33
  79.0 2.3 %collective-permute-start.34 = (bf16[256,256]{1,0:T(8,128)(2,1)S(1)}, bf16[256,256]{1,0:T(8,128)(2,1)S(1)}, u32[]{:S(2)}, u32[]{:S(2)}) collective-permute-start(bf16[256,256]{1,0:T(8,128)(2,1)S(1)} %merge_x.5.refs_2_), channel_id=1, source_target_pairs={{0,3},{1,0},{2,1},{3,2},{4,7},{5,4},{6,5},{7,6},{8,11},{9,8},{10,9... | collective-permute-start | bytes 393224 | tf_op jit(solution)/shard_map/ppermute | solution.py:295
  81.4 2.3 %collective-permute-start.35 = (bf16[256,256]{1,0:T(8,128)(2,1)S(1)}, bf16[256,256]{1,0:T(8,128)(2,1)S(1)}, u32[]{:S(2)}, u32[]{:S(2)}) collective-permute-start(bf16[256,256]{1,0:T(8,128)(2,1)S(1)} %merge_x.5.refs_2_), channel_id=1, source_target_pairs={{0,2},{1,3},{2,0},{3,1},{4,6},{5,7},{6,4},{7,5},{8,10},{9,11},{10,... | collective-permute-start | bytes 393224 | tf_op jit(solution)/shard_map/ppermute | solution.py:295
  83.7 1.9 %collective-permute-done.22.refs_1_ = bf16[256,256]{1,0:T(8,128)(2,1)S(1)} collective-permute-done((bf16[256,256]{1,0:T(8,128)(2,1)S(1)}, bf16[256,256]{1,0:T(8,128)(2,1)S(1)}, u32[]{:S(2)}, u32[]{:S(2)}) %collective-permute-start.22) | collective-permute-done | bytes 131104 | tf_op jit(solution)/shard_map/ppermute | solution.py:295
  85.6 1.5 %collective-permute-start.25 = (bf16[256,256]{1,0:T(8,128)(2,1)S(1)}, bf16[256,256]{1,0:T(8,128)(2,1)S(1)}, u32[]{:S(2)}, u32[]{:S(2)}) collective-permute-start(bf16[256,256]{1,0:T(8,128)(2,1)S(1)} %get-tuple-element.42), channel_id=1, source_target_pairs={{0,4},{1,5},{2,6},{3,7},{4,0},{5,1},{6,2},{7,3},{8,12},{9,13},{10,... | collective-permute-start | bytes 393224 | tf_op jit(solution)/shard_map/ppermute | solution.py:298
  87.1 1.8 %collective-permute-start.36 = (f32[1,1792]{1,0:T(1,128)S(1)}, f32[1,1792]{1,0:T(1,128)S(1)}, u32[]{:S(2)}, u32[]{:S(2)}) collective-permute-start(f32[1,1792]{1,0:T(1,128)S(1)} %get-tuple-element.36.refs_0_), channel_id=1, source_target_pairs={{0,128},{8,136},{16,144},{24,152},{32,160},{40,168},{48,176},{56,1... | collective-permute-start | bytes 21512 | tf_op jit(solution)/shard_map/ppermute | solution.py:291
  88.9 1.2 %backward.4.refs_6_ = f32[1792,256]{1,0:T(8,128)S(1)} custom-call(bf16[128,1792]{1,0:T(8,128)(2,1)S(1)} %copy-done.1, bf16[128,1792]{1,0:T(8,128)(2,1)S(1)} %collective-permute-done.refs_1_, bf16[128,1792]{1,0:T(8,128)(2,1)S(1)} %gate.8.refs_2_, bf16[128,1792]{1,0:T(8,128)(2,1)S(1)} %gate.9.refs_3_, ...), custom_call_target="tpu_custom_call" | custom-call | tf_op jit(solution)/shard_map/backward/pallas_call | solution.py:62
  90.1 2.7 %collective-permute-done.36.refs_8_ = f32[1,1792]{1,0:T(1,128)S(1)} collective-permute-done((f32[1,1792]{1,0:T(1,128)S(1)}, f32[1,1792]{1,0:T(1,128)S(1)}, u32[]{:S(2)}, u32[]{:S(2)}) %collective-permute-start.36) | collective-permute-done | bytes 7200 | tf_op jit(solution)/shard_map/ppermute | solution.py:291
  93.3 1.2 %backward.5 = bf16[1792,256]{1,0:T(8,128)(2,1)S(1)} custom-call(bf16[512,1792]{1,0:T(8,128)(2,1)S(1)} %stack.1.refs_0_.refs_8_, bf16[512,1792]{1,0:T(8,128)(2,1)S(1)} %collective-permute-done.17.refs_1_.refs_9_, bf16[256,256]{1,0:T(8,128)(2,1)S(1)} %merge_x.5.refs_2_, bf16[256,256]{1,0:T(8,128)(2,1)S(1)} %collective-permute-done.33.refs_3_, ...), custom_call_target="tpu_custom_call" | custom-call | tf_op jit(solution)/shard_map/backward/pallas_call | solution.py:62
  94.5 1.5 %collective-permute-start.37 = (bf16[1792,256]{1,0:T(8,128)(2,1)S(1)}, bf16[1792,256]{1,0:T(8,128)(2,1)S(1)}, u32[]{:S(2)}, u32[]{:S(2)}) collective-permute-start(bf16[1792,256]{1,0:T(8,128)(2,1)S(1)} %backward.5), channel_id=1, source_target_pairs={{0,128},{8,136},{16,144},{24,152},{32,160},{40,168},{48,176},{56,1... | collective-permute-start | bytes 2752520 | tf_op jit(solution)/shard_map/ppermute | solution.py:291
  96.1 3.2 %collective-permute-start.27 = (bf16[512,256]{1,0:T(8,128)(2,1)S(1)}, bf16[512,256]{1,0:T(8,128)(2,1)S(1)}, u32[]{:S(2)}, u32[]{:S(2)}) collective-permute-start(bf16[512,256]{1,0:T(8,128)(2,1)S(1)} %merge_x.4.refs_10_), channel_id=1, source_target_pairs={{0,3},{1,0},{2,1},{3,2},{4,7},{5,4},{6,5},{7,6},{8,11},{9,8},{10,9... | collective-permute-start | bytes 786440 | tf_op jit(solution)/shard_map/ppermute | solution.py:295
  99.4 4.3 %collective-permute-done.26.refs_11_ = bf16[512,256]{1,0:T(8,128)(2,1)S(1)} collective-permute-done((bf16[512,256]{1,0:T(8,128)(2,1)S(1)}, bf16[512,256]{1,0:T(8,128)(2,1)S(1)}, u32[]{:S(2)}, u32[]{:S(2)}) %collective-permute-start.26) | collective-permute-done | bytes 262176 | tf_op jit(solution)/shard_map/ppermute | solution.py:295
  103.7 2.4 %collective-permute-done.27.refs_12_ = bf16[512,256]{1,0:T(8,128)(2,1)S(1)} collective-permute-done((bf16[512,256]{1,0:T(8,128)(2,1)S(1)}, bf16[512,256]{1,0:T(8,128)(2,1)S(1)}, u32[]{:S(2)}, u32[]{:S(2)}) %collective-permute-start.27) | collective-permute-done | bytes 262176 | tf_op jit(solution)/shard_map/ppermute | solution.py:295
  106.1 1.2 %collective-permute-done.28.refs_13_ = bf16[512,256]{1,0:T(8,128)(2,1)S(1)} collective-permute-done((bf16[512,256]{1,0:T(8,128)(2,1)S(1)}, bf16[512,256]{1,0:T(8,128)(2,1)S(1)}, u32[]{:S(2)}, u32[]{:S(2)}) %collective-permute-start.28) | collective-permute-done | bytes 262176 | tf_op jit(solution)/shard_map/ppermute | solution.py:295
  107.2 2.2 %backward.3 = f32[1792,256]{1,0:T(8,128)S(1)} custom-call(bf16[128,1792]{1,0:T(8,128)(2,1)S(1)} %copy-done.1, bf16[128,1792]{1,0:T(8,128)(2,1)S(1)} %collective-permute-done.refs_1_, bf16[128,1792]{1,0:T(8,128)(2,1)S(1)} %gate.8.refs_2_, bf16[128,1792]{1,0:T(8,128)(2,1)S(1)} %gate.9.refs_3_, bf16[128,1792]{1,0:T(8,128)(2,1)S(1)} %collective-permute-done.4.refs_1_.refs_4_, ...), custom_call_target="tpu_custom_call" | custom-call | tf_op jit(solution)/shard_map/backward/pallas_call | solution.py:62
  109.5 2.1 %collective-permute-done.37 = bf16[1792,256]{1,0:T(8,128)(2,1)S(1)} collective-permute-done((bf16[1792,256]{1,0:T(8,128)(2,1)S(1)}, bf16[1792,256]{1,0:T(8,128)(2,1)S(1)}, u32[]{:S(2)}, u32[]{:S(2)}) %collective-permute-start.37) | collective-permute-done | bytes 917536 | tf_op jit(solution)/shard_map/ppermute | solution.py:291
  111.9 2.2 %fusion.2 = (bf16[1792,128]{1,0:T(8,128)(2,1)}, f32[1792,128]{1,0:T(8,128)}, f32[1792,128]{1,0:T(8,128)}) fusion(pred[1792,128]{1,0:T(8,128)(4,1)S(1)} %get-tuple-element.48, bf16[1792,128]{1,0:T(8,128)(2,1)S(1)} %copy-done, f32[1792,256]{1,0:T(8,128)S(1)} %convert_add_fusion, f32[1792,128]{1,0:T(8,128)S(1)} %copy-done.3, f32[1792]{0:T(1024)S(1)} %sqrt_reduce_fusion), kind=kLoop, calls=%fused_computation.6 | loop fusion | flops 3899392 | bytes 5741568 | tf_op jit(solution)/shard_map/convert_element_type | solution.py:358
  (60 shorter events, 5.6 us)
Async XLA Ops:
  0.6 2.6 %collective-permute-start = (bf16[128,1792]{1,0:T(8,128)(2,1)}, bf16[128,1792]{1,0:T(8,128)(2,1)S(1)}, u32[]{:S(2)}, u32[]{:S(2)}) collective-permute-start(bf16[128,1792]{1,0:T(8,128)(2,1)} %refs_0_.5), channel_id=1, source_target_pairs={{0,8},{8,0},{16,24},{24,16},{32,40},{40,32},{48,56},{56,48},{64,72... | collective-permute-start | bytes 1376264 | tf_op jit(solution)/shard_map/ppermute | solution.py:288
  0.7 12.6 %collective-permute-start.1 = (bf16[128,1792]{1,0:T(8,128)(2,1)}, bf16[128,1792]{1,0:T(8,128)(2,1)S(1)}, u32[]{:S(2)}, u32[]{:S(2)}) collective-permute-start(bf16[128,1792]{1,0:T(8,128)(2,1)} %refs_0_.5), channel_id=1, source_target_pairs={{0,16},{8,120},{16,32},{24,8},{32,48},{40,24},{48,64},{56,40},{64,... | collective-permute-start | bytes 1376264 | tf_op jit(solution)/shard_map/ppermute | solution.py:285
  2.7 10.8 %collective-permute-start.3 = (bf16[1792,128]{1,0:T(8,128)(2,1)}, bf16[1792,128]{1,0:T(8,128)(2,1)S(1)}, u32[]{:S(2)}, u32[]{:S(2)}) collective-permute-start(bf16[1792,128]{1,0:T(8,128)(2,1)} %refs_2_.1), channel_id=1, source_target_pairs={{0,128},{8,136},{16,144},{24,152},{32,160},{40,168},{48,176},{56,1... | collective-permute-start | bytes 1376264 | tf_op jit(solution)/shard_map/ppermute | solution.py:291
  3.3 15.0 %collective-permute-start.2 = (bf16[128,1792]{1,0:T(8,128)(2,1)S(1)}, bf16[128,1792]{1,0:T(8,128)(2,1)S(1)}, u32[]{:S(2)}, u32[]{:S(2)}) collective-permute-start(bf16[128,1792]{1,0:T(8,128)(2,1)S(1)} %collective-permute-done.refs_1_), channel_id=1, source_target_pairs={{0,16},{8,120},{16,32},{24,8},{32,48},{40,24},{48,64},{56,40},{64,... | collective-permute-start | bytes 1376264 | tf_op jit(solution)/shard_map/ppermute | solution.py:285
  6.7 16.3 %collective-permute-start.7 = (bf16[1792,128]{1,0:T(8,128)(2,1)S(1)}, bf16[1792,128]{1,0:T(8,128)(2,1)S(1)}, u32[]{:S(2)}, u32[]{:S(2)}) collective-permute-start(bf16[1792,128]{1,0:T(8,128)(2,1)S(1)} %get-tuple-element.47.refs_1_.refs_9_.refs_3_), channel_id=1, source_target_pairs={{0,128},{8,136},{16,144},{24,152},{32,160},{40,168},{48,176},{56,1... | collective-permute-start | bytes 1376264 | tf_op jit(solution)/shard_map/ppermute | solution.py:291
  13.3 13.1 %copy-start.2 = (bf16[512,128]{1,0:T(8,128)(2,1)S(1)}, bf16[512,128]{1,0:T(8,128)(2,1)}, u32[]{:S(2)}) copy-start(bf16[512,128]{1,0:T(8,128)(2,1)} %refs_6_.1) | copy-start | bytes 393220
  13.3 18.0 %copy-start = (bf16[1792,128]{1,0:T(8,128)(2,1)S(1)}, bf16[1792,128]{1,0:T(8,128)(2,1)}, u32[]{:S(2)}) copy-start(bf16[1792,128]{1,0:T(8,128)(2,1)} %refs_2_.1) | copy-start | bytes 1376260
  13.3 18.0 %copy-start.1 = (bf16[128,1792]{1,0:T(8,128)(2,1)S(1)}, bf16[128,1792]{1,0:T(8,128)(2,1)}, u32[]{:S(2)}) copy-start(bf16[128,1792]{1,0:T(8,128)(2,1)} %refs_0_.5) | copy-start | bytes 1376260
  13.3 9.6 %collective-permute-start.4 = (bf16[128,1792]{1,0:T(8,128)(2,1)S(1)}, bf16[128,1792]{1,0:T(8,128)(2,1)S(1)}, u32[]{:S(2)}, u32[]{:S(2)}) collective-permute-start(bf16[128,1792]{1,0:T(8,128)(2,1)S(1)} %gate.8.refs_2_), channel_id=1, source_target_pairs={{0,8},{8,0},{16,24},{24,16},{32,40},{40,32},{48,56},{56,48},{64,72... | collective-permute-start | bytes 1376264 | tf_op jit(solution)/shard_map/ppermute | solution.py:288
  13.4 9.8 %collective-permute-start.6 = (bf16[128,1792]{1,0:T(8,128)(2,1)S(1)}, bf16[128,1792]{1,0:T(8,128)(2,1)S(1)}, u32[]{:S(2)}, u32[]{:S(2)}) collective-permute-start(bf16[128,1792]{1,0:T(8,128)(2,1)S(1)} %gate.8.refs_2_), channel_id=1, source_target_pairs={{0,16},{8,120},{16,32},{24,8},{32,48},{40,24},{48,64},{56,40},{64,... | collective-permute-start | bytes 1376264 | tf_op jit(solution)/shard_map/ppermute | solution.py:285
  18.3 5.0 %collective-permute-start.5 = (bf16[128,1792]{1,0:T(8,128)(2,1)S(1)}, bf16[128,1792]{1,0:T(8,128)(2,1)S(1)}, u32[]{:S(2)}, u32[]{:S(2)}) collective-permute-start(bf16[128,1792]{1,0:T(8,128)(2,1)S(1)} %gate.9.refs_3_), channel_id=1, source_target_pairs={{0,8},{8,0},{16,24},{24,16},{32,40},{40,32},{48,56},{56,48},{64,72... | collective-permute-start | bytes 1376264 | tf_op jit(solution)/shard_map/ppermute | solution.py:288
  19.6 9.7 %collective-permute-start.9 = (bf16[128,1792]{1,0:T(8,128)(2,1)S(1)}, bf16[128,1792]{1,0:T(8,128)(2,1)S(1)}, u32[]{:S(2)}, u32[]{:S(2)}) collective-permute-start(bf16[128,1792]{1,0:T(8,128)(2,1)S(1)} %gate.9.refs_3_), channel_id=1, source_target_pairs={{0,16},{8,120},{16,32},{24,8},{32,48},{40,24},{48,64},{56,40},{64,... | collective-permute-start | bytes 1376264 | tf_op jit(solution)/shard_map/ppermute | solution.py:285
  23.2 8.2 %collective-permute-start.8 = (bf16[128,1792]{1,0:T(8,128)(2,1)S(1)}, bf16[128,1792]{1,0:T(8,128)(2,1)S(1)}, u32[]{:S(2)}, u32[]{:S(2)}) collective-permute-start(bf16[128,1792]{1,0:T(8,128)(2,1)S(1)} %gate.10.refs_6_), channel_id=1, source_target_pairs={{0,8},{8,0},{16,24},{24,16},{32,40},{40,32},{48,56},{56,48},{64,72... | collective-permute-start | bytes 1376264 | tf_op jit(solution)/shard_map/ppermute | solution.py:288
  26.4 10.4 %collective-permute-start.10 = (bf16[128,1792]{1,0:T(8,128)(2,1)S(1)}, bf16[128,1792]{1,0:T(8,128)(2,1)S(1)}, u32[]{:S(2)}, u32[]{:S(2)}) collective-permute-start(bf16[128,1792]{1,0:T(8,128)(2,1)S(1)} %gate.10.refs_6_), channel_id=1, source_target_pairs={{0,16},{8,120},{16,32},{24,8},{32,48},{40,24},{48,64},{56,40},{64,... | collective-permute-start | bytes 1376264 | tf_op jit(solution)/shard_map/ppermute | solution.py:285
  26.4 5.0 %collective-permute-start.11 = (bf16[512,128]{1,0:T(8,128)(2,1)S(1)}, bf16[512,128]{1,0:T(8,128)(2,1)S(1)}, u32[]{:S(2)}, u32[]{:S(2)}) collective-permute-start(bf16[512,128]{1,0:T(8,128)(2,1)S(1)} %copy-done.2), channel_id=1, source_target_pairs={{0,128},{8,136},{16,144},{24,152},{32,160},{40,168},{48,176},{56,1... | collective-permute-start | bytes 393224 | tf_op jit(solution)/shard_map/ppermute | solution.py:291
  29.3 23.5 %collective-permute-start.12 = (bf16[128,1792]{1,0:T(8,128)(2,1)S(1)}, bf16[128,1792]{1,0:T(8,128)(2,1)S(1)}, u32[]{:S(2)}, u32[]{:S(2)}) collective-permute-start(bf16[128,1792]{1,0:T(8,128)(2,1)S(1)} %collective-permute-done.9.refs_0_), channel_id=1, source_target_pairs={{0,16},{8,120},{16,32},{24,8},{32,48},{40,24},{48,64},{56,40},{64,... | collective-permute-start | bytes 1376264 | tf_op jit(solution)/shard_map/ppermute | solution.py:285
  36.8 16.0 %collective-permute-start.16 = (bf16[128,1792]{1,0:T(8,128)(2,1)S(1)}, bf16[128,1792]{1,0:T(8,128)(2,1)S(1)}, u32[]{:S(2)}, u32[]{:S(2)}) collective-permute-start(bf16[128,1792]{1,0:T(8,128)(2,1)S(1)} %gate.11.refs_1_), channel_id=1, source_target_pairs={{0,16},{8,120},{16,32},{24,8},{32,48},{40,24},{48,64},{56,40},{64,... | collective-permute-start | bytes 1376264 | tf_op jit(solution)/shard_map/ppermute | solution.py:285
  36.8 8.9 %collective-permute-start.13 = (bf16[256,512]{1,0:T(8,128)(2,1)S(1)}, bf16[256,512]{1,0:T(8,128)(2,1)S(1)}, u32[]{:S(2)}, u32[]{:S(2)}) collective-permute-start(bf16[256,512]{1,0:T(8,128)(2,1)S(1)} %get-tuple-element.26), channel_id=1, source_target_pairs={{0,1},{1,2},{2,3},{3,0},{4,5},{5,6},{6,7},{7,4},{8,9},{9,10},{10,1... | collective-permute-start | bytes 786440 | tf_op jit(solution)/shard_map/ppermute | solution.py:295
  38.4 8.1 %collective-permute-start.14 = (bf16[256,512]{1,0:T(8,128)(2,1)S(1)}, bf16[256,512]{1,0:T(8,128)(2,1)S(1)}, u32[]{:S(2)}, u32[]{:S(2)}) collective-permute-start(bf16[256,512]{1,0:T(8,128)(2,1)S(1)} %get-tuple-element.27), channel_id=1, source_target_pairs={{0,3},{1,0},{2,1},{3,2},{4,7},{5,4},{6,5},{7,6},{8,11},{9,8},{10,9... | collective-permute-start | bytes 786440 | tf_op jit(solution)/shard_map/ppermute | solution.py:295
  40.0 12.6 %collective-permute-start.15 = (bf16[256,512]{1,0:T(8,128)(2,1)S(1)}, bf16[256,512]{1,0:T(8,128)(2,1)S(1)}, u32[]{:S(2)}, u32[]{:S(2)}) collective-permute-start(bf16[256,512]{1,0:T(8,128)(2,1)S(1)} %get-tuple-element.28), channel_id=1, source_target_pairs={{0,2},{1,3},{2,0},{3,1},{4,6},{5,7},{6,4},{7,5},{8,10},{9,11},{10,... | collective-permute-start | bytes 786440 | tf_op jit(solution)/shard_map/ppermute | solution.py:295
  52.9 4.7 %collective-permute-start.17 = (bf16[512,1792]{1,0:T(8,128)(2,1)S(1)}, bf16[512,1792]{1,0:T(8,128)(2,1)S(1)}, u32[]{:S(2)}, u32[]{:S(2)}) collective-permute-start(bf16[512,1792]{1,0:T(8,128)(2,1)S(1)} %stack.1.refs_0_.refs_8_), channel_id=1, source_target_pairs={{0,8},{8,0},{16,24},{24,16},{32,40},{40,32},{48,56},{56,48},{64,72... | collective-permute-start | bytes 5505032 | tf_op jit(solution)/shard_map/ppermute | solution.py:288
  54.2 9.8 %collective-permute-start.21 = (bf16[256,512]{1,0:T(8,128)(2,1)S(1)}, bf16[256,512]{1,0:T(8,128)(2,1)S(1)}, u32[]{:S(2)}, u32[]{:S(2)}) collective-permute-start(bf16[256,512]{1,0:T(8,128)(2,1)S(1)} %get-tuple-element.35), channel_id=1, source_target_pairs={{0,4},{1,5},{2,6},{3,7},{4,0},{5,1},{6,2},{7,3},{8,12},{9,13},{10,... | collective-permute-start | bytes 786440 | tf_op jit(solution)/shard_map/ppermute | solution.py:298
  60.1 7.4 %collective-permute-start.18 = (bf16[256,256]{1,0:T(8,128)(2,1)S(1)}, bf16[256,256]{1,0:T(8,128)(2,1)S(1)}, u32[]{:S(2)}, u32[]{:S(2)}) collective-permute-start(bf16[256,256]{1,0:T(8,128)(2,1)S(1)} %get-tuple-element.32), channel_id=1, source_target_pairs={{0,1},{1,2},{2,3},{3,0},{4,5},{5,6},{6,7},{7,4},{8,9},{9,10},{10,1... | collective-permute-start | bytes 393224 | tf_op jit(solution)/shard_map/ppermute | solution.py:295
  61.6 7.5 %collective-permute-start.19 = (bf16[256,256]{1,0:T(8,128)(2,1)S(1)}, bf16[256,256]{1,0:T(8,128)(2,1)S(1)}, u32[]{:S(2)}, u32[]{:S(2)}) collective-permute-start(bf16[256,256]{1,0:T(8,128)(2,1)S(1)} %get-tuple-element.33), channel_id=1, source_target_pairs={{0,3},{1,0},{2,1},{3,2},{4,7},{5,4},{6,5},{7,6},{8,11},{9,8},{10,9... | collective-permute-start | bytes 393224 | tf_op jit(solution)/shard_map/ppermute | solution.py:295
  63.4 7.9 %collective-permute-start.20 = (bf16[256,256]{1,0:T(8,128)(2,1)S(1)}, bf16[256,256]{1,0:T(8,128)(2,1)S(1)}, u32[]{:S(2)}, u32[]{:S(2)}) collective-permute-start(bf16[256,256]{1,0:T(8,128)(2,1)S(1)} %get-tuple-element.34), channel_id=1, source_target_pairs={{0,2},{1,3},{2,0},{3,1},{4,6},{5,7},{6,4},{7,5},{8,10},{9,11},{10,... | collective-permute-start | bytes 393224 | tf_op jit(solution)/shard_map/ppermute | solution.py:295
  64.1 10.4 %collective-permute-start.30 = (bf16[256,256]{1,0:T(8,128)(2,1)S(1)}, bf16[256,256]{1,0:T(8,128)(2,1)S(1)}, u32[]{:S(2)}, u32[]{:S(2)}) collective-permute-start(bf16[256,256]{1,0:T(8,128)(2,1)S(1)} %get-tuple-element.37.refs_4_.refs_8_), channel_id=1, source_target_pairs={{0,1},{1,2},{2,3},{3,0},{4,5},{5,6},{6,7},{7,4},{8,9},{9,10},{10,1... | collective-permute-start | bytes 393224 | tf_op jit(solution)/shard_map/ppermute | solution.py:295
  65.6 11.6 %collective-permute-start.31 = (bf16[256,256]{1,0:T(8,128)(2,1)S(1)}, bf16[256,256]{1,0:T(8,128)(2,1)S(1)}, u32[]{:S(2)}, u32[]{:S(2)}) collective-permute-start(bf16[256,256]{1,0:T(8,128)(2,1)S(1)} %get-tuple-element.37.refs_4_.refs_8_), channel_id=1, source_target_pairs={{0,3},{1,0},{2,1},{3,2},{4,7},{5,4},{6,5},{7,6},{8,11},{9,8},{10,9... | collective-permute-start | bytes 393224 | tf_op jit(solution)/shard_map/ppermute | solution.py:295
  67.4 9.8 %collective-permute-start.32 = (bf16[256,256]{1,0:T(8,128)(2,1)S(1)}, bf16[256,256]{1,0:T(8,128)(2,1)S(1)}, u32[]{:S(2)}, u32[]{:S(2)}) collective-permute-start(bf16[256,256]{1,0:T(8,128)(2,1)S(1)} %get-tuple-element.37.refs_4_.refs_8_), channel_id=1, source_target_pairs={{0,2},{1,3},{2,0},{3,1},{4,6},{5,7},{6,4},{7,5},{8,10},{9,11},{10,... | collective-permute-start | bytes 393224 | tf_op jit(solution)/shard_map/ppermute | solution.py:295
  71.4 6.6 %collective-permute-start.29 = (bf16[256,256]{1,0:T(8,128)(2,1)S(1)}, bf16[256,256]{1,0:T(8,128)(2,1)S(1)}, u32[]{:S(2)}, u32[]{:S(2)}) collective-permute-start(bf16[256,256]{1,0:T(8,128)(2,1)S(1)} %get-tuple-element.44), channel_id=1, source_target_pairs={{0,4},{1,5},{2,6},{3,7},{4,0},{5,1},{6,2},{7,3},{8,12},{9,13},{10,... | collective-permute-start | bytes 393224 | tf_op jit(solution)/shard_map/ppermute | solution.py:298
  73.6 7.8 %collective-permute-start.24 = (bf16[256,256]{1,0:T(8,128)(2,1)S(1)}, bf16[256,256]{1,0:T(8,128)(2,1)S(1)}, u32[]{:S(2)}, u32[]{:S(2)}) collective-permute-start(bf16[256,256]{1,0:T(8,128)(2,1)S(1)} %gate.15), channel_id=1, source_target_pairs={{0,2},{1,3},{2,0},{3,1},{4,6},{5,7},{6,4},{7,5},{8,10},{9,11},{10,... | collective-permute-start | bytes 393224 | tf_op jit(solution)/shard_map/ppermute | solution.py:295
  74.5 9.1 %collective-permute-start.23 = (bf16[256,256]{1,0:T(8,128)(2,1)S(1)}, bf16[256,256]{1,0:T(8,128)(2,1)S(1)}, u32[]{:S(2)}, u32[]{:S(2)}) collective-permute-start(bf16[256,256]{1,0:T(8,128)(2,1)S(1)} %gate.14), channel_id=1, source_target_pairs={{0,3},{1,0},{2,1},{3,2},{4,7},{5,4},{6,5},{7,6},{8,11},{9,8},{10,9... | collective-permute-start | bytes 393224 | tf_op jit(solution)/shard_map/ppermute | solution.py:295
  77.2 8.4 %collective-permute-start.22 = (bf16[256,256]{1,0:T(8,128)(2,1)S(1)}, bf16[256,256]{1,0:T(8,128)(2,1)S(1)}, u32[]{:S(2)}, u32[]{:S(2)}) collective-permute-start(bf16[256,256]{1,0:T(8,128)(2,1)S(1)} %gate.13), channel_id=1, source_target_pairs={{0,1},{1,2},{2,3},{3,0},{4,5},{5,6},{6,7},{7,4},{8,9},{9,10},{10,1... | collective-permute-start | bytes 393224 | tf_op jit(solution)/shard_map/ppermute | solution.py:295
  78.0 14.8 %collective-permute-start.33 = (bf16[256,256]{1,0:T(8,128)(2,1)S(1)}, bf16[256,256]{1,0:T(8,128)(2,1)S(1)}, u32[]{:S(2)}, u32[]{:S(2)}) collective-permute-start(bf16[256,256]{1,0:T(8,128)(2,1)S(1)} %merge_x.5.refs_2_), channel_id=1, source_target_pairs={{0,1},{1,2},{2,3},{3,0},{4,5},{5,6},{6,7},{7,4},{8,9},{9,10},{10,1... | collective-permute-start | bytes 393224 | tf_op jit(solution)/shard_map/ppermute | solution.py:295
  79.0 13.8 %collective-permute-start.34 = (bf16[256,256]{1,0:T(8,128)(2,1)S(1)}, bf16[256,256]{1,0:T(8,128)(2,1)S(1)}, u32[]{:S(2)}, u32[]{:S(2)}) collective-permute-start(bf16[256,256]{1,0:T(8,128)(2,1)S(1)} %merge_x.5.refs_2_), channel_id=1, source_target_pairs={{0,3},{1,0},{2,1},{3,2},{4,7},{5,4},{6,5},{7,6},{8,11},{9,8},{10,9... | collective-permute-start | bytes 393224 | tf_op jit(solution)/shard_map/ppermute | solution.py:295
  81.4 11.4 %collective-permute-start.35 = (bf16[256,256]{1,0:T(8,128)(2,1)S(1)}, bf16[256,256]{1,0:T(8,128)(2,1)S(1)}, u32[]{:S(2)}, u32[]{:S(2)}) collective-permute-start(bf16[256,256]{1,0:T(8,128)(2,1)S(1)} %merge_x.5.refs_2_), channel_id=1, source_target_pairs={{0,2},{1,3},{2,0},{3,1},{4,6},{5,7},{6,4},{7,5},{8,10},{9,11},{10,... | collective-permute-start | bytes 393224 | tf_op jit(solution)/shard_map/ppermute | solution.py:295
  85.6 7.6 %collective-permute-start.25 = (bf16[256,256]{1,0:T(8,128)(2,1)S(1)}, bf16[256,256]{1,0:T(8,128)(2,1)S(1)}, u32[]{:S(2)}, u32[]{:S(2)}) collective-permute-start(bf16[256,256]{1,0:T(8,128)(2,1)S(1)} %get-tuple-element.42), channel_id=1, source_target_pairs={{0,4},{1,5},{2,6},{3,7},{4,0},{5,1},{6,2},{7,3},{8,12},{9,13},{10,... | collective-permute-start | bytes 393224 | tf_op jit(solution)/shard_map/ppermute | solution.py:298
  87.1 5.7 %collective-permute-start.36 = (f32[1,1792]{1,0:T(1,128)S(1)}, f32[1,1792]{1,0:T(1,128)S(1)}, u32[]{:S(2)}, u32[]{:S(2)}) collective-permute-start(f32[1,1792]{1,0:T(1,128)S(1)} %get-tuple-element.36.refs_0_), channel_id=1, source_target_pairs={{0,128},{8,136},{16,144},{24,152},{32,160},{40,168},{48,176},{56,1... | collective-permute-start | bytes 21512 | tf_op jit(solution)/shard_map/ppermute | solution.py:291
  94.5 17.1 %collective-permute-start.37 = (bf16[1792,256]{1,0:T(8,128)(2,1)S(1)}, bf16[1792,256]{1,0:T(8,128)(2,1)S(1)}, u32[]{:S(2)}, u32[]{:S(2)}) collective-permute-start(bf16[1792,256]{1,0:T(8,128)(2,1)S(1)} %backward.5), channel_id=1, source_target_pairs={{0,128},{8,136},{16,144},{24,152},{32,160},{40,168},{48,176},{56,1... | collective-permute-start | bytes 2752520 | tf_op jit(solution)/shard_map/ppermute | solution.py:291
  96.0 7.7 %collective-permute-start.26 = (bf16[512,256]{1,0:T(8,128)(2,1)S(1)}, bf16[512,256]{1,0:T(8,128)(2,1)S(1)}, u32[]{:S(2)}, u32[]{:S(2)}) collective-permute-start(bf16[512,256]{1,0:T(8,128)(2,1)S(1)} %merge_x.4.refs_10_), channel_id=1, source_target_pairs={{0,1},{1,2},{2,3},{3,0},{4,5},{5,6},{6,7},{7,4},{8,9},{9,10},{10,1... | collective-permute-start | bytes 786440 | tf_op jit(solution)/shard_map/ppermute | solution.py:295
  96.1 9.9 %collective-permute-start.27 = (bf16[512,256]{1,0:T(8,128)(2,1)S(1)}, bf16[512,256]{1,0:T(8,128)(2,1)S(1)}, u32[]{:S(2)}, u32[]{:S(2)}) collective-permute-start(bf16[512,256]{1,0:T(8,128)(2,1)S(1)} %merge_x.4.refs_10_), channel_id=1, source_target_pairs={{0,3},{1,0},{2,1},{3,2},{4,7},{5,4},{6,5},{7,6},{8,11},{9,8},{10,9... | collective-permute-start | bytes 786440 | tf_op jit(solution)/shard_map/ppermute | solution.py:295
  99.4 7.9 %collective-permute-start.28 = (bf16[512,256]{1,0:T(8,128)(2,1)S(1)}, bf16[512,256]{1,0:T(8,128)(2,1)S(1)}, u32[]{:S(2)}, u32[]{:S(2)}) collective-permute-start(bf16[512,256]{1,0:T(8,128)(2,1)S(1)} %merge_x.4.refs_10_), channel_id=1, source_target_pairs={{0,2},{1,3},{2,0},{3,1},{4,6},{5,7},{6,4},{7,5},{8,10},{9,11},{10,... | collective-permute-start | bytes 786440 | tf_op jit(solution)/shard_map/ppermute | solution.py:295
  109.5 2.4 %copy-start.3 = (f32[1792,128]{1,0:T(8,128)S(1)}, f32[1792,128]{1,0:T(8,128)}, u32[]{:S(2)}) copy-start(f32[1792,128]{1,0:T(8,128)} %param.9) | copy-start | bytes 2752516
